TPU v7x, 32 devices: a whole 2x2x4 slice. The times are simulated.
32 devices in a mesh: row: 4 (over z), col: 4 (over x, core), pair: 2 (over y).
Axes of the slice: x: 2, y: 2, z: 4, core: 2. Of those that a mesh axis runs over, the one named last changes fastest.
Arguments:
- pair_slab: bfloat16 [768, 16384], P('pair', 'row'), may hold values from -0.875 to 0.875
- pair_weights: float32 [768], P('pair'), may hold values from 0.2 to 2
Outputs:
- polarizability: float32 [16384, 16384], P('row', ('col', 'pair'))
All inputs are finite; a program needn't handle non-finite values.
Results may differ from a plain program's by a relative error of at most 0.0085.
Values may be sent and summed in bfloat16 or wider, within the bound.
No kernel may reach another device: no remote copies, remote signals or barrier semaphores. Data moves between devices by JAX's collectives and lax.ppermute only.
A program may use at most 128 MiB of HBM per device.

v0:
```python
import jax
import jax.numpy as jnp
from jax import lax
from jax.sharding import PartitionSpec as P


def from_root(block, axis, owner):
    block = jnp.where(lax.axis_index(axis) == owner, block, jnp.zeros_like(block))
    return lax.psum(block, axis)


def contract_pairs(left, right):
    return lax.dot_general(
        left, right, (((0,), (0,)), ((), ())), preferred_element_type=jnp.float32
    )


def on_device(pair_slab, pair_weights):
    col_index = lax.axis_index("col")
    column_block = from_root(pair_slab, "row", col_index)
    own_columns = lax.all_to_all(column_block, "pair", split_axis=1, concat_axis=0, tiled=True)
    rows_piece = lax.all_gather(pair_slab, "pair", axis=0, tiled=True)
    weight_piece = lax.all_gather(
        pair_weights.astype(jnp.bfloat16), "pair", axis=0, tiled=True
    ).astype(jnp.float32)
    weighted = (weight_piece[:, None] * rows_piece.astype(jnp.float32)).astype(jnp.bfloat16)
    return contract_pairs(weighted, own_columns)


def solution(mesh):
    placed = (P("pair", "row"), P("pair"))
    return jax.shard_map(
        on_device, mesh=mesh, in_specs=placed, out_specs=P("row", ("col", "pair")), check_vma=False
    )
```

profile of v0, /device:TPU:1, one launch (start us, length us, event | category | flops | bytes accessed | tf_op | source)
XLA Modules:
  0.0 209.5 jit_solution(1768566859428120808)
XLA Ops:
  7.4 0.0 all-reduce.2.cloned.1.call-start
  7.4 3.4 %copy.5 = bf16[384,4096]{0,1:T(8,128)(2,1)S(1)} copy(bf16[384,4096]{1,0:T(8,128)(2,1)} %param.2) | data formatting | bytes 6291456 | tf_op args[0]
  10.8 2.0 broadcast_select_fusion
  12.8 0.0 all-reduce.2.cloned.1.call-update
  12.8 0.0 all-gather.3.cloned.1.call-start
  12.8 0.5 all-gather.3.cloned.1.call-update
  13.4 0.0 copy-start
  13.4 122.7 %all-reduce.2.cloned.1.call-done = bf16[384,2,2048]{0,2,1:T(8,128)(2,1)} async-done(((bf16[384,2,2048]{0,2,1:T(8,128)(2,1)}), bf16[384,2,2048]{0,2,1:T(8,128)(2,1)}) %all-reduce.2.cloned.1.call-update) | async-done | bytes 3145744 | tf_op jit(solution)/shard_map/psum | solution.py:9
  136.1 3.9 %all-to-all-start = ((bf16[384,2,2048]{0,2,1:T(8,128)(2,1)}), bf16[384,2,2048]{0,2,1:T(8,128)(2,1)S(1)}, u32[]{:S(2)}, u32[]{:S(2)}) async-start(bf16[384,2,2048]{0,2,1:T(8,128)(2,1)} %all-reduce.2.cloned.1.call-done), calls=%async_computation | async-start | bytes 6291456 | tf_op jit(solution)/shard_map/all_to_all | solution.py:21
  140.0 0.0 copy-done
  140.1 35.5 %all-gather = bf16[2,1,384]{2,1,0:T(2,128)(2,1)S(1)} all-gather(bf16[1,1,384]{2,1,0:T(2,128)(2,1)S(1)} %reshape.4), channel_id=1, replica_groups=mesh['row'=4,'col'=4,'pair'=2] {'pair'}, dimensions={0}, use_global_device_ids=true | all-gather | bytes 2304 | tf_op jit(solution)/shard_map/all_gather | solution.py:23
  175.6 0.0 all-to-all-done
  175.6 3.0 %copy.6 = bf16[2,384,2048]{2,1,0:T(8,128)(2,1)} copy(bf16[2,384,2048]{1,2,0:T(8,128)(2,1)S(1)} %bitcast.4) | data formatting | bytes 6291456 | tf_op jit(solution)/shard_map/all_to_all | solution.py:21
  178.6 0.0 all-gather.3.cloned.1.call-done
  178.6 23.4 %fusion = f32[4096,2048]{1,0:T(8,128)} fusion(bf16[768,2048]{1,0:T(8,128)(2,1)} %bitcast.6, bf16[768,4096]{1,0:T(8,128)(2,1)} %all-gather.3.cloned.1.call-done, f32[768]{0:T(1024)S(1)} %reshape.6), kind=kOutput, calls=%fused_computation.1 | convolution fusion | flops 12894339072 | bytes 42994688 | tf_op jit(solution)/shard_map/dot_general | solution.py:13
  (4 shorter events, 0.0 us)
Async XLA Ops:
  7.4 128.7 %all-reduce.2.cloned.1.call-start = ((), (), s32[]{:S(2)}) async-start(), calls=%async_computation.2 | async-start | bytes 6291456 | tf_op jit(solution)/shard_map/psum | solution.py:9
  12.8 165.8 %all-gather.3.cloned.1.call-start = ((), (), s32[]{:S(2)}) async-start(), calls=%async_computation.1 | async-start | bytes 9437184 | tf_op jit(solution)/shard_map/all_gather | solution.py:22
  13.4 126.7 %copy-start = (f32[384]{0:T(512)S(1)}, f32[384]{0:T(512)}, u32[]{:S(2)}) copy-start(f32[384]{0:T(512)} %param.3) | copy-start | bytes 4612
  136.1 39.6 %all-to-all-start = ((bf16[384,2,2048]{0,2,1:T(8,128)(2,1)}), bf16[384,2,2048]{0,2,1:T(8,128)(2,1)S(1)}, u32[]{:S(2)}, u32[]{:S(2)}) async-start(bf16[384,2,2048]{0,2,1:T(8,128)(2,1)} %all-reduce.2.cloned.1.call-done), calls=%async_computation | async-start | bytes 6291456 | tf_op jit(solution)/shard_map/all_to_all | solution.py:21
Sparse Core Ops, SparseCore 0:
  12.9 123.1 all-reduce.1
Sparse Core Ops, SparseCore 1:
  14.8 82.2 all-gather.2
where the time goes:
time: 211 us; the launch traced here: 210 us
  waiting for transfers between devices  123 us (58%)
  blocking collectives  35.5 us (17%)
  matrix products  23.4 us (11%)
  between operations  14.9 us (7%)
  local copies, waits for them, and re-layouts  6.43 us (3%)
  starting transfers between devices  3.99 us (2%)
    psum x1, waiting for transfers between devices, from_root(): return lax.psum(block, axis)  123 us
    all_gather x1, blocking collectives, on_device(): lax.all_gather(pair_weights.astype(jnp.bfloat16), 'pair', axis=0, tiled=T...  35.5 us
    dot_general x1, matrix products, contract_pairs(): lax.dot_general(left, right, (((0,), (0,)), ((), ())), preferred_element_...  23.4 us
  transfers between devices with their start and end apart: 3, of which 1 were waited for; matrix products, arithmetic and copies ran while one was open for 1% of the time, Pallas kernels for 0%

commit v1 on v0

v1 whole, which is shorter than its diff:
```python
import jax
import jax.numpy as jnp
from jax import lax
from jax.experimental import pallas as pl
from jax.experimental.pallas import tpu as pltpu
from jax.sharding import PartitionSpec as P

AXES = ("row", "col", "pair")


def dot_over_pairs(left, right):
    return lax.dot_general(
        left, right, (((0,), (0,)), ((), ())), preferred_element_type=jnp.float32
    )


def product_kernel(own_rows, other_rows, own_cols, other_cols, *refs):
    out = refs[-1]
    out[...] = dot_over_pairs(own_rows[...], own_cols[...]) + dot_over_pairs(
        other_rows[...], other_cols[...]
    )


def product(own_rows, other_rows, own_cols, other_cols, result, place, columns):
    own, rows = own_rows.shape
    other, width = other_cols.shape
    tile = 1024 if rows % 1024 == 0 else rows
    in_specs = [
        pl.BlockSpec((own, tile), lambda i: (0, i)),
        pl.BlockSpec((other, tile), lambda i: (0, i)),
        pl.BlockSpec((own, width), lambda i: (0, 0)),
        pl.BlockSpec((other, width), lambda i: (0, 0)),
    ]
    args = [own_rows, other_rows, own_cols, other_cols]
    aliases = {}
    if result is not None:
        in_specs.append(pl.BlockSpec(memory_space=pl.ANY))
        args.append(result)
        aliases = {4: 0}
    return pl.pallas_call(
        product_kernel,
        grid=(rows // tile,),
        in_specs=in_specs,
        out_specs=pl.BlockSpec((tile, width), lambda i: (i, place)),
        out_shape=jax.ShapeDtypeStruct((rows, columns), jnp.float32),
        input_output_aliases=aliases,
        compiler_params=pltpu.CompilerParams(vmem_limit_bytes=40 * 2**20),
        cost_estimate=pl.CostEstimate(
            flops=2 * rows * width * (own + other),
            bytes_accessed=4 * rows * width + 2 * rows * (own + other),
            transcendentals=0,
        ),
    )(*args)


def solution(mesh):
    R, C, Q = (mesh.shape[axis] for axis in AXES)

    def number(r, c, p):
        return (r * C + c) * Q + p

    def permute(block, route):
        pairs = []
        for r in range(R):
            for c in range(C):
                for p in range(Q):
                    target = route(r, c, p)
                    if target is not None and 0 <= target[0] < R:
                        pairs.append((number(r, c, p), number(*target)))
        return lax.ppermute(block, AXES, pairs) if pairs else jnp.zeros_like(block)

    def spread(block, carried):
        step = permute(block, lambda r, c, p: (r - 1, c, p) if r == carried[c] else None)
        step = step + permute(block, lambda r, c, p: (r + 1, c, p) if r == carried[c] else None)
        total = step
        for hop in range(1, R - 1):

            def onward(r, c, p):
                way = r - carried[c]
                if abs(way) != hop:
                    return None
                return (r + 1, c, p) if way > 0 else (r - 1, c, p)

            step = permute(step, onward)
            total = total + step
        return total

    def cross(block, carried):
        return permute(
            block,
            lambda r, c, p: (r, carried[c], p) if carried[c] not in (c, r) else None,
        )

    def on_device(slab, weights):
        pairs, block = slab.shape
        width = block // Q
        half = width // 2
        r, c, p = (lax.axis_index(axis) for axis in AXES)
        core = c % 2
        mirrored = [C - 1 - i for i in range(C)]
        native = list(range(C))
        edges = [C - 1 - i if i in (0, C - 1) else i for i in range(C)]

        def columns_of(array, start, size):
            return lax.dynamic_slice_in_dim(array, start, size, 1)

        own0 = columns_of(slab, p * width, half)
        own1 = columns_of(slab, p * width + half, half)

        def exchange(shift, relative, offset, size):
            start = (p - shift + relative) % Q * width + offset
            mine = lax.dynamic_slice(slab, (core * (pairs // 2), start), (pairs // 2, size))
            mine = permute(mine, lambda r, c, p: (r, c, (p - shift) % Q))
            theirs = permute(mine, lambda r, c, p: (r, c ^ 1, p))
            return jnp.concatenate(
                [jnp.where(core == 0, mine, theirs), jnp.where(core == 0, theirs, mine)], 0
            )

        shifts = range(1, Q)
        other0 = jnp.concatenate([exchange(s, 0, 0, half) for s in shifts], 0)
        other1 = jnp.concatenate([exchange(s, 0, half, half) for s in shifts], 0)
        rest = [
            jnp.concatenate([exchange(s, j, 0, width) for s in shifts], 0) for j in range(1, Q)
        ]
        other_weights = jnp.concatenate(
            [permute(weights, lambda r, c, p: (r, c, (p - s) % Q)) for s in shifts]
        )

        def taken(carried, block):
            got = spread(block, carried)
            if carried == native:
                return jnp.where(r == c, block, got)
            crossed = cross(got, carried)
            away = jnp.zeros((), bool)
            for i in range(C):
                if carried[i] != i:
                    away = away | (c == i)
            return jnp.where(r == c, block, jnp.where(away, crossed, got))

        cols_own0 = taken(mirrored, own0)
        cols_own1 = taken(native, own1)
        cols_other0 = taken(edges, other0)
        cols_other1 = taken(native, other1)

        parts = [jnp.concatenate([other0, other1], 1)] + rest
        ordered = []
        for h in range(Q):
            chosen = parts[0]
            for j in range(1, Q):
                chosen = jnp.where((p + j) % Q == h, parts[j], chosen)
            ordered.append(chosen)
        other_rows = jnp.concatenate(ordered, 1)

        def weigh(rows, by):
            return (by[:, None] * rows.astype(jnp.float32)).astype(jnp.bfloat16)

        own_rows, other_rows = weigh(slab, weights), weigh(other_rows, other_weights)
        result = product(own_rows, other_rows, cols_own0, cols_other0, None, 0, width)
        return product(own_rows, other_rows, cols_own1, cols_other1, result, 1, width)

    return jax.shard_map(
        on_device,
        mesh=mesh,
        in_specs=(P("pair", "row"), P("pair")),
        out_specs=P("row", ("col", "pair")),
        check_vma=False,
    )
```

time: 211 us -> 160 us (0.76)
  waiting for transfers between devices: 123 us -> 44.6 us
  starting transfers between devices: 3.99 us -> 69.9 us
  blocking collectives: 35.5 us -> 0 us
  Pallas kernels: 0 us -> 24 us
  matrix products: 23.4 us -> 0 us
  between operations: 14.9 us -> 0.4 us
  other arithmetic: 1.99 us -> 16 us
  local copies, waits for them, and re-layouts: 6.43 us -> 4.04 us
    psum x1 -> x0, waiting for transfers between devices: 123 us -> none  [from_root(): return lax.psum(block, axis)]
    ppermute x0 -> x25, starting transfers between devices: none -> 69.9 us  [permute(): return lax.ppermute(block, AXES, pairs) if pairs else jnp.zeros_like(block)]
    ppermute x0 -> x25, waiting for transfers between devices: none -> 44.6 us  [permute(): return lax.ppermute(block, AXES, pairs) if pairs else jnp.zeros_like(block)]
    all_gather x1 -> x0, blocking collectives: 35.5 us -> none  [on_device(): lax.all_gather(pair_weights.astype(jnp.bfloat16), 'pair', axis=0, tiled=T...]
    pallas_call x0 -> x2, Pallas kernels: none -> 24 us  [product(): pl.pallas_call(product_kernel, grid=(rows // tile,), in_specs=in_specs, o...]
    dot_general x1 -> x0, matrix products: 23.4 us -> none  [contract_pairs(): lax.dot_general(left, right, (((0,), (0,)), ((), ())), preferred_element_...]
    select_n x1 -> x8, other arithmetic: 1.97 us -> 9.9 us  [the longest x1 6.08 us: on_device(): chosen = jnp.where((p + j) % Q == h, parts[j], chosen)]
    dynamic_slice x0 -> x3, local copies, waits for them, and re-layouts: none -> 4.03 us  [the longest x1 2.65 us: columns_of(): return lax.dynamic_slice_in_dim(array, start, size, 1)]
  transfers between devices with their start and end apart: 3 -> 25, of which waited for: 1 -> 6; matrix products, arithmetic and copies ran while one was open for 1% -> 11% of each run, Pallas kernels for 0% -> 0%
where the time goes in v1:
time: 160 us; the launch traced here: 159 us
  starting transfers between devices  69.9 us (44%)
  waiting for transfers between devices  44.6 us (28%)
  Pallas kernels  24 us (15%)
  other arithmetic  16 us (10%)
  local copies, waits for them, and re-layouts  4.04 us (3%)
    ppermute x25, starting transfers between devices, permute(): return lax.ppermute(block, AXES, pairs) if pairs else jnp.zeros_like(block)  69.9 us
    ppermute x25, waiting for transfers between devices, permute(): return lax.ppermute(block, AXES, pairs) if pairs else jnp.zeros_like(block)  44.6 us
    pallas_call x2, Pallas kernels, product(): pl.pallas_call(product_kernel, grid=(rows // tile,), in_specs=in_specs, o...  24 us
    select_n x1, other arithmetic, on_device(): chosen = jnp.where((p + j) % Q == h, parts[j], chosen)  6.08 us
    add x4, other arithmetic, spread(): step + permute(block, lambda r, c, p: (r + 1, c, p) if r == carried[c] el...  3.72 us
  transfers between devices with their start and end apart: 25, of which 6 were waited for; matrix products, arithmetic and copies ran while one was open for 11% of the time, Pallas kernels for 0%

profile of v1, /device:TPU:1, one launch (start us, length us, event | category | flops | bytes accessed | tf_op | source)
XLA Modules:
  0.0 158.9 jit_solution(5713346221800919788)
XLA Ops:
  0.0 1.3 fusion
  1.3 2.1 %collective-permute-start.3 = (bf16[192,1024]{1,0:T(8,128)(2,1)S(1)}, bf16[192,1024]{1,0:T(8,128)(2,1)S(1)}, u32[]{:S(2)}, u32[]{:S(2)}) collective-permute-start(bf16[192,1024]{1,0:T(8,128)(2,1)S(1)} %get-tuple-element.9), channel_id=1, source_target_pairs={{0,1},{1,0},{2,3},{3,2},{4,5},{5,4},{6,7},{7,6},{8,9},{9,8},{10,11... | collective-permute-start | bytes 1179656 | tf_op jit(solution)/shard_map/ppermute | solution.py:70
  3.5 0.1 collective-permute-start.5
  3.5 8.8 %collective-permute-done.3 = bf16[192,1024]{1,0:T(8,128)(2,1)S(1)} collective-permute-done((bf16[192,1024]{1,0:T(8,128)(2,1)S(1)}, bf16[192,1024]{1,0:T(8,128)(2,1)S(1)}, u32[]{:S(2)}, u32[]{:S(2)}) %collective-permute-start.3) | collective-permute-done | bytes 393248 | tf_op jit(solution)/shard_map/ppermute | solution.py:70
  12.3 2.1 %collective-permute-start.4 = (bf16[192,1024]{1,0:T(8,128)(2,1)S(1)}, bf16[192,1024]{1,0:T(8,128)(2,1)}, u32[]{:S(2)}, u32[]{:S(2)}) collective-permute-start(bf16[192,1024]{1,0:T(8,128)(2,1)S(1)} %collective-permute-done.3), channel_id=1, source_target_pairs={{0,2},{1,3},{2,0},{3,1},{4,6},{5,7},{6,4},{7,5},{8,10},{9,11},{10,... | collective-permute-start | bytes 1179656 | tf_op jit(solution)/shard_map/ppermute | solution.py:70
  14.4 6.5 %collective-permute-done.5 = bf16[192,1024]{1,0:T(8,128)(2,1)} collective-permute-done((bf16[192,1024]{1,0:T(8,128)(2,1)S(1)}, bf16[192,1024]{1,0:T(8,128)(2,1)}, u32[]{:S(2)}, u32[]{:S(2)}) %collective-permute-start.5) | collective-permute-done | bytes 393248 | tf_op jit(solution)/shard_map/ppermute | solution.py:70
  20.8 1.2 collective-permute-start.6
  22.1 2.6 %constant_dynamic-slice_fusion = (bf16[384,1024]{1,0:T(8,128)(2,1)}, bf16[384,1024]{1,0:T(8,128)(2,1)}) fusion(bf16[384,4096]{1,0:T(8,128)(2,1)} %param.2, s32[]{:T(128)S(6)} %select_n.145, s32[]{:T(128)S(6)} %select_n.142), kind=kLoop, calls=%fused_computation.20 | loop fusion | bytes 3145736 | tf_op jit(solution)/shard_map/dynamic_slice | solution.py:105
  24.7 1.5 collective-permute-start.16
  26.2 1.6 collective-permute-start.15
  27.8 1.6 %collective-permute-start.8 = (bf16[384,1024]{1,0:T(8,128)(2,1)}, bf16[384,1024]{1,0:T(8,128)(2,1)}, u32[]{:S(2)}, u32[]{:S(2)}) collective-permute-start(bf16[384,1024]{1,0:T(8,128)(2,1)} %get-tuple-element.6), channel_id=1, source_target_pairs={{0,8},{1,9},{10,18},{11,19},{20,28},{21,29}} | collective-permute-start | bytes 2359304 | tf_op jit(solution)/shard_map/ppermute | solution.py:70
  29.4 0.1 dynamic_slice.15
  29.5 0.0 copy-start.1
  29.5 0.0 collective-permute-done.4
  29.5 1.3 collective-permute-start.7
  30.8 1.5 collective-permute-start.1
  32.4 1.2 broadcast_select_fusion.5
  33.5 0.1 pad_maximum_fusion.2
  33.6 1.1 broadcast_select_fusion.7
  34.6 0.1 pad_maximum_fusion.1
  34.7 12.8 %collective-permute-done.1 = bf16[192,2048]{1,0:T(8,128)(2,1)S(1)} collective-permute-done((bf16[192,2048]{1,0:T(8,128)(2,1)S(1)}, bf16[192,2048]{1,0:T(8,128)(2,1)S(1)}, u32[]{:S(2)}, u32[]{:S(2)}) %collective-permute-start.1) | collective-permute-done | bytes 786464 | tf_op jit(solution)/shard_map/ppermute | solution.py:70
  47.5 1.3 collective-permute-start.20
  48.8 0.7 collective-permute-start.21
  49.5 0.0 collective-permute-done.15
  49.5 1.3 collective-permute-start.11
  50.8 0.7 collective-permute-start.12
  51.5 0.0 collective-permute-done.7
  51.5 2.9 %collective-permute-start.2 = (bf16[192,2048]{1,0:T(8,128)(2,1)S(1)}, bf16[192,2048]{1,0:T(8,128)(2,1)S(1)}, u32[]{:S(2)}, u32[]{:S(2)}) collective-permute-start(bf16[192,2048]{1,0:T(8,128)(2,1)S(1)} %collective-permute-done.1), channel_id=1, source_target_pairs={{0,2},{1,3},{2,0},{3,1},{4,6},{5,7},{6,4},{7,5},{8,10},{9,11},{10,... | collective-permute-start | bytes 2359304 | tf_op jit(solution)/shard_map/ppermute | solution.py:70
  54.5 1.0 multiply_convert_fusion.1.own_rows
  55.5 1.7 %add.108 = bf16[384,1024]{1,0:T(8,128)(2,1)S(1)} add(bf16[384,1024]{1,0:T(8,128)(2,1)} %collective-permute-done.15, bf16[384,1024]{1,0:T(8,128)(2,1)} %collective-permute-done.16) | non-fusion elementwise | flops 393216 | bytes 2359296 | tf_op jit(solution)/shard_map/add | solution.py:74
  57.1 1.4 add.101
  58.6 3.4 %collective-permute-done.20 = bf16[384,1024]{1,0:T(8,128)(2,1)S(1)} collective-permute-done((bf16[384,1024]{1,0:T(8,128)(2,1)S(1)}, bf16[384,1024]{1,0:T(8,128)(2,1)S(1)}, u32[]{:S(2)}, u32[]{:S(2)}) %collective-permute-start.20) | collective-permute-done | bytes 786464 | tf_op jit(solution)/shard_map/ppermute | solution.py:70
  62.0 1.4 collective-permute-start
  63.3 1.3 collective-permute-start.17
  64.6 0.3 add.111
  64.9 5.5 %collective-permute-done.11 = bf16[384,1024]{1,0:T(8,128)(2,1)S(1)} collective-permute-done((bf16[384,1024]{1,0:T(8,128)(2,1)S(1)}, bf16[384,1024]{1,0:T(8,128)(2,1)S(1)}, u32[]{:S(2)}, u32[]{:S(2)}) %collective-permute-start.11) | collective-permute-done | bytes 786464 | tf_op jit(solution)/shard_map/ppermute | solution.py:70
  70.4 0.7 collective-permute-start.9
  71.1 0.0 collective-permute-done.12
  71.1 0.7 collective-permute-start.22
  71.8 0.3 add.104
  72.2 0.7 collective-permute-start.13
  72.9 0.1 broadcast_select_fusion.3
  73.0 6.1 %broadcast_select_fusion.1 = (bf16[384,2048]{1,0:T(8,128)(2,1)S(1)}, bf16[384,2048]{1,0:T(8,128)(2,1)S(1)}) fusion(pred[]{:T(512)S(6)} %eq.41, bf16[192,2048]{1,0:T(8,128)(2,1)S(1)} %get-tuple-element.12, bf16[192,2048]{1,0:T(8,128)(2,1)S(1)} %get-tuple-element.11, bf16[192,1024]{1,0:T(8,128)(2,1)S(1)} %get-tuple-element.16, ...), kind=kLoop, calls=%fused_computation.5 | loop fusion | flops 11010048 | bytes 6291458 | tf_op jit(solution)/shard_map/jit(_where)/select_n | solution.py:150
  79.1 0.0 collective-permute-done.17
  79.1 0.7 collective-permute-start.18
  79.8 0.0 collective-permute-done.9
  79.8 0.7 collective-permute-start.10
  80.6 0.7 collective-permute-start.23
  81.3 1.0 multiply_convert_fusion.other_rows
  82.3 0.0 collective-permute-done.13
  82.3 0.7 collective-permute-start.14
  83.0 0.0 collective-permute-done.18
  83.0 0.1 add_add_fusion.1
  83.2 41.4 %collective-permute-start.19 = (bf16[384,1024]{1,0:T(8,128)(2,1)S(1)}, bf16[384,1024]{1,0:T(8,128)(2,1)S(1)}, u32[]{:S(2)}, u32[]{:S(2)}) collective-permute-start(bf16[384,1024]{1,0:T(8,128)(2,1)S(1)} %add_add_fusion.1), channel_id=1, source_target_pairs={{0,6},{1,7},{2,4},{3,5},{4,2},{5,3},{8,14},{9,15},{10,12},{11,13},... | collective-permute-start | bytes 2359304 | tf_op jit(solution)/shard_map/ppermute | solution.py:70
  124.6 0.0 collective-permute-done.23
  124.6 0.1 add_add_fusion
  124.7 0.9 collective-permute-start.24
  125.6 0.2 add_select_fusion.1.own_cols
  125.8 0.6 add_select_fusion.other_cols
  126.5 7.8 %collective-permute-done.19 = bf16[384,1024]{1,0:T(8,128)(2,1)S(1)} collective-permute-done((bf16[384,1024]{1,0:T(8,128)(2,1)S(1)}, bf16[384,1024]{1,0:T(8,128)(2,1)S(1)}, u32[]{:S(2)}, u32[]{:S(2)}) %collective-permute-start.19) | collective-permute-done | bytes 786464 | tf_op jit(solution)/shard_map/ppermute | solution.py:70
  134.2 0.2 select_select_fusion.1.own_cols
  134.5 0.5 select_select_fusion.other_cols
  134.9 12.0 %shard_map.28.refs_0_ = f32[4096,2048]{1,0:T(8,128)} custom-call(bf16[384,4096]{1,0:T(8,128)(2,1)S(1)} %multiply_convert_fusion.1.own_rows, bf16[384,4096]{1,0:T(8,128)(2,1)S(1)} %multiply_convert_fusion.other_rows, bf16[384,1024]{1,0:T(8,128)(2,1)S(1)} %select_select_fusion.1.own_cols, bf16[384,1024]{1,0:T(8,128)(2,1)S(1)} %select_select_fusion.other_cols), custom_call_target="tpu_custom_call" | custom-call | flops 6442450944 | bytes 23068672 | tf_op jit(solution)/shard_map/pallas_call | solution.py:40
  146.9 12.0 %shard_map.29 = f32[4096,2048]{1,0:T(8,128)} custom-call(bf16[384,4096]{1,0:T(8,128)(2,1)S(1)} %multiply_convert_fusion.1.own_rows, bf16[384,4096]{1,0:T(8,128)(2,1)S(1)} %multiply_convert_fusion.other_rows, bf16[384,1024]{1,0:T(8,128)(2,1)S(1)} %add_select_fusion.1.own_cols, ...), custom_call_target="tpu_custom_call", output_to_operand_aliasing={{}: (4, {})} | custom-call | flops 6442450944 | bytes 23068672 | tf_op jit(solution)/shard_map/pallas_call | solution.py:40
  (13 shorter events, 0.0 us)
Async XLA Ops:
  0.0 29.4 %copy-start = (bf16[384,4096]{1,0:T(8,128)(2,1)S(1)}, bf16[384,4096]{1,0:T(8,128)(2,1)}, u32[]{:S(2)}) copy-start(bf16[384,4096]{1,0:T(8,128)(2,1)} %param.2) | copy-start | bytes 9437188
  1.3 11.0 %collective-permute-start.3 = (bf16[192,1024]{1,0:T(8,128)(2,1)S(1)}, bf16[192,1024]{1,0:T(8,128)(2,1)S(1)}, u32[]{:S(2)}, u32[]{:S(2)}) collective-permute-start(bf16[192,1024]{1,0:T(8,128)(2,1)S(1)} %get-tuple-element.9), channel_id=1, source_target_pairs={{0,1},{1,0},{2,3},{3,2},{4,5},{5,4},{6,7},{7,6},{8,9},{9,8},{10,11... | collective-permute-start | bytes 1179656 | tf_op jit(solution)/shard_map/ppermute | solution.py:70
  3.5 17.4 %collective-permute-start.5 = (bf16[192,1024]{1,0:T(8,128)(2,1)S(1)}, bf16[192,1024]{1,0:T(8,128)(2,1)}, u32[]{:S(2)}, u32[]{:S(2)}) collective-permute-start(bf16[192,1024]{1,0:T(8,128)(2,1)S(1)} %get-tuple-element.10), channel_id=1, source_target_pairs={{0,1},{1,0},{2,3},{3,2},{4,5},{5,4},{6,7},{7,6},{8,9},{9,8},{10,11... | collective-permute-start | bytes 1179656 | tf_op jit(solution)/shard_map/ppermute | solution.py:70
  12.3 17.2 %collective-permute-start.4 = (bf16[192,1024]{1,0:T(8,128)(2,1)S(1)}, bf16[192,1024]{1,0:T(8,128)(2,1)}, u32[]{:S(2)}, u32[]{:S(2)}) collective-permute-start(bf16[192,1024]{1,0:T(8,128)(2,1)S(1)} %collective-permute-done.3), channel_id=1, source_target_pairs={{0,2},{1,3},{2,0},{3,1},{4,6},{5,7},{6,4},{7,5},{8,10},{9,11},{10,... | collective-permute-start | bytes 1179656 | tf_op jit(solution)/shard_map/ppermute | solution.py:70
  20.8 10.0 %collective-permute-start.6 = (bf16[192,1024]{1,0:T(8,128)(2,1)}, bf16[192,1024]{1,0:T(8,128)(2,1)}, u32[]{:S(2)}, u32[]{:S(2)}) collective-permute-start(bf16[192,1024]{1,0:T(8,128)(2,1)} %collective-permute-done.5), channel_id=1, source_target_pairs={{0,2},{1,3},{2,0},{3,1},{4,6},{5,7},{6,4},{7,5},{8,10},{9,11},{10,... | collective-permute-start | bytes 1179656 | tf_op jit(solution)/shard_map/ppermute | solution.py:70
  24.7 24.1 %collective-permute-start.16 = (bf16[384,1024]{1,0:T(8,128)(2,1)}, bf16[384,1024]{1,0:T(8,128)(2,1)}, u32[]{:S(2)}, u32[]{:S(2)}) collective-permute-start(bf16[384,1024]{1,0:T(8,128)(2,1)} %get-tuple-element.5), channel_id=1, source_target_pairs={{6,14},{7,15},{12,20},{13,21},{18,26},{19,27}} | collective-permute-start | bytes 2359304 | tf_op jit(solution)/shard_map/ppermute | solution.py:70
  26.2 23.2 %collective-permute-start.15 = (bf16[384,1024]{1,0:T(8,128)(2,1)}, bf16[384,1024]{1,0:T(8,128)(2,1)}, u32[]{:S(2)}, u32[]{:S(2)}) collective-permute-start(bf16[384,1024]{1,0:T(8,128)(2,1)} %get-tuple-element.5), channel_id=1, source_target_pairs={{12,4},{13,5},{18,10},{19,11},{24,16},{25,17}} | collective-permute-start | bytes 2359304 | tf_op jit(solution)/shard_map/ppermute | solution.py:70
  27.8 23.0 %collective-permute-start.8 = (bf16[384,1024]{1,0:T(8,128)(2,1)}, bf16[384,1024]{1,0:T(8,128)(2,1)}, u32[]{:S(2)}, u32[]{:S(2)}) collective-permute-start(bf16[384,1024]{1,0:T(8,128)(2,1)} %get-tuple-element.6), channel_id=1, source_target_pairs={{0,8},{1,9},{10,18},{11,19},{20,28},{21,29}} | collective-permute-start | bytes 2359304 | tf_op jit(solution)/shard_map/ppermute | solution.py:70
  29.5 25.0 %copy-start.1 = (f32[384]{0:T(512)S(1)}, f32[384]{0:T(512)}, u32[]{:S(2)}) copy-start(f32[384]{0:T(512)} %param.3) | copy-start | bytes 4612
  29.5 22.0 %collective-permute-start.7 = (bf16[384,1024]{1,0:T(8,128)(2,1)}, bf16[384,1024]{1,0:T(8,128)(2,1)S(1)}, u32[]{:S(2)}, u32[]{:S(2)}) collective-permute-start(bf16[384,1024]{1,0:T(8,128)(2,1)} %get-tuple-element.6), channel_id=1, source_target_pairs={{10,2},{11,3},{20,12},{21,13},{30,22},{31,23}} | collective-permute-start | bytes 2359304 | tf_op jit(solution)/shard_map/ppermute | solution.py:70
  30.8 16.6 %collective-permute-start.1 = (bf16[192,2048]{1,0:T(8,128)(2,1)S(1)}, bf16[192,2048]{1,0:T(8,128)(2,1)S(1)}, u32[]{:S(2)}, u32[]{:S(2)}) collective-permute-start(bf16[192,2048]{1,0:T(8,128)(2,1)S(1)} %dynamic_slice.15), channel_id=1, source_target_pairs={{0,1},{1,0},{2,3},{3,2},{4,5},{5,4},{6,7},{7,6},{8,9},{9,8},{10,11... | collective-permute-start | bytes 2359304 | tf_op jit(solution)/shard_map/ppermute | solution.py:70
  47.5 14.5 %collective-permute-start.20 = (bf16[384,1024]{1,0:T(8,128)(2,1)S(1)}, bf16[384,1024]{1,0:T(8,128)(2,1)S(1)}, u32[]{:S(2)}, u32[]{:S(2)}) collective-permute-start(bf16[384,1024]{1,0:T(8,128)(2,1)S(1)} %pad_maximum_fusion.1), channel_id=1, source_target_pairs={{10,2},{11,3},{20,12},{21,13},{24,16},{25,17}} | collective-permute-start | bytes 2359304 | tf_op jit(solution)/shard_map/ppermute | solution.py:70
  48.8 14.6 %collective-permute-start.21 = (bf16[384,1024]{1,0:T(8,128)(2,1)S(1)}, bf16[384,1024]{1,0:T(8,128)(2,1)S(1)}, u32[]{:S(2)}, u32[]{:S(2)}) collective-permute-start(bf16[384,1024]{1,0:T(8,128)(2,1)S(1)} %pad_maximum_fusion.1), channel_id=1, source_target_pairs={{6,14},{7,15},{10,18},{11,19},{20,28},{21,29}} | collective-permute-start | bytes 2359304 | tf_op jit(solution)/shard_map/ppermute | solution.py:70
  49.5 20.9 %collective-permute-start.11 = (bf16[384,1024]{1,0:T(8,128)(2,1)S(1)}, bf16[384,1024]{1,0:T(8,128)(2,1)S(1)}, u32[]{:S(2)}, u32[]{:S(2)}) collective-permute-start(bf16[384,1024]{1,0:T(8,128)(2,1)S(1)} %pad_maximum_fusion.2), channel_id=1, source_target_pairs={{10,2},{11,3},{20,12},{21,13},{30,22},{31,23}} | collective-permute-start | bytes 2359304 | tf_op jit(solution)/shard_map/ppermute | solution.py:70
  50.8 20.3 %collective-permute-start.12 = (bf16[384,1024]{1,0:T(8,128)(2,1)S(1)}, bf16[384,1024]{1,0:T(8,128)(2,1)S(1)}, u32[]{:S(2)}, u32[]{:S(2)}) collective-permute-start(bf16[384,1024]{1,0:T(8,128)(2,1)S(1)} %pad_maximum_fusion.2), channel_id=1, source_target_pairs={{0,8},{1,9},{10,18},{11,19},{20,28},{21,29}} | collective-permute-start | bytes 2359304 | tf_op jit(solution)/shard_map/ppermute | solution.py:70
  51.5 20.6 %collective-permute-start.2 = (bf16[192,2048]{1,0:T(8,128)(2,1)S(1)}, bf16[192,2048]{1,0:T(8,128)(2,1)S(1)}, u32[]{:S(2)}, u32[]{:S(2)}) collective-permute-start(bf16[192,2048]{1,0:T(8,128)(2,1)S(1)} %collective-permute-done.1), channel_id=1, source_target_pairs={{0,2},{1,3},{2,0},{3,1},{4,6},{5,7},{6,4},{7,5},{8,10},{9,11},{10,... | collective-permute-start | bytes 2359304 | tf_op jit(solution)/shard_map/ppermute | solution.py:70
  62.0 19.3 %collective-permute-start = (f32[384]{0:T(512)S(1)}, f32[384]{0:T(512)S(1)}, u32[]{:S(2)}, u32[]{:S(2)}) collective-permute-start(f32[384]{0:T(512)S(1)} %copy-done.1), channel_id=1, source_target_pairs={{0,1},{1,0},{2,3},{3,2},{4,5},{5,4},{6,7},{7,6},{8,9},{9,8},{10,11... | collective-permute-start | bytes 4616 | tf_op jit(solution)/shard_map/ppermute | solution.py:70
  63.3 15.7 %collective-permute-start.17 = (bf16[384,1024]{1,0:T(8,128)(2,1)S(1)}, bf16[384,1024]{1,0:T(8,128)(2,1)S(1)}, u32[]{:S(2)}, u32[]{:S(2)}) collective-permute-start(bf16[384,1024]{1,0:T(8,128)(2,1)S(1)} %add.108), channel_id=1, source_target_pairs={{10,2},{11,3},{14,22},{15,23},{16,8},{17,9},{20,28},{21,29}} | collective-permute-start | bytes 2359304 | tf_op jit(solution)/shard_map/ppermute | solution.py:70
  70.4 9.4 %collective-permute-start.9 = (bf16[384,1024]{1,0:T(8,128)(2,1)S(1)}, bf16[384,1024]{1,0:T(8,128)(2,1)S(1)}, u32[]{:S(2)}, u32[]{:S(2)}) collective-permute-start(bf16[384,1024]{1,0:T(8,128)(2,1)S(1)} %add.101), channel_id=1, source_target_pairs={{8,16},{9,17},{12,4},{13,5},{18,26},{19,27},{22,14},{23,15}} | collective-permute-start | bytes 2359304 | tf_op jit(solution)/shard_map/ppermute | solution.py:70
  71.1 9.4 %collective-permute-start.22 = (bf16[384,1024]{1,0:T(8,128)(2,1)S(1)}, bf16[384,1024]{1,0:T(8,128)(2,1)S(1)}, u32[]{:S(2)}, u32[]{:S(2)}) collective-permute-start(bf16[384,1024]{1,0:T(8,128)(2,1)S(1)} %add.111), channel_id=1, source_target_pairs={{12,4},{13,5},{14,22},{15,23},{16,8},{17,9},{18,26},{19,27}} | collective-permute-start | bytes 2359304 | tf_op jit(solution)/shard_map/ppermute | solution.py:70
  72.2 10.1 %collective-permute-start.13 = (bf16[384,1024]{1,0:T(8,128)(2,1)S(1)}, bf16[384,1024]{1,0:T(8,128)(2,1)S(1)}, u32[]{:S(2)}, u32[]{:S(2)}) collective-permute-start(bf16[384,1024]{1,0:T(8,128)(2,1)S(1)} %add.104), channel_id=1, source_target_pairs={{8,16},{9,17},{12,4},{13,5},{18,26},{19,27},{22,14},{23,15}} | collective-permute-start | bytes 2359304 | tf_op jit(solution)/shard_map/ppermute | solution.py:70
  79.1 3.9 %collective-permute-start.18 = (bf16[384,1024]{1,0:T(8,128)(2,1)S(1)}, bf16[384,1024]{1,0:T(8,128)(2,1)S(1)}, u32[]{:S(2)}, u32[]{:S(2)}) collective-permute-start(bf16[384,1024]{1,0:T(8,128)(2,1)S(1)} %collective-permute-done.17), channel_id=1, source_target_pairs={{8,0},{9,1},{22,30},{23,31}} | collective-permute-start | bytes 2359304 | tf_op jit(solution)/shard_map/ppermute | solution.py:70
  79.8 45.8 %collective-permute-start.10 = (bf16[384,1024]{1,0:T(8,128)(2,1)S(1)}, bf16[384,1024]{1,0:T(8,128)(2,1)S(1)}, u32[]{:S(2)}, u32[]{:S(2)}) collective-permute-start(bf16[384,1024]{1,0:T(8,128)(2,1)S(1)} %collective-permute-done.9), channel_id=1, source_target_pairs={{14,6},{15,7},{16,24},{17,25}} | collective-permute-start | bytes 2359304 | tf_op jit(solution)/shard_map/ppermute | solution.py:70
  80.6 44.0 %collective-permute-start.23 = (bf16[384,1024]{1,0:T(8,128)(2,1)S(1)}, bf16[384,1024]{1,0:T(8,128)(2,1)S(1)}, u32[]{:S(2)}, u32[]{:S(2)}) collective-permute-start(bf16[384,1024]{1,0:T(8,128)(2,1)S(1)} %collective-permute-done.22), channel_id=1, source_target_pairs={{8,0},{9,1},{22,30},{23,31}} | collective-permute-start | bytes 2359304 | tf_op jit(solution)/shard_map/ppermute | solution.py:70
  82.3 43.5 %collective-permute-start.14 = (bf16[384,1024]{1,0:T(8,128)(2,1)S(1)}, bf16[384,1024]{1,0:T(8,128)(2,1)S(1)}, u32[]{:S(2)}, u32[]{:S(2)}) collective-permute-start(bf16[384,1024]{1,0:T(8,128)(2,1)S(1)} %collective-permute-done.13), channel_id=1, source_target_pairs={{14,6},{15,7},{16,24},{17,25}} | collective-permute-start | bytes 2359304 | tf_op jit(solution)/shard_map/ppermute | solution.py:70
  83.2 51.1 %collective-permute-start.19 = (bf16[384,1024]{1,0:T(8,128)(2,1)S(1)}, bf16[384,1024]{1,0:T(8,128)(2,1)S(1)}, u32[]{:S(2)}, u32[]{:S(2)}) collective-permute-start(bf16[384,1024]{1,0:T(8,128)(2,1)S(1)} %add_add_fusion.1), channel_id=1, source_target_pairs={{0,6},{1,7},{2,4},{3,5},{4,2},{5,3},{8,14},{9,15},{10,12},{11,13},... | collective-permute-start | bytes 2359304 | tf_op jit(solution)/shard_map/ppermute | solution.py:70
  124.7 9.7 %collective-permute-start.24 = (bf16[384,1024]{1,0:T(8,128)(2,1)S(1)}, bf16[384,1024]{1,0:T(8,128)(2,1)S(1)}, u32[]{:S(2)}, u32[]{:S(2)}) collective-permute-start(bf16[384,1024]{1,0:T(8,128)(2,1)S(1)} %add_add_fusion), channel_id=1, source_target_pairs={{0,6},{1,7},{8,14},{9,15},{14,8},{15,9},{16,22},{17,23},{22,16},{2... | collective-permute-start | bytes 2359304 | tf_op jit(solution)/shard_map/ppermute | solution.py:70

commit v2 on v0

v2 whole, which is shorter than its diff:
```python
import jax
import jax.numpy as jnp
from jax import lax
from jax.experimental import pallas as pl
from jax.experimental.pallas import tpu as pltpu
from jax.sharding import PartitionSpec as P

AXES = ("row", "col", "pair")
LANES = 128
VMEM = pl.BlockSpec(memory_space=pltpu.VMEM)
SMEM = pl.BlockSpec(memory_space=pltpu.SMEM)
ANY = pl.BlockSpec(memory_space=pl.ANY)


def params(mib):
    return pltpu.CompilerParams(vmem_limit_bytes=mib * 2**20)


def product(source, rows, own, other, result, first, columns):
    depth, height = rows.shape
    pairs, width = own[0].shape
    tile = 1024 if height % 1024 == 0 else height
    args = [source, rows, *own, *other]
    in_specs = [SMEM] + [VMEM] * (len(args) - 1)
    aliases = {}
    if result is not None:
        aliases = {len(args): 0}
        in_specs.append(ANY)
        args.append(result)

    def kernel(source, rows, *refs):
        out, held = refs[-2:]

        @pl.when(pl.program_id(0) == 0)
        def _():
            for part, choices in ((pl.ds(0, pairs), own), (pl.ds(pairs, depth - pairs), other)):
                skip = 0 if choices is own else len(own)
                for i in range(len(choices)):
                    here = source[0] == i if i < len(choices) - 1 else source[0] >= i

                    @pl.when(here)
                    def _(part=part, i=skip + i):
                        held[part, :] = refs[i][...]

        at = pl.ds(pl.multiple_of(pl.program_id(0) * tile, tile), tile)
        out[...] = lax.dot_general(
            rows[:, at], held[...], (((0,), (0,)), ((), ())), preferred_element_type=jnp.float32
        )

    return pl.pallas_call(
        kernel,
        grid=(height // tile,),
        in_specs=in_specs,
        out_specs=pl.BlockSpec((pl.Element(tile), pl.Element(width)), lambda i: (i * tile, first)),
        out_shape=jax.ShapeDtypeStruct((height, columns), jnp.float32),
        scratch_shapes=[pltpu.VMEM((depth, width), jnp.bfloat16)],
        input_output_aliases=aliases,
        compiler_params=params(24),
        cost_estimate=pl.CostEstimate(
            flops=2 * height * width * depth, bytes_accessed=4 * height * width, transcendentals=0
        ),
    )(*args)


def weigh(index, slab, weights, other_parts, other_weights, width):
    pairs, height = slab.shape
    others = other_weights.shape[0]
    count = len(other_parts)
    step = 64 if pairs % 64 == 0 else pairs

    def kernel(index, slab, weights, other_weights, *refs):
        parts, out = refs[:count], refs[-1]

        def scaled(by, rows):
            return (by * rows.astype(jnp.float32)).astype(out.dtype)

        @pl.loop(0, pairs // step)
        def _(i):
            at = pl.ds(pl.multiple_of(i * step, step), step)
            out[at, :] = scaled(weights[at, :], slab[at, :])

        @pl.loop(0, others // step)
        def _(i):
            at = pl.ds(pl.multiple_of(i * step, step), step)
            to = pl.ds(pl.multiple_of(pairs + i * step, step), step)
            by = other_weights[at, :]
            offset = 0
            for part in parts:
                size = part.shape[1]
                start = lax.rem(index[0] * width + offset, height)
                out[to, pl.ds(pl.multiple_of(start, LANES), size)] = scaled(by, part[at, :])
                offset += size

    return pl.pallas_call(
        kernel,
        in_specs=[SMEM] + [VMEM] * (3 + count),
        out_specs=VMEM,
        out_shape=jax.ShapeDtypeStruct((pairs + others, height), slab.dtype),
        compiler_params=params(16),
    )(index, slab, weights[:, None], other_weights[:, None], *other_parts)


def assemble(core, mine, theirs, start, size, *earlier):
    count = len(mine)
    half = mine[0].shape[0]

    def kernel(core, *refs):
        out = refs[-1]
        for i in range(count):
            for rows, ref in ((core[0], refs[i]), (1 - core[0], refs[count + i])):
                at = pl.multiple_of((2 * i + rows) * half, half)
                out[pl.ds(at, half), :] = ref[:, start : start + size]

    return pl.pallas_call(
        kernel,
        in_specs=[SMEM] + [VMEM] * (2 * count) + [ANY] * len(earlier),
        out_specs=VMEM,
        out_shape=jax.ShapeDtypeStruct((2 * count * half, size), mine[0].dtype),
        compiler_params=params(16),
    )(core, *mine, *theirs, *earlier)


def hold(values, *earlier):
    count = len(values)

    def kernel(*refs):
        for value, out in zip(refs[:count], refs[-count:]):
            out[...] = value[...]

    return pl.pallas_call(
        kernel,
        in_specs=[VMEM] * count + [ANY] * len(earlier),
        out_specs=[VMEM] * count,
        out_shape=[jax.ShapeDtypeStruct(v.shape, v.dtype) for v in values],
        compiler_params=params(16),
    )(*values, *earlier)


def pick_senders(planes, columns, stage):
    per_side = columns // 2
    sends = [(k, b, t, side) for k, (_, part) in enumerate(stage) for b, t, side in part]
    chosen = [b // per_side if side is None else side for _, b, _, side in sends]

    def cost():
        load = {}
        for (k, b, t, _), side in zip(sends, chosen):
            way = 1 if t > b else -1
            links = [(side, z, way) for z in range(b, t, way)]
            if side != b // per_side:
                links.append((t, side, "across"))
            for link in links:
                load[link] = load.get(link, 0) + stage[k][0]
        return sum(value**6 for value in load.values())

    for i in sorted(range(len(sends)), key=lambda i: -abs(sends[i][1] - sends[i][2])):
        k, b, _, free = sends[i]
        if free is None and sum(s[:2] == (k, b) and c == chosen[i] for s, c in zip(sends, chosen)) > per_side:
            chosen[i] = 1 - chosen[i]
    best = cost()
    better = True
    while better:
        better = False
        for i, (k, b, _, free) in enumerate(sends):
            others = [j for j in range(len(sends)) if j > i and sends[j][3] is None]
            for flips in [[i]] + [[i, j] for j in others]:
                if free is not None:
                    continue
                before = list(chosen)
                for j in flips:
                    chosen[j] = 1 - chosen[j]
                full = any(
                    sum(s[:2] == sends[j][:2] and c == chosen[j] for s, c in zip(sends, chosen)) > per_side
                    for j in flips
                )
                value = best if full else cost()
                if value < best:
                    best, better = value, True
                else:
                    chosen[:] = before
    result = [{} for _ in stage]
    for (k, b, t, free), side in zip(sends, chosen):
        used = [c for (x, _), c in result[k].items() if x == b]
        columns_left = [c for c in range(side * per_side, (side + 1) * per_side) if c not in used]
        result[k][b, t] = columns_left[0] if free is None else b
    return result


def solution(mesh):
    R, C, Q = (mesh.shape[axis] for axis in AXES)
    every = [(b, t, None) for b in range(R) for t in range(R) if b != t]
    ends = [(b, t) for b, t, _ in every if t in (0, R - 1) and abs(b - t) > 1]
    forwards = [(1 if t == 0 else R - 2, t, b // (C // 2)) for b, t in ends]
    near, direct_own = pick_senders(R, C, [(3, [s for s in every if s[:2] not in ends]), (5, every)])
    _, direct_first = pick_senders(R, C, [(3, forwards), (5, every)])
    (direct_last,) = pick_senders(R, C, [(1, every)])

    def number(r, c, p):
        return (r * C + c) * Q + p

    def permute(block, moves):
        pairs = [(number(*source), number(*target)) for source, target in moves]
        return lax.ppermute(block, AXES, pairs) if pairs else jnp.zeros_like(block)

    def permute_all(block, route):
        every = [(r, c, p) for r in range(R) for c in range(C) for p in range(Q)]
        return permute(block, [(device, route(*device)) for device in every])

    def send(block, senders):
        return permute(
            block, [((b, c, p), (t, b, p)) for (b, t), c in senders.items() for p in range(Q)]
        )

    def forward(block):
        moves = [((1, b), (0, b)) for b in range(2, C)]
        moves += [((R - 2, b), (R - 1, b)) for b in range(R - 2)]
        return permute(block, [((*s, p), (*t, p)) for s, t in moves for p in range(Q)])

    def on_device(slab, weights):
        pairs, block = slab.shape
        width = block // Q
        wide = max(LANES, width * 5 // 8 // LANES * LANES)
        shifts = range(1, Q)
        r, c, p = (lax.axis_index(axis) for axis in AXES)
        core = c % 2

        def scalar(value):
            return value.astype(jnp.int32).reshape(1)

        far = ((r == 0) & (c >= 2)) | ((r == R - 1) & (c <= R - 3))
        source = scalar(jnp.where(r == c, 0, jnp.where(far, 2, 1)))
        core_index = scalar(core)

        def own_columns(start, size):
            return lax.dynamic_slice_in_dim(slab, p * width + start, size, 1)

        def share(shift, relative):
            start = (p - shift + relative) % Q * width
            return lax.dynamic_slice(slab, (core * (pairs // 2), start), (pairs // 2, width))

        def exchange(shares):
            return [
                permute_all(m, lambda r, c, p: (r, c, (p - s) % Q)) for s, m in zip(shifts, shares)
            ]

        def swap(mine):
            return [permute_all(m, lambda r, c, p: (r, c ^ 1, p)) for m in mine]

        own0, own1 = own_columns(0, wide), own_columns(wide, width - wide)
        near1, direct0 = send(own1, near), send(own0, direct_own)
        mine = hold(exchange([share(s, 0) for s in shifts]), near1)
        theirs = swap(mine)
        rest_mine = [exchange(hold([share(s, j) for s in shifts], *mine)) for j in range(1, Q)]
        far1 = forward(near1)
        other0 = assemble(core_index, mine, theirs, 0, wide, direct0)
        other1 = assemble(core_index, mine, theirs, wide, width - wide)
        direct_other0 = send(other0, direct_first)
        rest = [assemble(core_index, m, swap(m), 0, width) for m in rest_mine]
        other_weights = jnp.concatenate(
            [permute_all(weights, lambda r, c, p: (r, c, (p - s) % Q)) for s in shifts]
        )
        rows = weigh(scalar(p), slab, weights, [other0, other1, *rest], other_weights, width)
        direct_other1 = send(hold([other1], rows, far1, direct_other0)[0], direct_last)
        result = product(source, rows, [own0, direct0], [other0, direct_other0], None, 0, width)
        return product(
            source, rows, [own1, near1, far1], [other1, direct_other1], result, wide, width
        )

    return jax.shard_map(
        on_device,
        mesh=mesh,
        in_specs=(P("pair", "row"), P("pair")),
        out_specs=P("row", ("col", "pair")),
        check_vma=False,
    )
```

time: 211 us -> 99.5 us (0.47)
  waiting for transfers between devices: 123 us -> 25.9 us
  blocking collectives: 35.5 us -> 0 us
  starting transfers between devices: 3.99 us -> 36.7 us
  Pallas kernels: 0 us -> 29.7 us
  matrix products: 23.4 us -> 0 us
  between operations: 14.9 us -> 0.22 us
    psum x1 -> x0, waiting for transfers between devices: 123 us -> none  [from_root(): return lax.psum(block, axis)]
    ppermute x0 -> x10, starting transfers between devices: none -> 36.7 us  [permute(): return lax.ppermute(block, AXES, pairs) if pairs else jnp.zeros_like(block)]
    all_gather x1 -> x0, blocking collectives: 35.5 us -> none  [on_device(): lax.all_gather(pair_weights.astype(jnp.bfloat16), 'pair', axis=0, tiled=T...]
    pallas_call x0 -> x9, Pallas kernels: none -> 29.7 us  [the longest x2 22.6 us: product(): pl.pallas_call(kernel, grid=(height // tile,), in_specs=in_specs, out_spe...]
    ppermute x0 -> x10, waiting for transfers between devices: none -> 25.9 us  [permute(): return lax.ppermute(block, AXES, pairs) if pairs else jnp.zeros_like(block)]
    dot_general x1 -> x0, matrix products: 23.4 us -> none  [contract_pairs(): lax.dot_general(left, right, (((0,), (0,)), ((), ())), preferred_element_...]
    all_to_all x1 -> x0, starting transfers between devices: 3.95 us -> none  [on_device(): lax.all_to_all(column_block, 'pair', split_axis=1, concat_axis=0, tiled=T...]
    dynamic_slice x0 -> x3, local copies, waits for them, and re-layouts: none -> 3.84 us  [the longest x1 2.87 us: share(): lax.dynamic_slice(slab, (core * (pairs // 2), start), (pairs // 2, width))]
  transfers between devices with their start and end apart: 3 -> 10, of which waited for: 1 -> 6; matrix products, arithmetic and copies ran while one was open for 1% -> 1% of each run, Pallas kernels for 0% -> 21%
where the time goes in v2:
time: 99.5 us; the launch traced here: 99.1 us
  starting transfers between devices  36.7 us (37%)
  Pallas kernels  29.7 us (30%)
  waiting for transfers between devices  25.9 us (26%)
  local copies, waits for them, and re-layouts  6.48 us (7%)
    ppermute x10, starting transfers between devices, permute(): return lax.ppermute(block, AXES, pairs) if pairs else jnp.zeros_like(block)  36.7 us
    ppermute x10, waiting for transfers between devices, permute(): return lax.ppermute(block, AXES, pairs) if pairs else jnp.zeros_like(block)  25.9 us
    pallas_call x2, Pallas kernels, product(): pl.pallas_call(kernel, grid=(height // tile,), in_specs=in_specs, out_spe...  22.6 us
    pallas_call x1, Pallas kernels, weigh(): pl.pallas_call(kernel, in_specs=[SMEM] + [VMEM] * (3 + count), out_specs=...  3.14 us
    dynamic_slice x1, local copies, waits for them, and re-layouts, share(): lax.dynamic_slice(slab, (core * (pairs // 2), start), (pairs // 2, width))  2.87 us
    pallas_call x3, Pallas kernels, assemble(): pl.pallas_call(kernel, in_specs=[SMEM] + [VMEM] * (2 * count) + [ANY] * l...  2.64 us
    unnamed x22, local copies, waits for them, and re-layouts  2.44 us
  transfers between devices with their start and end apart: 10, of which 6 were waited for; matrix products, arithmetic and copies ran while one was open for 1% of the time, Pallas kernels for 21%

profile of v2, /device:TPU:1, one launch (start us, length us, event | category | flops | bytes accessed | tf_op | source)
XLA Modules:
  0.0 99.1 jit_solution(11126872260779558372)
XLA Ops:
  0.0 0.0 copy-start
  0.0 2.9 %fusion = (bf16[192,2048]{1,0:T(8,128)(2,1)}, bf16[192,2048]{1,0:T(8,128)(2,1)}) fusion(bf16[384,4096]{1,0:T(8,128)(2,1)} %slab.1, s32[]{:T(128)S(6)} %select_n.42, s32[]{:T(128)S(6)} %select_n.48, s32[]{:T(128)S(6)} %select_n.44), kind=kLoop, calls=%fused_computation.2 | loop fusion | bytes 3145740 | tf_op jit(solution)/shard_map/dynamic_slice | solution.py:238
  2.9 2.1 %collective-permute-start.1 = (bf16[192,2048]{1,0:T(8,128)(2,1)}, bf16[192,2048]{1,0:T(8,128)(2,1)}, u32[]{:S(2)}, u32[]{:S(2)}) collective-permute-start(bf16[192,2048]{1,0:T(8,128)(2,1)} %get-tuple-element.6), channel_id=1, source_target_pairs={{0,1},{1,0},{2,3},{3,2},{4,5},{5,4},{6,7},{7,6},{8,9},{9,8},{10,11... | collective-permute-start | bytes 2359304 | tf_op jit(solution)/shard_map/ppermute | solution.py:202
  4.9 0.0 copy-done
  4.9 0.9 constant_dynamic-slice_fusion.1.refs_0_
  5.8 1.3 %collective-permute-start.2 = (bf16[384,768]{1,0:T(8,128)(2,1)}, bf16[384,768]{1,0:T(8,128)(2,1)}, u32[]{:S(2)}, u32[]{:S(2)}) collective-permute-start(bf16[384,768]{1,0:T(8,128)(2,1)} %constant_dynamic-slice_fusion.1.refs_0_), channel_id=1, source_target_pairs={{4,8},{5,9},{6,16},{7,17},{12,2},{13,3},{8,18},{9,19},{20,12},{21,... | collective-permute-start | bytes 1769480 | tf_op jit(solution)/shard_map/ppermute | solution.py:202
  7.1 0.0 copy-start.7
  7.1 0.1 constant_dynamic-slice_fusion.refs_0_
  7.2 0.0 copy-start.3
  7.2 8.3 %collective-permute-start.4 = (bf16[384,1280]{1,0:T(8,128)(2,1)S(1)}, bf16[384,1280]{1,0:T(8,128)(2,1)S(1)}, u32[]{:S(2)}, u32[]{:S(2)}) collective-permute-start(bf16[384,1280]{1,0:T(8,128)(2,1)S(1)} %constant_dynamic-slice_fusion.refs_0_), channel_id=1, source_target_pairs={{0,8},{1,9},{2,16},{3,17},{4,24},{5,25},{12,2},{13,3},{8,18},{9,19... | collective-permute-start | bytes 2949128 | tf_op jit(solution)/shard_map/ppermute | solution.py:202
  15.5 3.1 %collective-permute-done.2.refs_1_ = bf16[384,768]{1,0:T(8,128)(2,1)} collective-permute-done((bf16[384,768]{1,0:T(8,128)(2,1)}, bf16[384,768]{1,0:T(8,128)(2,1)}, u32[]{:S(2)}, u32[]{:S(2)}) %collective-permute-start.2) | collective-permute-done | bytes 589856 | tf_op jit(solution)/shard_map/ppermute | solution.py:202
  18.7 3.9 %collective-permute-done.1.refs_0_ = bf16[192,2048]{1,0:T(8,128)(2,1)} collective-permute-done((bf16[192,2048]{1,0:T(8,128)(2,1)}, bf16[192,2048]{1,0:T(8,128)(2,1)}, u32[]{:S(2)}, u32[]{:S(2)}) %collective-permute-start.1) | collective-permute-done | bytes 786464 | tf_op jit(solution)/shard_map/ppermute | solution.py:202
  22.5 1.2 %shard_map.28.refs_0_.refs_1_ = bf16[192,2048]{1,0:T(8,128)(2,1)S(1)} custom-call(bf16[192,2048]{1,0:T(8,128)(2,1)} %collective-permute-done.1.refs_0_, bf16[384,768]{1,0:T(8,128)(2,1)} %collective-permute-done.2.refs_1_), custom_call_target="tpu_custom_call" | custom-call | tf_op jit(solution)/shard_map/pallas_call | solution.py:130
  23.7 0.0 copy-start.1
  23.7 0.0 copy-start.10
  23.7 1.3 %collective-permute-start.3 = (bf16[192,2048]{1,0:T(8,128)(2,1)S(1)}, bf16[192,2048]{1,0:T(8,128)(2,1)S(1)}, u32[]{:S(2)}, u32[]{:S(2)}) collective-permute-start(bf16[192,2048]{1,0:T(8,128)(2,1)S(1)} %shard_map.28.refs_0_.refs_1_), channel_id=1, source_target_pairs={{0,2},{1,3},{2,0},{3,1},{4,6},{5,7},{6,4},{7,5},{8,10},{9,11},{10,... | collective-permute-start | bytes 2359304 | tf_op jit(solution)/shard_map/ppermute | solution.py:202
  25.0 0.0 copy-done.7
  25.0 0.1 shard_map.31
  25.1 1.5 %collective-permute-start.5 = (bf16[192,2048]{1,0:T(8,128)(2,1)S(1)}, bf16[192,2048]{1,0:T(8,128)(2,1)}, u32[]{:S(2)}, u32[]{:S(2)}) collective-permute-start(bf16[192,2048]{1,0:T(8,128)(2,1)S(1)} %shard_map.31), channel_id=1, source_target_pairs={{0,1},{1,0},{2,3},{3,2},{4,5},{5,4},{6,7},{7,6},{8,9},{9,8},{10,11... | collective-permute-start | bytes 2359304 | tf_op jit(solution)/shard_map/ppermute | solution.py:202
  26.6 8.3 %collective-permute-done.4.refs_2_.refs_1_ = bf16[384,1280]{1,0:T(8,128)(2,1)S(1)} collective-permute-done((bf16[384,1280]{1,0:T(8,128)(2,1)S(1)}, bf16[384,1280]{1,0:T(8,128)(2,1)S(1)}, u32[]{:S(2)}, u32[]{:S(2)}) %collective-permute-start.4) | collective-permute-done | bytes 983072 | tf_op jit(solution)/shard_map/ppermute | solution.py:202
  34.9 0.0 copy-start.5
  34.9 0.0 collective-permute-done.3.refs_1_
  34.9 0.0 copy-done.3
  34.9 0.0 copy-start.8
  35.0 0.0 copy-done.1
  35.0 1.1 %shard_map.29.refs_0_.refs_2_ = bf16[384,1280]{1,0:T(8,128)(2,1)} custom-call(s32[1]{0:T(128)} %bitcast.2.core, bf16[192,2048]{1,0:T(8,128)(2,1)S(1)} %shard_map.28.refs_0_.refs_1_, bf16[192,2048]{1,0:T(8,128)(2,1)S(1)} %collective-permute-done.3.refs_1_, bf16[384,1280]{1,0:T(8,128)(2,1)S(1)} %collective-permute-done.4.refs_2_.refs_1_), custom_call_target="tpu_custom_call" | custom-call | tf_op jit(solution)/shard_map/pallas_call | solution.py:114
  36.1 0.1 copy-done.5
  36.2 6.5 %collective-permute-start.8 = (bf16[384,1280]{1,0:T(8,128)(2,1)}, bf16[384,1280]{1,0:T(8,128)(2,1)}, u32[]{:S(2)}, u32[]{:S(2)}) collective-permute-start(bf16[384,1280]{1,0:T(8,128)(2,1)} %shard_map.29.refs_0_.refs_2_), channel_id=1, source_target_pairs={{0,8},{1,9},{4,16},{5,17},{2,24},{3,25},{12,2},{13,3},{8,18},{9,19... | collective-permute-start | bytes 2949128 | tf_op jit(solution)/shard_map/ppermute | solution.py:202
  42.8 0.0 copy-done.8
  42.8 1.6 %collective-permute-done.5.refs_0_ = bf16[192,2048]{1,0:T(8,128)(2,1)} collective-permute-done((bf16[192,2048]{1,0:T(8,128)(2,1)S(1)}, bf16[192,2048]{1,0:T(8,128)(2,1)}, u32[]{:S(2)}, u32[]{:S(2)}) %collective-permute-start.5) | collective-permute-done | bytes 786464 | tf_op jit(solution)/shard_map/ppermute | solution.py:202
  44.4 0.8 collective-permute-start.6
  45.2 1.5 %collective-permute-start.7 = (bf16[384,768]{1,0:T(8,128)(2,1)}, bf16[384,768]{1,0:T(8,128)(2,1)}, u32[]{:S(2)}, u32[]{:S(2)}) collective-permute-start(bf16[384,768]{1,0:T(8,128)(2,1)} %collective-permute-done.2.refs_1_), channel_id=1, source_target_pairs={{12,4},{13,5},{14,6},{15,7},{16,24},{17,25},{18,26},{19,27}} | collective-permute-start | bytes 1769480 | tf_op jit(solution)/shard_map/ppermute | solution.py:202
  46.7 0.0 copy-done.10
  46.7 1.5 %collective-permute-start = (f32[384]{0:T(512)S(1)}, f32[384]{0:T(512)S(1)}, u32[]{:S(2)}, u32[]{:S(2)}) collective-permute-start(f32[384]{0:T(512)S(1)} %copy-done.10), channel_id=1, source_target_pairs={{0,1},{1,0},{2,3},{3,2},{4,5},{5,4},{6,7},{7,6},{8,9},{9,8},{10,11... | collective-permute-start | bytes 4616 | tf_op jit(solution)/shard_map/ppermute | solution.py:202
  48.2 0.1 broadcast_in_dim.8.weights
  48.3 0.8 collective-permute-done
  49.1 0.1 broadcast_in_dim.9.other_weights
  49.2 0.0 copy-start.2
  49.3 1.1 %copy-done.2 = bf16[192,2048]{1,0:T(8,128)(2,1)S(1)} copy-done((bf16[192,2048]{1,0:T(8,128)(2,1)S(1)}, bf16[192,2048]{1,0:T(8,128)(2,1)}, u32[]{:S(2)}) %copy-start.2) | copy-done | bytes 786456
  50.4 0.0 copy-start.9
  50.4 1.1 %copy-done.9 = bf16[192,2048]{1,0:T(8,128)(2,1)S(1)} copy-done((bf16[192,2048]{1,0:T(8,128)(2,1)S(1)}, bf16[192,2048]{1,0:T(8,128)(2,1)}, u32[]{:S(2)}) %copy-start.9) | copy-done | bytes 786456
  51.6 0.0 collective-permute-done.6.refs_1_
  51.6 1.5 %shard_map.32.refs_2_ = bf16[384,2048]{1,0:T(8,128)(2,1)S(1)} custom-call(s32[1]{0:T(128)} %bitcast.2.core, bf16[192,2048]{1,0:T(8,128)(2,1)} %collective-permute-done.5.refs_0_, bf16[192,2048]{1,0:T(8,128)(2,1)} %collective-permute-done.6.refs_1_), custom_call_target="tpu_custom_call" | custom-call | tf_op jit(solution)/shard_map/pallas_call | solution.py:114
  53.1 3.1 %shard_map.33.refs_1_.rows = bf16[768,4096]{1,0:T(8,128)(2,1)S(1)} custom-call(s32[1]{0:T(128)} %bitcast.1.index, bf16[384,4096]{1,0:T(8,128)(2,1)S(1)} %copy-done, f32[384,1]{1,0:T(8,128)S(1)} %broadcast_in_dim.8.weights, f32[384,1]{1,0:T(8,128)S(1)} %broadcast_in_dim.9.other_weights, bf16[384,1280]{1,0:T(8,128)(2,1)} %shard_map.29.refs_0_.refs_2_, ...), custom_call_target="tpu_custom_call" | custom-call | tf_op jit(solution)/shard_map/pallas_call | solution.py:94
  56.2 0.0 copy-start.4
  56.2 0.0 copy-start.6
  56.2 0.0 collective-permute-done.7.refs_2_
  56.2 8.2 %collective-permute-done.8.refs_3_ = bf16[384,1280]{1,0:T(8,128)(2,1)} collective-permute-done((bf16[384,1280]{1,0:T(8,128)(2,1)}, bf16[384,1280]{1,0:T(8,128)(2,1)}, u32[]{:S(2)}, u32[]{:S(2)}) %collective-permute-start.8) | collective-permute-done | bytes 983072 | tf_op jit(solution)/shard_map/ppermute | solution.py:202
  64.4 12.0 %collective-permute-start.9 = (bf16[384,768]{1,0:T(8,128)(2,1)S(1)}, bf16[384,768]{1,0:T(8,128)(2,1)S(1)}, u32[]{:S(2)}, u32[]{:S(2)}) collective-permute-start(bf16[384,768]{1,0:T(8,128)(2,1)S(1)} %shard_map.34), channel_id=1, source_target_pairs={{0,8},{1,9},{4,16},{5,17},{2,24},{3,25},{8,2},{9,3},{10,18},{11,19... | collective-permute-start | bytes 1769480 | tf_op jit(solution)/shard_map/ppermute | solution.py:202
  76.4 0.0 copy-done.4
  76.4 0.0 copy-done.6
  76.4 13.3 %shard_map.35.refs_5_ = f32[4096,2048]{1,0:T(8,128)} custom-call(s32[1]{0:T(128)} %bitcast.source, bf16[768,4096]{1,0:T(8,128)(2,1)S(1)} %shard_map.33.refs_1_.rows, bf16[384,1280]{1,0:T(8,128)(2,1)S(1)} %copy-done.4, bf16[384,1280]{1,0:T(8,128)(2,1)S(1)} %copy-done.6, bf16[384,1280]{1,0:T(8,128)(2,1)} %shard_map.29.refs_0_.refs_2_, ...), custom_call_target="tpu_custom_call" | custom-call | flops 8053063680 | bytes 20971520 | tf_op jit(solution)/shard_map/pallas_call | solution.py:50
  89.7 0.0 collective-permute-done.9.refs_4_
  89.7 9.3 %shard_map.36 = f32[4096,2048]{1,0:T(8,128)} custom-call(s32[1]{0:T(128)} %bitcast.source, bf16[768,4096]{1,0:T(8,128)(2,1)S(1)} %shard_map.33.refs_1_.rows, bf16[384,768]{1,0:T(8,128)(2,1)} %constant_dynamic-slice_fusion.1.refs_0_, bf16[384,768]{1,0:T(8,128)(2,1)} %collective-permute-done.2.refs_1_, ...), custom_call_target="tpu_custom_call", output_to_operand_aliasing={{}: (7, {})} | custom-call | flops 4831838208 | bytes 12582912 | tf_op jit(solution)/shard_map/pallas_call | solution.py:50
  (2 shorter events, 0.1 us)
Async XLA Ops:
  0.0 4.9 %copy-start = (bf16[384,4096]{1,0:T(8,128)(2,1)S(1)}, bf16[384,4096]{1,0:T(8,128)(2,1)}, u32[]{:S(2)}) copy-start(bf16[384,4096]{1,0:T(8,128)(2,1)} %slab.1) | copy-start | bytes 9437188
  2.9 19.6 %collective-permute-start.1 = (bf16[192,2048]{1,0:T(8,128)(2,1)}, bf16[192,2048]{1,0:T(8,128)(2,1)}, u32[]{:S(2)}, u32[]{:S(2)}) collective-permute-start(bf16[192,2048]{1,0:T(8,128)(2,1)} %get-tuple-element.6), channel_id=1, source_target_pairs={{0,1},{1,0},{2,3},{3,2},{4,5},{5,4},{6,7},{7,6},{8,9},{9,8},{10,11... | collective-permute-start | bytes 2359304 | tf_op jit(solution)/shard_map/ppermute | solution.py:202
  5.8 12.8 %collective-permute-start.2 = (bf16[384,768]{1,0:T(8,128)(2,1)}, bf16[384,768]{1,0:T(8,128)(2,1)}, u32[]{:S(2)}, u32[]{:S(2)}) collective-permute-start(bf16[384,768]{1,0:T(8,128)(2,1)} %constant_dynamic-slice_fusion.1.refs_0_), channel_id=1, source_target_pairs={{4,8},{5,9},{6,16},{7,17},{12,2},{13,3},{8,18},{9,19},{20,12},{21,... | collective-permute-start | bytes 1769480 | tf_op jit(solution)/shard_map/ppermute | solution.py:202
  7.1 17.9 %copy-start.7 = (bf16[192,2048]{1,0:T(8,128)(2,1)S(1)}, bf16[192,2048]{1,0:T(8,128)(2,1)}, u32[]{:S(2)}) copy-start(bf16[192,2048]{1,0:T(8,128)(2,1)} %get-tuple-element.5.refs_0_) | copy-start | bytes 2359300
  7.2 27.7 %copy-start.3 = (bf16[384,1280]{1,0:T(8,128)(2,1)}, bf16[384,1280]{1,0:T(8,128)(2,1)S(1)}, u32[]{:S(2)}) copy-start(bf16[384,1280]{1,0:T(8,128)(2,1)S(1)} %constant_dynamic-slice_fusion.refs_0_) | copy-start | bytes 2949124
  7.2 27.7 %collective-permute-start.4 = (bf16[384,1280]{1,0:T(8,128)(2,1)S(1)}, bf16[384,1280]{1,0:T(8,128)(2,1)S(1)}, u32[]{:S(2)}, u32[]{:S(2)}) collective-permute-start(bf16[384,1280]{1,0:T(8,128)(2,1)S(1)} %constant_dynamic-slice_fusion.refs_0_), channel_id=1, source_target_pairs={{0,8},{1,9},{2,16},{3,17},{4,24},{5,25},{12,2},{13,3},{8,18},{9,19... | collective-permute-start | bytes 2949128 | tf_op jit(solution)/shard_map/ppermute | solution.py:202
  23.7 11.2 %copy-start.1 = (bf16[192,2048]{1,0:T(8,128)(2,1)}, bf16[192,2048]{1,0:T(8,128)(2,1)S(1)}, u32[]{:S(2)}) copy-start(bf16[192,2048]{1,0:T(8,128)(2,1)S(1)} %shard_map.28.refs_0_.refs_1_) | copy-start | bytes 2359300
  23.7 23.0 %copy-start.10 = (f32[384]{0:T(512)S(1)}, f32[384]{0:T(512)}, u32[]{:S(2)}) copy-start(f32[384]{0:T(512)} %param.3) | copy-start | bytes 4612
  23.7 11.2 %collective-permute-start.3 = (bf16[192,2048]{1,0:T(8,128)(2,1)S(1)}, bf16[192,2048]{1,0:T(8,128)(2,1)S(1)}, u32[]{:S(2)}, u32[]{:S(2)}) collective-permute-start(bf16[192,2048]{1,0:T(8,128)(2,1)S(1)} %shard_map.28.refs_0_.refs_1_), channel_id=1, source_target_pairs={{0,2},{1,3},{2,0},{3,1},{4,6},{5,7},{6,4},{7,5},{8,10},{9,11},{10,... | collective-permute-start | bytes 2359304 | tf_op jit(solution)/shard_map/ppermute | solution.py:202
  25.1 19.3 %collective-permute-start.5 = (bf16[192,2048]{1,0:T(8,128)(2,1)S(1)}, bf16[192,2048]{1,0:T(8,128)(2,1)}, u32[]{:S(2)}, u32[]{:S(2)}) collective-permute-start(bf16[192,2048]{1,0:T(8,128)(2,1)S(1)} %shard_map.31), channel_id=1, source_target_pairs={{0,1},{1,0},{2,3},{3,2},{4,5},{5,4},{6,7},{7,6},{8,9},{9,8},{10,11... | collective-permute-start | bytes 2359304 | tf_op jit(solution)/shard_map/ppermute | solution.py:202
  34.9 1.3 %copy-start.5 = (bf16[384,1280]{1,0:T(8,128)(2,1)}, bf16[384,1280]{1,0:T(8,128)(2,1)S(1)}, u32[]{:S(2)}) copy-start(bf16[384,1280]{1,0:T(8,128)(2,1)S(1)} %collective-permute-done.4.refs_2_.refs_1_) | copy-start | bytes 2949124
  34.9 7.8 %copy-start.8 = (bf16[192,2048]{1,0:T(8,128)(2,1)}, bf16[192,2048]{1,0:T(8,128)(2,1)S(1)}, u32[]{:S(2)}) copy-start(bf16[192,2048]{1,0:T(8,128)(2,1)S(1)} %collective-permute-done.3.refs_1_) | copy-start | bytes 2359300
  36.2 28.2 %collective-permute-start.8 = (bf16[384,1280]{1,0:T(8,128)(2,1)}, bf16[384,1280]{1,0:T(8,128)(2,1)}, u32[]{:S(2)}, u32[]{:S(2)}) collective-permute-start(bf16[384,1280]{1,0:T(8,128)(2,1)} %shard_map.29.refs_0_.refs_2_), channel_id=1, source_target_pairs={{0,8},{1,9},{4,16},{5,17},{2,24},{3,25},{12,2},{13,3},{8,18},{9,19... | collective-permute-start | bytes 2949128 | tf_op jit(solution)/shard_map/ppermute | solution.py:202
  44.4 7.2 %collective-permute-start.6 = (bf16[192,2048]{1,0:T(8,128)(2,1)}, bf16[192,2048]{1,0:T(8,128)(2,1)}, u32[]{:S(2)}, u32[]{:S(2)}) collective-permute-start(bf16[192,2048]{1,0:T(8,128)(2,1)} %collective-permute-done.5.refs_0_), channel_id=1, source_target_pairs={{0,2},{1,3},{2,0},{3,1},{4,6},{5,7},{6,4},{7,5},{8,10},{9,11},{10,... | collective-permute-start | bytes 2359304 | tf_op jit(solution)/shard_map/ppermute | solution.py:202
  45.2 11.0 %collective-permute-start.7 = (bf16[384,768]{1,0:T(8,128)(2,1)}, bf16[384,768]{1,0:T(8,128)(2,1)}, u32[]{:S(2)}, u32[]{:S(2)}) collective-permute-start(bf16[384,768]{1,0:T(8,128)(2,1)} %collective-permute-done.2.refs_1_), channel_id=1, source_target_pairs={{12,4},{13,5},{14,6},{15,7},{16,24},{17,25},{18,26},{19,27}} | collective-permute-start | bytes 1769480 | tf_op jit(solution)/shard_map/ppermute | solution.py:202
  46.7 2.4 %collective-permute-start = (f32[384]{0:T(512)S(1)}, f32[384]{0:T(512)S(1)}, u32[]{:S(2)}, u32[]{:S(2)}) collective-permute-start(f32[384]{0:T(512)S(1)} %copy-done.10), channel_id=1, source_target_pairs={{0,1},{1,0},{2,3},{3,2},{4,5},{5,4},{6,7},{7,6},{8,9},{9,8},{10,11... | collective-permute-start | bytes 4616 | tf_op jit(solution)/shard_map/ppermute | solution.py:202
  49.2 1.1 %copy-start.2 = (bf16[192,2048]{1,0:T(8,128)(2,1)S(1)}, bf16[192,2048]{1,0:T(8,128)(2,1)}, u32[]{:S(2)}) copy-start(bf16[192,2048]{1,0:T(8,128)(2,1)} %copy-done.1) | copy-start | bytes 2359300
  50.4 1.1 %copy-start.9 = (bf16[192,2048]{1,0:T(8,128)(2,1)S(1)}, bf16[192,2048]{1,0:T(8,128)(2,1)}, u32[]{:S(2)}) copy-start(bf16[192,2048]{1,0:T(8,128)(2,1)} %copy-done.8) | copy-start | bytes 2359300
  56.2 20.2 %copy-start.4 = (bf16[384,1280]{1,0:T(8,128)(2,1)S(1)}, bf16[384,1280]{1,0:T(8,128)(2,1)}, u32[]{:S(2)}) copy-start(bf16[384,1280]{1,0:T(8,128)(2,1)} %copy-done.3) | copy-start | bytes 2949124
  56.2 20.2 %copy-start.6 = (bf16[384,1280]{1,0:T(8,128)(2,1)S(1)}, bf16[384,1280]{1,0:T(8,128)(2,1)}, u32[]{:S(2)}) copy-start(bf16[384,1280]{1,0:T(8,128)(2,1)} %copy-done.5) | copy-start | bytes 2949124
  64.4 25.3 %collective-permute-start.9 = (bf16[384,768]{1,0:T(8,128)(2,1)S(1)}, bf16[384,768]{1,0:T(8,128)(2,1)S(1)}, u32[]{:S(2)}, u32[]{:S(2)}) collective-permute-start(bf16[384,768]{1,0:T(8,128)(2,1)S(1)} %shard_map.34), channel_id=1, source_target_pairs={{0,8},{1,9},{4,16},{5,17},{2,24},{3,25},{8,2},{9,3},{10,18},{11,19... | collective-permute-start | bytes 1769480 | tf_op jit(solution)/shard_map/ppermute | solution.py:202

commit v3 on v2

--- a/solution.py
+++ b/solution.py
@@ -100,24 +100,55 @@
     )(index, slab, weights[:, None], other_weights[:, None], *other_parts)
 
 
-def assemble(core, mine, theirs, start, size, *earlier):
-    count = len(mine)
-    half = mine[0].shape[0]
+def cut_out(starts, slab, shapes):
+    count = len(shapes)
+
+    def kernel(starts, slab, *refs):
+        outs, done = refs[:count], refs[-1]
+        copies = []
+        for i, (rows, size) in enumerate(shapes):
+            at = pl.ds(pl.multiple_of(starts[2 * i], 16), rows)
+            across = pl.ds(pl.multiple_of(starts[2 * i + 1], LANES), size)
+            copies.append(pltpu.make_async_copy(slab.at[at, across], outs[i], done.at[i]))
+        for copy in copies:
+            copy.start()
+        for copy in copies:
+            copy.wait()
+
+    return pl.pallas_call(
+        kernel,
+        in_specs=[SMEM, ANY],
+        out_specs=[VMEM] * count,
+        out_shape=[jax.ShapeDtypeStruct(shape, slab.dtype) for shape in shapes],
+        scratch_shapes=[pltpu.SemaphoreType.DMA((count,))],
+        compiler_params=params(16),
+    )(starts, slab)
+
+
+def assemble(core, pieces, *earlier):
+    count = len(pieces[0][0])
+    half = pieces[0][0][0].shape[0]
+    sizes = [mine[0].shape[1] for mine, _ in pieces]
 
     def kernel(core, *refs):
         out = refs[-1]
-        for i in range(count):
-            for rows, ref in ((core[0], refs[i]), (1 - core[0], refs[count + i])):
-                at = pl.multiple_of((2 * i + rows) * half, half)
-                out[pl.ds(at, half), :] = ref[:, start : start + size]
-
-    return pl.pallas_call(
-        kernel,
-        in_specs=[SMEM] + [VMEM] * (2 * count) + [ANY] * len(earlier),
+        refs = list(refs)
+        start = 0
+        for size in sizes:
+            for first in (core[0], 1 - core[0]):
+                for i in range(count):
+                    at = pl.multiple_of((2 * i + first) * half, half)
+                    out[pl.ds(at, half), start : start + size] = refs.pop(0)[...]
+            start += size
+
+    parts = [array for mine, theirs in pieces for array in (*mine, *theirs)]
+    return pl.pallas_call(
+        kernel,
+        in_specs=[SMEM] + [VMEM] * len(parts) + [ANY] * len(earlier),
         out_specs=VMEM,
-        out_shape=jax.ShapeDtypeStruct((2 * count * half, size), mine[0].dtype),
+        out_shape=jax.ShapeDtypeStruct((2 * count * half, sum(sizes)), parts[0].dtype),
         compiler_params=params(16),
-    )(core, *mine, *theirs, *earlier)
+    )(core, *parts, *earlier)
 
 
 def hold(values, *earlier):
@@ -192,7 +223,7 @@
     forwards = [(1 if t == 0 else R - 2, t, b // (C // 2)) for b, t in ends]
     near, direct_own = pick_senders(R, C, [(3, [s for s in every if s[:2] not in ends]), (5, every)])
     _, direct_first = pick_senders(R, C, [(3, forwards), (5, every)])
-    (direct_last,) = pick_senders(R, C, [(1, every)])
+
 
     def number(r, c, p):
         return (r * C + c) * Q + p
@@ -219,6 +250,7 @@
         pairs, block = slab.shape
         width = block // Q
         wide = max(LANES, width * 5 // 8 // LANES * LANES)
+        cut = max(LANES, wide // 2 // LANES * LANES)
         shifts = range(1, Q)
         r, c, p = (lax.axis_index(axis) for axis in AXES)
         core = c % 2
@@ -230,12 +262,9 @@
         source = scalar(jnp.where(r == c, 0, jnp.where(far, 2, 1)))
         core_index = scalar(core)
 
-        def own_columns(start, size):
-            return lax.dynamic_slice_in_dim(slab, p * width + start, size, 1)
-
-        def share(shift, relative):
-            start = (p - shift + relative) % Q * width
-            return lax.dynamic_slice(slab, (core * (pairs // 2), start), (pairs // 2, width))
+        def share(shift, relative, offset, size):
+            start = (p - shift + relative) % Q * width + offset
+            return (core * (pairs // 2), start), (pairs // 2, size)
 
         def exchange(shares):
             return [
@@ -245,21 +274,35 @@
         def swap(mine):
             return [permute_all(m, lambda r, c, p: (r, c ^ 1, p)) for m in mine]
 
-        own0, own1 = own_columns(0, wide), own_columns(wide, width - wide)
+        spans = [(0, cut), (cut, wide - cut), (wide, width - wide)]
+        spans = [(start, size) for start, size in spans if size]
+        blocks = [((0, p * width + wide), (pairs, width - wide)), ((0, p * width), (pairs, wide))]
+        blocks += [share(s, 0, *span) for span in spans for s in shifts]
+        blocks += [share(s, j, 0, width) for j in range(1, Q) for s in shifts]
+        starts = jnp.stack([jnp.asarray(x, jnp.int32) for start, _ in blocks for x in start])
+        own1, own0, *shares = cut_out(starts, slab, [shape for _, shape in blocks])
+
+        def take():
+            return [shares.pop(0) for _ in shifts]
+
         near1, direct0 = send(own1, near), send(own0, direct_own)
-        mine = hold(exchange([share(s, 0) for s in shifts]), near1)
-        theirs = swap(mine)
-        rest_mine = [exchange(hold([share(s, j) for s in shifts], *mine)) for j in range(1, Q)]
+        pieces = []
+        for _ in spans:
+            m = exchange(take())
+            pieces.append((m, swap(m)))
+        mine = [m for piece, _ in pieces for m in piece]
+        rest_mine = [exchange(hold(take(), *mine)) for j in range(1, Q)]
         far1 = forward(near1)
-        other0 = assemble(core_index, mine, theirs, 0, wide, direct0)
-        other1 = assemble(core_index, mine, theirs, wide, width - wide)
+        other0 = assemble(core_index, pieces[:-1], direct0)
+        other1 = assemble(core_index, pieces[-1:])
         direct_other0 = send(other0, direct_first)
-        rest = [assemble(core_index, m, swap(m), 0, width) for m in rest_mine]
+        rest_mine = [hold(m, far1) for m in rest_mine]
+        rest = [assemble(core_index, [(m, swap(m))]) for m in rest_mine]
         other_weights = jnp.concatenate(
             [permute_all(weights, lambda r, c, p: (r, c, (p - s) % Q)) for s in shifts]
         )
         rows = weigh(scalar(p), slab, weights, [other0, other1, *rest], other_weights, width)
-        direct_other1 = send(hold([other1], rows, far1, direct_other0)[0], direct_last)
+        direct_other1 = send(hold([other1], rows, direct_other0)[0], direct_first)
         result = product(source, rows, [own0, direct0], [other0, direct_other0], None, 0, width)
         return product(
             source, rows, [own1, near1, far1], [other1, direct_other1], result, wide, width

time: 99.5 us -> 93.9 us (0.944)
  the two profiles are of different devices: /device:TPU:1 before, /device:TPU:11 now
where the time goes in v3:
time: 93.9 us; the launch traced here: 93.6 us
  Pallas kernels  30 us (32%)
  starting transfers between devices  29.3 us (31%)
  waiting for transfers between devices  28.4 us (30%)
  local copies, waits for them, and re-layouts  5.62 us (6%)
    ppermute x14, starting transfers between devices, permute(): return lax.ppermute(block, AXES, pairs) if pairs else jnp.zeros_like(block)  29.3 us
    ppermute x14, waiting for transfers between devices, permute(): return lax.ppermute(block, AXES, pairs) if pairs else jnp.zeros_like(block)  28.4 us
    pallas_call x2, Pallas kernels, product(): pl.pallas_call(kernel, grid=(height // tile,), in_specs=in_specs, out_spe...  21.4 us
    unnamed x28, local copies, waits for them, and re-layouts  4.63 us
    pallas_call x3, Pallas kernels, assemble(): pl.pallas_call(kernel, in_specs=[SMEM] + [VMEM] * len(parts) + [ANY] * le...  3.53 us
    pallas_call x1, Pallas kernels, weigh(): pl.pallas_call(kernel, in_specs=[SMEM] + [VMEM] * (3 + count), out_specs=...  3.14 us
  transfers between devices with their start and end apart: 14, of which 8 were waited for; matrix products, arithmetic and copies ran while one was open for 1% of the time, Pallas kernels for 23%

profile of v3, /device:TPU:11, one launch (start us, length us, event | category | flops | bytes accessed | tf_op | source)
XLA Modules:
  0.0 93.6 jit_solution(2505689225435273833)
XLA Ops:
  0.0 0.1 stack.34.starts
  0.1 0.0 copy-start
  0.1 1.9 %copy-done = bf16[384,4096]{1,0:T(8,128)(2,1)S(1)} copy-done((bf16[384,4096]{1,0:T(8,128)(2,1)S(1)}, bf16[384,4096]{1,0:T(8,128)(2,1)}, u32[]{:S(2)}) %copy-start) | copy-done | bytes 3145752
  2.0 0.9 shard_map.28
  2.9 0.0 copy-start.9
  2.9 0.0 copy-start.6
  2.9 0.0 copy-start.1
  3.0 1.6 %collective-permute-start.9 = (bf16[384,768]{1,0:T(8,128)(2,1)S(1)}, bf16[384,768]{1,0:T(8,128)(2,1)S(1)}, u32[]{:S(2)}, u32[]{:S(2)}) collective-permute-start(bf16[384,768]{1,0:T(8,128)(2,1)S(1)} %get-tuple-element.16.refs_0_), channel_id=1, source_target_pairs={{4,8},{5,9},{6,16},{7,17},{12,2},{13,3},{8,18},{9,19},{20,12},{21,... | collective-permute-start | bytes 1769480 | tf_op jit(solution)/shard_map/ppermute | solution.py:233
  4.5 5.9 %collective-permute-start.5 = (bf16[384,1280]{1,0:T(8,128)(2,1)S(1)}, bf16[384,1280]{1,0:T(8,128)(2,1)S(1)}, u32[]{:S(2)}, u32[]{:S(2)}) collective-permute-start(bf16[384,1280]{1,0:T(8,128)(2,1)S(1)} %get-tuple-element.13.refs_0_), channel_id=1, source_target_pairs={{0,8},{1,9},{2,16},{3,17},{4,24},{5,25},{12,2},{13,3},{8,18},{9,19... | collective-permute-start | bytes 2949128 | tf_op jit(solution)/shard_map/ppermute | solution.py:233
  10.5 1.3 %collective-permute-start.6 = (bf16[192,768]{1,0:T(8,128)(2,1)S(1)}, bf16[192,768]{1,0:T(8,128)(2,1)S(1)}, u32[]{:S(2)}, u32[]{:S(2)}) collective-permute-start(bf16[192,768]{1,0:T(8,128)(2,1)S(1)} %get-tuple-element.14), channel_id=1, source_target_pairs={{0,1},{1,0},{2,3},{3,2},{4,5},{5,4},{6,7},{7,6},{8,9},{9,8},{10,11... | collective-permute-start | bytes 884744 | tf_op jit(solution)/shard_map/ppermute | solution.py:233
  11.8 0.2 collective-permute-start.1
  12.0 1.2 %collective-permute-start.3 = (bf16[192,640]{1,0:T(8,128)(2,1)S(1)}, bf16[192,640]{1,0:T(8,128)(2,1)S(1)}, u32[]{:S(2)}, u32[]{:S(2)}) collective-permute-start(bf16[192,640]{1,0:T(8,128)(2,1)S(1)} %get-tuple-element.12), channel_id=1, source_target_pairs={{0,1},{1,0},{2,3},{3,2},{4,5},{5,4},{6,7},{7,6},{8,9},{9,8},{10,11... | collective-permute-start | bytes 737288 | tf_op jit(solution)/shard_map/ppermute | solution.py:233
  13.2 11.7 %collective-permute-done.1.refs_0_.refs_1_ = bf16[192,640]{1,0:T(8,128)(2,1)S(1)} collective-permute-done((bf16[192,640]{1,0:T(8,128)(2,1)S(1)}, bf16[192,640]{1,0:T(8,128)(2,1)S(1)}, u32[]{:S(2)}, u32[]{:S(2)}) %collective-permute-start.1) | collective-permute-done | bytes 245792 | tf_op jit(solution)/shard_map/ppermute | solution.py:233
  24.9 3.0 %collective-permute-done.3.refs_2_ = bf16[192,640]{1,0:T(8,128)(2,1)S(1)} collective-permute-done((bf16[192,640]{1,0:T(8,128)(2,1)S(1)}, bf16[192,640]{1,0:T(8,128)(2,1)S(1)}, u32[]{:S(2)}, u32[]{:S(2)}) %collective-permute-start.3) | collective-permute-done | bytes 245792 | tf_op jit(solution)/shard_map/ppermute | solution.py:233
  27.8 0.0 collective-permute-done.6.refs_0_.refs_3_
  27.8 0.1 shard_map.31
  27.9 1.3 %collective-permute-start.8 = (bf16[192,2048]{1,0:T(8,128)(2,1)S(1)}, bf16[192,2048]{1,0:T(8,128)(2,1)S(1)}, u32[]{:S(2)}, u32[]{:S(2)}) collective-permute-start(bf16[192,2048]{1,0:T(8,128)(2,1)S(1)} %shard_map.31), channel_id=1, source_target_pairs={{0,1},{1,0},{2,3},{3,2},{4,5},{5,4},{6,7},{7,6},{8,9},{9,8},{10,11... | collective-permute-start | bytes 2359304 | tf_op jit(solution)/shard_map/ppermute | solution.py:233
  29.2 0.0 copy-done.9
  29.2 0.0 collective-permute-done.9.refs_1_
  29.2 1.3 %collective-permute-start.10 = (bf16[384,768]{1,0:T(8,128)(2,1)S(1)}, bf16[384,768]{1,0:T(8,128)(2,1)S(1)}, u32[]{:S(2)}, u32[]{:S(2)}) collective-permute-start(bf16[384,768]{1,0:T(8,128)(2,1)S(1)} %collective-permute-done.9.refs_1_), channel_id=1, source_target_pairs={{12,4},{13,5},{14,6},{15,7},{16,24},{17,25},{18,26},{19,27}} | collective-permute-start | bytes 1769480 | tf_op jit(solution)/shard_map/ppermute | solution.py:233
  30.5 3.3 %collective-permute-start.2 = (bf16[192,640]{1,0:T(8,128)(2,1)S(1)}, bf16[192,640]{1,0:T(8,128)(2,1)S(1)}, u32[]{:S(2)}, u32[]{:S(2)}) collective-permute-start(bf16[192,640]{1,0:T(8,128)(2,1)S(1)} %collective-permute-done.1.refs_0_.refs_1_), channel_id=1, source_target_pairs={{0,2},{1,3},{2,0},{3,1},{4,6},{5,7},{6,4},{7,5},{8,10},{9,11},{10,... | collective-permute-start | bytes 737288 | tf_op jit(solution)/shard_map/ppermute | solution.py:233
  33.8 0.1 collective-permute-start.4
  33.9 1.1 %collective-permute-done.2.refs_1_ = bf16[192,640]{1,0:T(8,128)(2,1)S(1)} collective-permute-done((bf16[192,640]{1,0:T(8,128)(2,1)S(1)}, bf16[192,640]{1,0:T(8,128)(2,1)S(1)}, u32[]{:S(2)}, u32[]{:S(2)}) %collective-permute-start.2) | collective-permute-done | bytes 245792 | tf_op jit(solution)/shard_map/ppermute | solution.py:233
  34.9 0.4 collective-permute-done.4.refs_3_
  35.3 1.7 %collective-permute-done.5.refs_4_.refs_1_ = bf16[384,1280]{1,0:T(8,128)(2,1)S(1)} collective-permute-done((bf16[384,1280]{1,0:T(8,128)(2,1)S(1)}, bf16[384,1280]{1,0:T(8,128)(2,1)S(1)}, u32[]{:S(2)}, u32[]{:S(2)}) %collective-permute-start.5) | collective-permute-done | bytes 983072 | tf_op jit(solution)/shard_map/ppermute | solution.py:233
  37.0 1.1 %shard_map.29.refs_0_.refs_2_ = bf16[384,1280]{1,0:T(8,128)(2,1)} custom-call(s32[1]{0:T(128)} %bitcast.2.core, bf16[192,640]{1,0:T(8,128)(2,1)S(1)} %collective-permute-done.1.refs_0_.refs_1_, bf16[192,640]{1,0:T(8,128)(2,1)S(1)} %collective-permute-done.2.refs_1_, bf16[192,640]{1,0:T(8,128)(2,1)S(1)} %collective-permute-done.3.refs_2_, ...), custom_call_target="tpu_custom_call" | custom-call | tf_op jit(solution)/shard_map/pallas_call | solution.py:145
  38.1 0.9 %copy-done.2 = bf16[384,1280]{1,0:T(8,128)(2,1)} copy-done((bf16[384,1280]{1,0:T(8,128)(2,1)}, bf16[384,1280]{1,0:T(8,128)(2,1)S(1)}, u32[]{:S(2)}) %copy-start.2) | copy-done | bytes 983064
  39.0 5.6 %collective-permute-start.12 = (bf16[384,1280]{1,0:T(8,128)(2,1)}, bf16[384,1280]{1,0:T(8,128)(2,1)}, u32[]{:S(2)}, u32[]{:S(2)}) collective-permute-start(bf16[384,1280]{1,0:T(8,128)(2,1)} %shard_map.29.refs_0_.refs_2_), channel_id=1, source_target_pairs={{0,8},{1,9},{4,16},{5,17},{2,24},{3,25},{12,2},{13,3},{8,18},{9,19... | collective-permute-start | bytes 2949128 | tf_op jit(solution)/shard_map/ppermute | solution.py:233
  44.6 1.6 %collective-permute-done.8.refs_0_ = bf16[192,2048]{1,0:T(8,128)(2,1)S(1)} collective-permute-done((bf16[192,2048]{1,0:T(8,128)(2,1)S(1)}, bf16[192,2048]{1,0:T(8,128)(2,1)S(1)}, u32[]{:S(2)}, u32[]{:S(2)}) %collective-permute-start.8) | collective-permute-done | bytes 786464 | tf_op jit(solution)/shard_map/ppermute | solution.py:233
  46.2 0.0 collective-permute-done.10.refs_1_.refs_2_
  46.2 1.0 %shard_map.32.refs_0_ = bf16[192,2048]{1,0:T(8,128)(2,1)} custom-call(bf16[192,2048]{1,0:T(8,128)(2,1)S(1)} %collective-permute-done.8.refs_0_, bf16[384,768]{1,0:T(8,128)(2,1)S(1)} %collective-permute-done.10.refs_1_.refs_2_), custom_call_target="tpu_custom_call" | custom-call | tf_op jit(solution)/shard_map/pallas_call | solution.py:161
  47.1 0.0 copy-done.6
  47.1 0.8 copy-done.4
  48.0 0.0 collective-permute-start.11
  48.0 0.0 copy-done.11
  48.0 0.5 collective-permute-start.7
  48.5 0.0 copy-done.13
  48.5 1.2 %collective-permute-start = (f32[384]{0:T(512)S(1)}, f32[384]{0:T(512)S(1)}, u32[]{:S(2)}, u32[]{:S(2)}) collective-permute-start(f32[384]{0:T(512)S(1)} %copy-done.13), channel_id=1, source_target_pairs={{0,1},{1,0},{2,3},{3,2},{4,5},{5,4},{6,7},{7,6},{8,9},{9,8},{10,11... | collective-permute-start | bytes 4616 | tf_op jit(solution)/shard_map/ppermute | solution.py:233
  49.7 0.8 broadcast_in_dim.8.weights
  50.5 0.8 collective-permute-done
  51.3 0.1 broadcast_in_dim.9.other_weights
  51.4 0.0 collective-permute-done.7.refs_1_
  51.4 1.0 %shard_map.30.refs_1_.refs_0_.refs_3_ = bf16[384,768]{1,0:T(8,128)(2,1)S(1)} custom-call(s32[1]{0:T(128)} %bitcast.2.core, bf16[192,768]{1,0:T(8,128)(2,1)S(1)} %collective-permute-done.6.refs_0_.refs_3_, bf16[192,768]{1,0:T(8,128)(2,1)} %collective-permute-done.7.refs_1_), custom_call_target="tpu_custom_call" | custom-call | tf_op jit(solution)/shard_map/pallas_call | solution.py:145
  52.4 0.0 collective-permute-done.11.refs_1_
  52.5 1.5 %shard_map.33.refs_2_ = bf16[384,2048]{1,0:T(8,128)(2,1)S(1)} custom-call(s32[1]{0:T(128)} %bitcast.2.core, bf16[192,2048]{1,0:T(8,128)(2,1)} %shard_map.32.refs_0_, bf16[192,2048]{1,0:T(8,128)(2,1)} %collective-permute-done.11.refs_1_), custom_call_target="tpu_custom_call" | custom-call | tf_op jit(solution)/shard_map/pallas_call | solution.py:145
  53.9 0.0 copy-done.1
  53.9 0.0 copy-start.8
  54.0 0.9 copy-done.8
  54.9 3.1 %shard_map.34.refs_1_.rows = bf16[768,4096]{1,0:T(8,128)(2,1)S(1)} custom-call(s32[1]{0:T(128)} %bitcast.1.index, bf16[384,4096]{1,0:T(8,128)(2,1)S(1)} %copy-done.1, f32[384,1]{1,0:T(8,128)S(1)} %copy-done.8, f32[384,1]{1,0:T(8,128)S(1)} %broadcast_in_dim.9.other_weights, bf16[384,1280]{1,0:T(8,128)(2,1)} %shard_map.29.refs_0_.refs_2_, ...), custom_call_target="tpu_custom_call" | custom-call | tf_op jit(solution)/shard_map/pallas_call | solution.py:94
  58.0 0.0 copy-start.3
  58.0 0.0 copy-start.7
  58.0 8.3 %collective-permute-done.12.refs_2_.refs_3_ = bf16[384,1280]{1,0:T(8,128)(2,1)} collective-permute-done((bf16[384,1280]{1,0:T(8,128)(2,1)}, bf16[384,1280]{1,0:T(8,128)(2,1)}, u32[]{:S(2)}, u32[]{:S(2)}) %collective-permute-start.12) | collective-permute-done | bytes 983072 | tf_op jit(solution)/shard_map/ppermute | solution.py:233
  66.4 5.7 %collective-permute-start.13 = (bf16[384,768]{1,0:T(8,128)(2,1)S(1)}, bf16[384,768]{1,0:T(8,128)(2,1)S(1)}, u32[]{:S(2)}, u32[]{:S(2)}) collective-permute-start(bf16[384,768]{1,0:T(8,128)(2,1)S(1)} %shard_map.35), channel_id=1, source_target_pairs={{0,8},{1,9},{4,16},{5,17},{2,24},{3,25},{12,2},{13,3},{8,18},{9,19... | collective-permute-start | bytes 1769480 | tf_op jit(solution)/shard_map/ppermute | solution.py:233
  72.1 0.0 copy-done.3
  72.1 0.0 copy-done.7
  72.1 0.0 copy-start.5
  72.1 0.0 copy-start.10
  72.1 0.0 copy-start.12
  72.1 13.4 %shard_map.36.refs_5_ = f32[4096,2048]{1,0:T(8,128)} custom-call(s32[1]{0:T(128)} %bitcast.source, bf16[768,4096]{1,0:T(8,128)(2,1)S(1)} %shard_map.34.refs_1_.rows, bf16[384,1280]{1,0:T(8,128)(2,1)S(1)} %copy-done.7, bf16[384,1280]{1,0:T(8,128)(2,1)S(1)} %copy-done.3, bf16[384,1280]{1,0:T(8,128)(2,1)} %shard_map.29.refs_0_.refs_2_, ...), custom_call_target="tpu_custom_call" | custom-call | flops 8053063680 | bytes 20971520 | tf_op jit(solution)/shard_map/pallas_call | solution.py:50
  85.6 0.0 collective-permute-done.13.refs_4_
  85.6 0.0 copy-done.5
  85.6 0.0 copy-done.10
  85.6 0.0 copy-done.12
  85.6 8.0 %shard_map.37 = f32[4096,2048]{1,0:T(8,128)} custom-call(s32[1]{0:T(128)} %bitcast.source, bf16[768,4096]{1,0:T(8,128)(2,1)S(1)} %shard_map.34.refs_1_.rows, bf16[384,768]{1,0:T(8,128)(2,1)S(1)} %copy-done.10, bf16[384,768]{1,0:T(8,128)(2,1)S(1)} %copy-done.12, bf16[384,768]{1,0:T(8,128)(2,1)S(1)} %copy-done.5, ...), custom_call_target="tpu_custom_call", output_to_operand_aliasing={{}: (7, {})} | custom-call | flops 4831838208 | bytes 12582912 | tf_op jit(solution)/shard_map/pallas_call | solution.py:50
  (5 shorter events, 0.0 us)
Async XLA Ops:
  0.0 48.5 %copy-start.13 = (f32[384]{0:T(512)S(1)}, f32[384]{0:T(512)}, u32[]{:S(2)}) copy-start(f32[384]{0:T(512)} %param.3) | copy-start | bytes 4612
  0.1 1.9 %copy-start = (bf16[384,4096]{1,0:T(8,128)(2,1)S(1)}, bf16[384,4096]{1,0:T(8,128)(2,1)}, u32[]{:S(2)}) copy-start(bf16[384,4096]{1,0:T(8,128)(2,1)} %slab.3) | copy-start | bytes 9437188
  2.9 26.3 %copy-start.9 = (bf16[384,768]{1,0:T(8,128)(2,1)}, bf16[384,768]{1,0:T(8,128)(2,1)S(1)}, u32[]{:S(2)}) copy-start(bf16[384,768]{1,0:T(8,128)(2,1)S(1)} %get-tuple-element.16.refs_0_) | copy-start | bytes 1769476
  2.9 44.2 %copy-start.6 = (bf16[384,1280]{1,0:T(8,128)(2,1)}, bf16[384,1280]{1,0:T(8,128)(2,1)S(1)}, u32[]{:S(2)}) copy-start(bf16[384,1280]{1,0:T(8,128)(2,1)S(1)} %get-tuple-element.13.refs_0_) | copy-start | bytes 2949124
  2.9 51.0 %copy-start.1 = (bf16[384,4096]{1,0:T(8,128)(2,1)S(1)}, bf16[384,4096]{1,0:T(8,128)(2,1)}, u32[]{:S(2)}) copy-start(bf16[384,4096]{1,0:T(8,128)(2,1)} %slab.3) | copy-start | bytes 9437188
  3.0 26.3 %collective-permute-start.9 = (bf16[384,768]{1,0:T(8,128)(2,1)S(1)}, bf16[384,768]{1,0:T(8,128)(2,1)S(1)}, u32[]{:S(2)}, u32[]{:S(2)}) collective-permute-start(bf16[384,768]{1,0:T(8,128)(2,1)S(1)} %get-tuple-element.16.refs_0_), channel_id=1, source_target_pairs={{4,8},{5,9},{6,16},{7,17},{12,2},{13,3},{8,18},{9,19},{20,12},{21,... | collective-permute-start | bytes 1769480 | tf_op jit(solution)/shard_map/ppermute | solution.py:233
  4.5 32.5 %collective-permute-start.5 = (bf16[384,1280]{1,0:T(8,128)(2,1)S(1)}, bf16[384,1280]{1,0:T(8,128)(2,1)S(1)}, u32[]{:S(2)}, u32[]{:S(2)}) collective-permute-start(bf16[384,1280]{1,0:T(8,128)(2,1)S(1)} %get-tuple-element.13.refs_0_), channel_id=1, source_target_pairs={{0,8},{1,9},{2,16},{3,17},{4,24},{5,25},{12,2},{13,3},{8,18},{9,19... | collective-permute-start | bytes 2949128 | tf_op jit(solution)/shard_map/ppermute | solution.py:233
  10.5 17.4 %collective-permute-start.6 = (bf16[192,768]{1,0:T(8,128)(2,1)S(1)}, bf16[192,768]{1,0:T(8,128)(2,1)S(1)}, u32[]{:S(2)}, u32[]{:S(2)}) collective-permute-start(bf16[192,768]{1,0:T(8,128)(2,1)S(1)} %get-tuple-element.14), channel_id=1, source_target_pairs={{0,1},{1,0},{2,3},{3,2},{4,5},{5,4},{6,7},{7,6},{8,9},{9,8},{10,11... | collective-permute-start | bytes 884744 | tf_op jit(solution)/shard_map/ppermute | solution.py:233
  11.8 13.1 %collective-permute-start.1 = (bf16[192,640]{1,0:T(8,128)(2,1)S(1)}, bf16[192,640]{1,0:T(8,128)(2,1)S(1)}, u32[]{:S(2)}, u32[]{:S(2)}) collective-permute-start(bf16[192,640]{1,0:T(8,128)(2,1)S(1)} %get-tuple-element.11), channel_id=1, source_target_pairs={{0,1},{1,0},{2,3},{3,2},{4,5},{5,4},{6,7},{7,6},{8,9},{9,8},{10,11... | collective-permute-start | bytes 737288 | tf_op jit(solution)/shard_map/ppermute | solution.py:233
  12.0 15.8 %collective-permute-start.3 = (bf16[192,640]{1,0:T(8,128)(2,1)S(1)}, bf16[192,640]{1,0:T(8,128)(2,1)S(1)}, u32[]{:S(2)}, u32[]{:S(2)}) collective-permute-start(bf16[192,640]{1,0:T(8,128)(2,1)S(1)} %get-tuple-element.12), channel_id=1, source_target_pairs={{0,1},{1,0},{2,3},{3,2},{4,5},{5,4},{6,7},{7,6},{8,9},{9,8},{10,11... | collective-permute-start | bytes 737288 | tf_op jit(solution)/shard_map/ppermute | solution.py:233
  27.9 18.3 %collective-permute-start.8 = (bf16[192,2048]{1,0:T(8,128)(2,1)S(1)}, bf16[192,2048]{1,0:T(8,128)(2,1)S(1)}, u32[]{:S(2)}, u32[]{:S(2)}) collective-permute-start(bf16[192,2048]{1,0:T(8,128)(2,1)S(1)} %shard_map.31), channel_id=1, source_target_pairs={{0,1},{1,0},{2,3},{3,2},{4,5},{5,4},{6,7},{7,6},{8,9},{9,8},{10,11... | collective-permute-start | bytes 2359304 | tf_op jit(solution)/shard_map/ppermute | solution.py:233
  29.2 18.8 %copy-start.11 = (bf16[384,768]{1,0:T(8,128)(2,1)}, bf16[384,768]{1,0:T(8,128)(2,1)S(1)}, u32[]{:S(2)}) copy-start(bf16[384,768]{1,0:T(8,128)(2,1)S(1)} %collective-permute-done.9.refs_1_) | copy-start | bytes 1769476
  29.2 17.0 %collective-permute-start.10 = (bf16[384,768]{1,0:T(8,128)(2,1)S(1)}, bf16[384,768]{1,0:T(8,128)(2,1)S(1)}, u32[]{:S(2)}, u32[]{:S(2)}) collective-permute-start(bf16[384,768]{1,0:T(8,128)(2,1)S(1)} %collective-permute-done.9.refs_1_), channel_id=1, source_target_pairs={{12,4},{13,5},{14,6},{15,7},{16,24},{17,25},{18,26},{19,27}} | collective-permute-start | bytes 1769480 | tf_op jit(solution)/shard_map/ppermute | solution.py:233
  30.5 4.4 %collective-permute-start.2 = (bf16[192,640]{1,0:T(8,128)(2,1)S(1)}, bf16[192,640]{1,0:T(8,128)(2,1)S(1)}, u32[]{:S(2)}, u32[]{:S(2)}) collective-permute-start(bf16[192,640]{1,0:T(8,128)(2,1)S(1)} %collective-permute-done.1.refs_0_.refs_1_), channel_id=1, source_target_pairs={{0,2},{1,3},{2,0},{3,1},{4,6},{5,7},{6,4},{7,5},{8,10},{9,11},{10,... | collective-permute-start | bytes 737288 | tf_op jit(solution)/shard_map/ppermute | solution.py:233
  33.8 1.5 %collective-permute-start.4 = (bf16[192,640]{1,0:T(8,128)(2,1)S(1)}, bf16[192,640]{1,0:T(8,128)(2,1)S(1)}, u32[]{:S(2)}, u32[]{:S(2)}) collective-permute-start(bf16[192,640]{1,0:T(8,128)(2,1)S(1)} %collective-permute-done.3.refs_2_), channel_id=1, source_target_pairs={{0,2},{1,3},{2,0},{3,1},{4,6},{5,7},{6,4},{7,5},{8,10},{9,11},{10,... | collective-permute-start | bytes 737288 | tf_op jit(solution)/shard_map/ppermute | solution.py:233
  38.1 0.9 %copy-start.2 = (bf16[384,1280]{1,0:T(8,128)(2,1)}, bf16[384,1280]{1,0:T(8,128)(2,1)S(1)}, u32[]{:S(2)}) copy-start(bf16[384,1280]{1,0:T(8,128)(2,1)S(1)} %collective-permute-done.5.refs_4_.refs_1_) | copy-start | bytes 2949124
  39.0 27.4 %collective-permute-start.12 = (bf16[384,1280]{1,0:T(8,128)(2,1)}, bf16[384,1280]{1,0:T(8,128)(2,1)}, u32[]{:S(2)}, u32[]{:S(2)}) collective-permute-start(bf16[384,1280]{1,0:T(8,128)(2,1)} %shard_map.29.refs_0_.refs_2_), channel_id=1, source_target_pairs={{0,8},{1,9},{4,16},{5,17},{2,24},{3,25},{12,2},{13,3},{8,18},{9,19... | collective-permute-start | bytes 2949128 | tf_op jit(solution)/shard_map/ppermute | solution.py:233
  47.1 0.8 copy-start.4
  48.0 4.5 %collective-permute-start.11 = (bf16[192,2048]{1,0:T(8,128)(2,1)}, bf16[192,2048]{1,0:T(8,128)(2,1)}, u32[]{:S(2)}, u32[]{:S(2)}) collective-permute-start(bf16[192,2048]{1,0:T(8,128)(2,1)} %shard_map.32.refs_0_), channel_id=1, source_target_pairs={{0,2},{1,3},{2,0},{3,1},{4,6},{5,7},{6,4},{7,5},{8,10},{9,11},{10,... | collective-permute-start | bytes 2359304 | tf_op jit(solution)/shard_map/ppermute | solution.py:233
  48.0 3.5 %collective-permute-start.7 = (bf16[192,768]{1,0:T(8,128)(2,1)S(1)}, bf16[192,768]{1,0:T(8,128)(2,1)}, u32[]{:S(2)}, u32[]{:S(2)}) collective-permute-start(bf16[192,768]{1,0:T(8,128)(2,1)S(1)} %collective-permute-done.6.refs_0_.refs_3_), channel_id=1, source_target_pairs={{0,2},{1,3},{2,0},{3,1},{4,6},{5,7},{6,4},{7,5},{8,10},{9,11},{10,... | collective-permute-start | bytes 884744 | tf_op jit(solution)/shard_map/ppermute | solution.py:233
  48.5 2.8 %collective-permute-start = (f32[384]{0:T(512)S(1)}, f32[384]{0:T(512)S(1)}, u32[]{:S(2)}, u32[]{:S(2)}) collective-permute-start(f32[384]{0:T(512)S(1)} %copy-done.13), channel_id=1, source_target_pairs={{0,1},{1,0},{2,3},{3,2},{4,5},{5,4},{6,7},{7,6},{8,9},{9,8},{10,11... | collective-permute-start | bytes 4616 | tf_op jit(solution)/shard_map/ppermute | solution.py:233
  53.9 0.9 copy-start.8
  58.0 14.1 %copy-start.3 = (bf16[384,1280]{1,0:T(8,128)(2,1)S(1)}, bf16[384,1280]{1,0:T(8,128)(2,1)}, u32[]{:S(2)}) copy-start(bf16[384,1280]{1,0:T(8,128)(2,1)} %copy-done.2) | copy-start | bytes 2949124
  58.0 14.1 %copy-start.7 = (bf16[384,1280]{1,0:T(8,128)(2,1)S(1)}, bf16[384,1280]{1,0:T(8,128)(2,1)}, u32[]{:S(2)}) copy-start(bf16[384,1280]{1,0:T(8,128)(2,1)} %copy-done.6) | copy-start | bytes 2949124
  66.4 19.2 %collective-permute-start.13 = (bf16[384,768]{1,0:T(8,128)(2,1)S(1)}, bf16[384,768]{1,0:T(8,128)(2,1)S(1)}, u32[]{:S(2)}, u32[]{:S(2)}) collective-permute-start(bf16[384,768]{1,0:T(8,128)(2,1)S(1)} %shard_map.35), channel_id=1, source_target_pairs={{0,8},{1,9},{4,16},{5,17},{2,24},{3,25},{12,2},{13,3},{8,18},{9,19... | collective-permute-start | bytes 1769480 | tf_op jit(solution)/shard_map/ppermute | solution.py:233
  72.1 13.5 %copy-start.5 = (bf16[384,768]{1,0:T(8,128)(2,1)S(1)}, bf16[384,768]{1,0:T(8,128)(2,1)}, u32[]{:S(2)}) copy-start(bf16[384,768]{1,0:T(8,128)(2,1)} %copy-done.4) | copy-start | bytes 1769476
  72.1 13.5 %copy-start.10 = (bf16[384,768]{1,0:T(8,128)(2,1)S(1)}, bf16[384,768]{1,0:T(8,128)(2,1)}, u32[]{:S(2)}) copy-start(bf16[384,768]{1,0:T(8,128)(2,1)} %copy-done.9) | copy-start | bytes 1769476
  72.1 13.5 %copy-start.12 = (bf16[384,768]{1,0:T(8,128)(2,1)S(1)}, bf16[384,768]{1,0:T(8,128)(2,1)}, u32[]{:S(2)}) copy-start(bf16[384,768]{1,0:T(8,128)(2,1)} %copy-done.11) | copy-start | bytes 1769476

commit v4 on v2

v4 whole, which is shorter than its diff:
```python
import jax
import jax.numpy as jnp
from jax import lax
from jax.experimental import pallas as pl
from jax.experimental.pallas import tpu as pltpu
from jax.sharding import PartitionSpec as P

AXES = ("row", "col", "pair")
LANES = 128
VMEM = pl.BlockSpec(memory_space=pltpu.VMEM)
SMEM = pl.BlockSpec(memory_space=pltpu.SMEM)
ANY = pl.BlockSpec(memory_space=pl.ANY)


def params(mib):
    return pltpu.CompilerParams(vmem_limit_bytes=mib * 2**20)


def product(source, rows, own, other, result, first, columns):
    depth, height = rows.shape
    pairs, width = own[0].shape[0], other[0].shape[1]
    tile = 1024 if height % 1024 == 0 else height
    args = [source, rows, *own, *other]
    in_specs = [SMEM] + [VMEM] * (len(args) - 1)
    aliases = {}
    if result is not None:
        aliases = {len(args): 0}
        in_specs.append(ANY)
        args.append(result)

    def kernel(source, rows, *refs):
        out, held = refs[-2:]

        @pl.when(pl.program_id(0) == 0)
        def _():
            for part, choices in ((pl.ds(0, pairs), own), (pl.ds(pairs, depth - pairs), other)):
                skip = 0 if choices is own else len(own)
                for i in range(len(choices)):
                    start = first if choices is own else 0

                    @pl.when(source[0] == i)
                    def _(part=part, i=skip + i, start=start):
                        held[part, :] = refs[i][:, start : start + width]

        at = pl.ds(pl.multiple_of(pl.program_id(0) * tile, tile), tile)
        out[...] = lax.dot_general(
            rows[:, at], held[...], (((0,), (0,)), ((), ())), preferred_element_type=jnp.float32
        )

    return pl.pallas_call(
        kernel,
        grid=(height // tile,),
        in_specs=in_specs,
        out_specs=pl.BlockSpec((pl.Element(tile), pl.Element(width)), lambda i: (i * tile, first)),
        out_shape=jax.ShapeDtypeStruct((height, columns), jnp.float32),
        scratch_shapes=[pltpu.VMEM((depth, width), jnp.bfloat16)],
        input_output_aliases=aliases,
        compiler_params=params(24),
        cost_estimate=pl.CostEstimate(
            flops=2 * height * width * depth, bytes_accessed=4 * height * width, transcendentals=0
        ),
    )(*args)


def weigh(index, slab, weights, other_parts, other_weights, width):
    pairs, height = slab.shape
    others = other_weights.shape[0]
    count = len(other_parts)
    step = 64 if pairs % 64 == 0 else pairs

    def kernel(index, slab, weights, other_weights, *refs):
        parts, out = refs[:count], refs[-1]

        def scaled(by, rows):
            return (by * rows.astype(jnp.float32)).astype(out.dtype)

        @pl.loop(0, pairs // step)
        def _(i):
            at = pl.ds(pl.multiple_of(i * step, step), step)
            out[at, :] = scaled(weights[at, :], slab[at, :])

        @pl.loop(0, others // step)
        def _(i):
            at = pl.ds(pl.multiple_of(i * step, step), step)
            to = pl.ds(pl.multiple_of(pairs + i * step, step), step)
            by = other_weights[at, :]
            offset = 0
            for part in parts:
                size = part.shape[1]
                start = lax.rem(index[0] * width + offset, height)
                out[to, pl.ds(pl.multiple_of(start, LANES), size)] = scaled(by, part[at, :])
                offset += size

    return pl.pallas_call(
        kernel,
        in_specs=[SMEM] + [VMEM] * (3 + count),
        out_specs=VMEM,
        out_shape=jax.ShapeDtypeStruct((pairs + others, height), slab.dtype),
        compiler_params=params(16),
    )(index, slab, weights[:, None], other_weights[:, None], *other_parts)


def cut_out(starts, slab, shapes):
    count = len(shapes)

    def kernel(starts, slab, *refs):
        outs, done = refs[:count], refs[-1]
        copies = []
        for i, (rows, size) in enumerate(shapes):
            at = pl.ds(pl.multiple_of(starts[2 * i], 16), rows)
            across = pl.ds(pl.multiple_of(starts[2 * i + 1], LANES), size)
            copies.append(pltpu.make_async_copy(slab.at[at, across], outs[i], done.at[i]))
        for copy in copies:
            copy.start()
        for copy in copies:
            copy.wait()

    return pl.pallas_call(
        kernel,
        in_specs=[SMEM, ANY],
        out_specs=[VMEM] * count,
        out_shape=[jax.ShapeDtypeStruct(shape, slab.dtype) for shape in shapes],
        scratch_shapes=[pltpu.SemaphoreType.DMA((count,))],
        compiler_params=params(16),
    )(starts, slab)


def assemble(core, mine, theirs, start, size):
    count = len(mine)
    half = mine[0].shape[0]

    def kernel(core, *refs):
        out = refs[-1]
        for i in range(count):
            for rows, ref in ((core[0], refs[i]), (1 - core[0], refs[count + i])):
                at = pl.multiple_of((2 * i + rows) * half, half)
                out[pl.ds(at, half), :] = ref[:, start : start + size]

    return pl.pallas_call(
        kernel,
        in_specs=[SMEM] + [VMEM] * (2 * count),
        out_specs=VMEM,
        out_shape=jax.ShapeDtypeStruct((2 * count * half, size), mine[0].dtype),
        compiler_params=params(16),
    )(core, *mine, *theirs)


def hold(values, *earlier):
    count = len(values)

    def kernel(*refs):
        for value, out in zip(refs[:count], refs[-count:]):
            out[...] = value[...]

    return pl.pallas_call(
        kernel,
        in_specs=[VMEM] * count + [ANY] * len(earlier),
        out_specs=[VMEM] * count,
        out_shape=[jax.ShapeDtypeStruct(v.shape, v.dtype) for v in values],
        compiler_params=params(16),
    )(*values, *earlier)


def pick_senders(planes, columns):
    per_side = columns // 2
    sends = [(b, t) for b in range(planes) for t in range(planes) if b != t]

    def cost(chosen):
        load, sources = {}, {}
        for (b, t), side in zip(sends, chosen):
            way = 1 if t > b else -1
            links = [(side, z, way) for z in range(b, t, way)]
            if side != b // per_side:
                links.append((t, side, "across"))
            for link in links:
                load[link] = load.get(link, 0) + 1
                sources.setdefault(link, set()).add(b)
        return sum(value**6 * (4 + len(sources[link])) for link, value in load.items())

    def full(chosen, i):
        return sum(s[0] == sends[i][0] and c == chosen[i] for s, c in zip(sends, chosen)) > per_side

    def settle(chosen):
        for i in sorted(range(len(sends)), key=lambda i: -abs(sends[i][0] - sends[i][1])):
            if full(chosen, i):
                chosen[i] = 1 - chosen[i]
        every = range(len(sends))
        best, better = cost(chosen), True
        while better:
            better = False
            for flips in [[i] for i in every] + [[i, j] for i in every for j in range(i)]:
                trial = list(chosen)
                for j in flips:
                    trial[j] = 1 - trial[j]
                if not any(full(trial, j) for j in flips) and cost(trial) < best:
                    chosen, best, better = trial, cost(trial), True
        return best, chosen

    def native(b, t):
        return b // per_side

    def apart(b, t):
        inward = t < b if b >= planes // 2 else t > b
        return 1 - native(b, t) if inward and (b not in (0, planes - 1) or abs(b - t) == 1) else native(b, t)

    starts = [[rule(*send) for send in sends] for rule in (native, apart)]
    _, chosen = min((settle(start) for start in starts), key=lambda result: result[0])
    result = {}
    for (b, t), side in zip(sends, chosen):
        used = [c for (x, _), c in result.items() if x == b]
        result[b, t] = [c for c in range(side * per_side, (side + 1) * per_side) if c not in used][0]
    return result


def solution(mesh):
    R, C, Q = (mesh.shape[axis] for axis in AXES)
    senders = pick_senders(R, C)

    def number(r, c, p):
        return (r * C + c) * Q + p

    def permute(block, moves):
        pairs = [(number(*source), number(*target)) for source, target in moves]
        return lax.ppermute(block, AXES, pairs) if pairs else jnp.zeros_like(block)

    def permute_all(block, route):
        every = [(r, c, p) for r in range(R) for c in range(C) for p in range(Q)]
        return permute(block, [(device, route(*device)) for device in every])

    def send(block):
        return permute(
            block, [((b, c, p), (t, b, p)) for (b, t), c in senders.items() for p in range(Q)]
        )

    def on_device(slab, weights):
        pairs, block = slab.shape
        width = block // Q
        wide = max(LANES, width * 5 // 8 // LANES * LANES)
        shifts = range(1, Q)
        r, c, p = (lax.axis_index(axis) for axis in AXES)
        core = c % 2

        def scalar(value):
            return value.astype(jnp.int32).reshape(1)

        source = scalar(jnp.where(r == c, 0, 1))
        core_index = scalar(core)

        def share(shift, relative, offset, size):
            start = (p - shift + relative) % Q * width + offset
            return (core * (pairs // 2), start), (pairs // 2, size)

        def exchange(shares):
            return [
                permute_all(m, lambda r, c, p: (r, c, (p - s) % Q)) for s, m in zip(shifts, shares)
            ]

        def swap(mine):
            return [permute_all(m, lambda r, c, p: (r, c ^ 1, p)) for m in mine]

        blocks = [((0, p * width), (pairs, width))]
        blocks += [share(s, j, 0, width) for j in range(Q) for s in shifts]
        starts = jnp.stack([jnp.asarray(x, jnp.int32) for start, _ in blocks for x in start])
        own, *shares = cut_out(starts, slab, [shape for _, shape in blocks])
        shares = [shares[i : i + Q - 1] for i in range(0, len(shares), Q - 1)]

        direct_own = send(own)
        mine = exchange(shares[0])
        theirs = swap(mine)
        others = [
            assemble(core_index, mine, theirs, start, size)
            for start, size in ((0, wide), (wide, width - wide))
        ]
        direct_other0 = send(others[0])
        rest = []
        for part in shares[1:]:
            received = hold(exchange(hold(part, *mine)), direct_own)
            rest.append(assemble(core_index, received, swap(received), 0, width))
        other_weights = jnp.concatenate(
            [permute_all(weights, lambda r, c, p: (r, c, (p - s) % Q)) for s in shifts]
        )
        rows = weigh(scalar(p), slab, weights, [*others, *rest], other_weights, width)
        direct_other1 = send(hold(others[1:], rows)[0])
        columns = [own, direct_own]
        result = product(source, rows, columns, [others[0], direct_other0], None, 0, width)
        return product(source, rows, columns, [others[1], direct_other1], result, wide, width)

    return jax.shard_map(
        on_device,
        mesh=mesh,
        in_specs=(P("pair", "row"), P("pair")),
        out_specs=P("row", ("col", "pair")),
        check_vma=False,
    )
```

time: 99.5 us -> 87.9 us (0.88)
  starting transfers between devices: 36.7 us -> 24.4 us
  waiting for transfers between devices: 25.9 us -> 32.9 us
  Pallas kernels: 29.7 us -> 26.3 us
  local copies, waits for them, and re-layouts: 6.48 us -> 3.34 us
    ppermute x10 -> x8, starting transfers between devices: 36.7 us -> 24.4 us  [permute(): return lax.ppermute(block, AXES, pairs) if pairs else jnp.zeros_like(block)]
    ppermute x10 -> x8, waiting for transfers between devices: 25.9 us -> 32.9 us  [permute(): return lax.ppermute(block, AXES, pairs) if pairs else jnp.zeros_like(block)]
    dynamic_slice x3 -> x0, local copies, waits for them, and re-layouts: 3.84 us -> none  [the longest x1 2.87 us: share(): lax.dynamic_slice(slab, (core * (pairs // 2), start), (pairs // 2, width))]
    pallas_call x2, Pallas kernels: 22.6 us -> 20.9 us  [product(): pl.pallas_call(kernel, grid=(height // tile,), in_specs=in_specs, out_spe...]
    pallas_call x1, Pallas kernels: 3.14 us -> 1.94 us  [weigh(): pl.pallas_call(kernel, in_specs=[SMEM] + [VMEM] * (3 + count), out_specs=...]
    unnamed x22 -> x14, local copies, waits for them, and re-layouts: 2.44 us -> 3.05 us
    pallas_call x3 -> x4, Pallas kernels: 2.64 us -> 2.49 us  [the longest x3 1.58 us: assemble(): pl.pallas_call(kernel, in_specs=[SMEM] + [VMEM] * (2 * count), out_specs=...]
  transfers between devices with their start and end apart: 10 -> 8, of which waited for: 6 -> 6; matrix products, arithmetic and copies ran while one was open for 1% -> 0% of each run, Pallas kernels for 21% -> 20%
where the time goes in v4:
time: 87.9 us; the launch traced here: 87.2 us
  waiting for transfers between devices  32.9 us (37%)
  Pallas kernels  26.3 us (30%)
  starting transfers between devices  24.4 us (28%)
  local copies, waits for them, and re-layouts  3.34 us (4%)
    ppermute x8, waiting for transfers between devices, permute(): return lax.ppermute(block, AXES, pairs) if pairs else jnp.zeros_like(block)  32.9 us
    ppermute x8, starting transfers between devices, permute(): return lax.ppermute(block, AXES, pairs) if pairs else jnp.zeros_like(block)  24.4 us
    pallas_call x2, Pallas kernels, product(): pl.pallas_call(kernel, grid=(height // tile,), in_specs=in_specs, out_spe...  20.9 us
    unnamed x14, local copies, waits for them, and re-layouts  3.05 us
    pallas_call x1, Pallas kernels, weigh(): pl.pallas_call(kernel, in_specs=[SMEM] + [VMEM] * (3 + count), out_specs=...  1.94 us
  transfers between devices with their start and end apart: 8, of which 6 were waited for; matrix products, arithmetic and copies ran while one was open for 0% of the time, Pallas kernels for 20%

profile of v4, /device:TPU:1, one launch (start us, length us, event | category | flops | bytes accessed | tf_op | source)
XLA Modules:
  0.0 87.2 jit_solution(1739806649282513253)
XLA Ops:
  0.0 0.1 stack.20.starts
  0.1 0.0 copy-start
  0.1 1.9 %copy-done = bf16[384,4096]{1,0:T(8,128)(2,1)S(1)} copy-done((bf16[384,4096]{1,0:T(8,128)(2,1)S(1)}, bf16[384,4096]{1,0:T(8,128)(2,1)}, u32[]{:S(2)}) %copy-start) | copy-done | bytes 3145752
  2.0 0.9 %shard_map.28 = (bf16[384,2048]{1,0:T(8,128)(2,1)S(1)}, bf16[192,2048]{1,0:T(8,128)(2,1)S(1)}, bf16[192,2048]{1,0:T(8,128)(2,1)S(1)}) custom-call(s32[6]{0:T(128)S(1)} %stack.20.starts, bf16[384,4096]{1,0:T(8,128)(2,1)S(1)} %copy-done), custom_call_target="tpu_custom_call" | custom-call | tf_op jit(solution)/shard_map/pallas_call | solution.py:118
  2.9 0.0 copy-start.2
  2.9 2.1 %collective-permute-start.1 = (bf16[192,2048]{1,0:T(8,128)(2,1)S(1)}, bf16[192,2048]{1,0:T(8,128)(2,1)S(1)}, u32[]{:S(2)}, u32[]{:S(2)}) collective-permute-start(bf16[192,2048]{1,0:T(8,128)(2,1)S(1)} %get-tuple-element.8), channel_id=1, source_target_pairs={{0,1},{1,0},{2,3},{3,2},{4,5},{5,4},{6,7},{7,6},{8,9},{9,8},{10,11... | collective-permute-start | bytes 2359304 | tf_op jit(solution)/shard_map/ppermute | solution.py:224
  5.0 6.1 %collective-permute-start.4 = (bf16[384,2048]{1,0:T(8,128)(2,1)S(1)}, bf16[384,2048]{1,0:T(8,128)(2,1)S(1)}, u32[]{:S(2)}, u32[]{:S(2)}) collective-permute-start(bf16[384,2048]{1,0:T(8,128)(2,1)S(1)} %get-tuple-element.10.refs_0_), channel_id=1, source_target_pairs={{4,8},{5,9},{0,16},{1,17},{2,24},{3,25},{8,2},{9,3},{12,18},{13,19... | collective-permute-start | bytes 4718600 | tf_op jit(solution)/shard_map/ppermute | solution.py:224
  11.1 11.2 %collective-permute-done.1.refs_0_.refs_1_ = bf16[192,2048]{1,0:T(8,128)(2,1)S(1)} collective-permute-done((bf16[192,2048]{1,0:T(8,128)(2,1)S(1)}, bf16[192,2048]{1,0:T(8,128)(2,1)S(1)}, u32[]{:S(2)}, u32[]{:S(2)}) %collective-permute-start.1) | collective-permute-done | bytes 786464 | tf_op jit(solution)/shard_map/ppermute | solution.py:224
  22.3 1.2 %collective-permute-start.2 = (bf16[192,2048]{1,0:T(8,128)(2,1)S(1)}, bf16[192,2048]{1,0:T(8,128)(2,1)S(1)}, u32[]{:S(2)}, u32[]{:S(2)}) collective-permute-start(bf16[192,2048]{1,0:T(8,128)(2,1)S(1)} %collective-permute-done.1.refs_0_.refs_1_), channel_id=1, source_target_pairs={{0,2},{1,3},{2,0},{3,1},{4,6},{5,7},{6,4},{7,5},{8,10},{9,11},{10,... | collective-permute-start | bytes 2359304 | tf_op jit(solution)/shard_map/ppermute | solution.py:224
  23.5 0.1 shard_map.31
  23.6 0.0 copy-start.6
  23.6 1.5 %collective-permute-start.3 = (bf16[192,2048]{1,0:T(8,128)(2,1)S(1)}, bf16[192,2048]{1,0:T(8,128)(2,1)S(1)}, u32[]{:S(2)}, u32[]{:S(2)}) collective-permute-start(bf16[192,2048]{1,0:T(8,128)(2,1)S(1)} %shard_map.31), channel_id=1, source_target_pairs={{0,1},{1,0},{2,3},{3,2},{4,5},{5,4},{6,7},{7,6},{8,9},{9,8},{10,11... | collective-permute-start | bytes 2359304 | tf_op jit(solution)/shard_map/ppermute | solution.py:224
  25.1 0.3 collective-permute-done.2.refs_1_
  25.4 0.0 copy-start.4
  25.4 0.1 shard_map.29.refs_0_.refs_2_
  25.5 5.7 %collective-permute-start.7 = (bf16[384,1280]{1,0:T(8,128)(2,1)S(1)}, bf16[384,1280]{1,0:T(8,128)(2,1)}, u32[]{:S(2)}, u32[]{:S(2)}) collective-permute-start(bf16[384,1280]{1,0:T(8,128)(2,1)S(1)} %shard_map.29.refs_0_.refs_2_), channel_id=1, source_target_pairs={{4,8},{5,9},{0,16},{1,17},{2,24},{3,25},{8,2},{9,3},{12,18},{13,19... | collective-permute-start | bytes 2949128 | tf_op jit(solution)/shard_map/ppermute | solution.py:224
  31.2 0.0 copy-done.4
  31.2 11.6 %collective-permute-done.3.refs_0_ = bf16[192,2048]{1,0:T(8,128)(2,1)S(1)} collective-permute-done((bf16[192,2048]{1,0:T(8,128)(2,1)S(1)}, bf16[192,2048]{1,0:T(8,128)(2,1)S(1)}, u32[]{:S(2)}, u32[]{:S(2)}) %collective-permute-start.3) | collective-permute-done | bytes 786464 | tf_op jit(solution)/shard_map/ppermute | solution.py:224
  42.8 2.4 %collective-permute-done.4.refs_1_ = bf16[384,2048]{1,0:T(8,128)(2,1)S(1)} collective-permute-done((bf16[384,2048]{1,0:T(8,128)(2,1)S(1)}, bf16[384,2048]{1,0:T(8,128)(2,1)S(1)}, u32[]{:S(2)}, u32[]{:S(2)}) %collective-permute-start.4) | collective-permute-done | bytes 1572896 | tf_op jit(solution)/shard_map/ppermute | solution.py:224
  45.2 0.9 %shard_map.32.refs_0_ = bf16[192,2048]{1,0:T(8,128)(2,1)} custom-call(bf16[192,2048]{1,0:T(8,128)(2,1)S(1)} %collective-permute-done.3.refs_0_, bf16[384,2048]{1,0:T(8,128)(2,1)S(1)} %collective-permute-done.4.refs_1_), custom_call_target="tpu_custom_call" | custom-call | tf_op jit(solution)/shard_map/pallas_call | solution.py:155
  46.2 0.0 copy-done.2
  46.2 0.0 collective-permute-start.5
  46.2 0.0 copy-done.6
  46.2 0.3 collective-permute-start
  46.5 0.1 broadcast_in_dim.8.weights
  46.6 0.0 copy-start.1
  46.6 2.1 %collective-permute-done = f32[384]{0:T(512)S(1)} collective-permute-done((f32[384]{0:T(512)S(1)}, f32[384]{0:T(512)S(1)}, u32[]{:S(2)}, u32[]{:S(2)}) %collective-permute-start) | collective-permute-done | bytes 1568 | tf_op jit(solution)/shard_map/ppermute | solution.py:224
  48.7 0.1 broadcast_in_dim.9.other_weights
  48.8 0.0 copy-start.5
  48.8 1.1 %copy-done.5 = bf16[192,2048]{1,0:T(8,128)(2,1)S(1)} copy-done((bf16[192,2048]{1,0:T(8,128)(2,1)S(1)}, bf16[192,2048]{1,0:T(8,128)(2,1)}, u32[]{:S(2)}) %copy-start.5) | copy-done | bytes 786456
  50.0 0.0 collective-permute-done.5.refs_1_
  50.0 1.5 %shard_map.33.refs_2_ = bf16[384,2048]{1,0:T(8,128)(2,1)S(1)} custom-call(s32[1]{0:T(128)} %bitcast.2.core, bf16[192,2048]{1,0:T(8,128)(2,1)} %shard_map.32.refs_0_, bf16[192,2048]{1,0:T(8,128)(2,1)} %collective-permute-done.5.refs_1_), custom_call_target="tpu_custom_call" | custom-call | tf_op jit(solution)/shard_map/pallas_call | solution.py:139
  51.5 0.0 copy-done.1
  51.5 1.9 %shard_map.34.refs_1_.rows = bf16[768,4096]{1,0:T(8,128)(2,1)S(1)} custom-call(s32[1]{0:T(128)} %bitcast.1.index, bf16[384,4096]{1,0:T(8,128)(2,1)S(1)} %copy-done.1, f32[384,1]{1,0:T(8,128)S(1)} %broadcast_in_dim.8.weights, f32[384,1]{1,0:T(8,128)S(1)} %broadcast_in_dim.9.other_weights, bf16[384,1280]{1,0:T(8,128)(2,1)S(1)} %shard_map.29.refs_0_.refs_2_, ...), custom_call_target="tpu_custom_call" | custom-call | tf_op jit(solution)/shard_map/pallas_call | solution.py:94
  53.4 0.0 copy-start.3
  53.5 7.5 %collective-permute-start.6 = (bf16[384,768]{1,0:T(8,128)(2,1)S(1)}, bf16[384,768]{1,0:T(8,128)(2,1)S(1)}, u32[]{:S(2)}, u32[]{:S(2)}) collective-permute-start(bf16[384,768]{1,0:T(8,128)(2,1)S(1)} %shard_map.35), channel_id=1, source_target_pairs={{4,8},{5,9},{0,16},{1,17},{2,24},{3,25},{8,2},{9,3},{12,18},{13,19... | collective-permute-start | bytes 1769480 | tf_op jit(solution)/shard_map/ppermute | solution.py:224
  60.9 5.3 %collective-permute-done.7.refs_3_ = bf16[384,1280]{1,0:T(8,128)(2,1)} collective-permute-done((bf16[384,1280]{1,0:T(8,128)(2,1)S(1)}, bf16[384,1280]{1,0:T(8,128)(2,1)}, u32[]{:S(2)}, u32[]{:S(2)}) %collective-permute-start.7) | collective-permute-done | bytes 983072 | tf_op jit(solution)/shard_map/ppermute | solution.py:224
  66.3 0.0 copy-done.3
  66.3 13.0 %shard_map.36.refs_4_ = f32[4096,2048]{1,0:T(8,128)} custom-call(s32[1]{0:T(128)} %bitcast.source, bf16[768,4096]{1,0:T(8,128)(2,1)S(1)} %shard_map.34.refs_1_.rows, bf16[384,2048]{1,0:T(8,128)(2,1)S(1)} %copy-done.3, bf16[384,2048]{1,0:T(8,128)(2,1)S(1)} %collective-permute-done.4.refs_1_, bf16[384,1280]{1,0:T(8,128)(2,1)S(1)} %shard_map.29.refs_0_.refs_2_, ...), custom_call_target="tpu_custom_call" | custom-call | flops 8053063680 | bytes 20971520 | tf_op jit(solution)/shard_map/pallas_call | solution.py:50
  79.3 0.0 collective-permute-done.6.refs_3_
  79.3 7.9 %shard_map.37 = f32[4096,2048]{1,0:T(8,128)} custom-call(s32[1]{0:T(128)} %bitcast.source, bf16[768,4096]{1,0:T(8,128)(2,1)S(1)} %shard_map.34.refs_1_.rows, bf16[384,2048]{1,0:T(8,128)(2,1)S(1)} %copy-done.3, bf16[384,2048]{1,0:T(8,128)(2,1)S(1)} %collective-permute-done.4.refs_1_, ...), custom_call_target="tpu_custom_call", output_to_operand_aliasing={{}: (6, {})} | custom-call | flops 4831838208 | bytes 12582912 | tf_op jit(solution)/shard_map/pallas_call | solution.py:50
  (2 shorter events, 0.1 us)
Async XLA Ops:
  0.1 1.9 %copy-start = (bf16[384,4096]{1,0:T(8,128)(2,1)S(1)}, bf16[384,4096]{1,0:T(8,128)(2,1)}, u32[]{:S(2)}) copy-start(bf16[384,4096]{1,0:T(8,128)(2,1)} %slab.3) | copy-start | bytes 9437188
  2.9 43.3 %copy-start.2 = (bf16[384,2048]{1,0:T(8,128)(2,1)}, bf16[384,2048]{1,0:T(8,128)(2,1)S(1)}, u32[]{:S(2)}) copy-start(bf16[384,2048]{1,0:T(8,128)(2,1)S(1)} %get-tuple-element.10.refs_0_) | copy-start | bytes 4718596
  2.9 19.4 %collective-permute-start.1 = (bf16[192,2048]{1,0:T(8,128)(2,1)S(1)}, bf16[192,2048]{1,0:T(8,128)(2,1)S(1)}, u32[]{:S(2)}, u32[]{:S(2)}) collective-permute-start(bf16[192,2048]{1,0:T(8,128)(2,1)S(1)} %get-tuple-element.8), channel_id=1, source_target_pairs={{0,1},{1,0},{2,3},{3,2},{4,5},{5,4},{6,7},{7,6},{8,9},{9,8},{10,11... | collective-permute-start | bytes 2359304 | tf_op jit(solution)/shard_map/ppermute | solution.py:224
  5.0 40.2 %collective-permute-start.4 = (bf16[384,2048]{1,0:T(8,128)(2,1)S(1)}, bf16[384,2048]{1,0:T(8,128)(2,1)S(1)}, u32[]{:S(2)}, u32[]{:S(2)}) collective-permute-start(bf16[384,2048]{1,0:T(8,128)(2,1)S(1)} %get-tuple-element.10.refs_0_), channel_id=1, source_target_pairs={{4,8},{5,9},{0,16},{1,17},{2,24},{3,25},{8,2},{9,3},{12,18},{13,19... | collective-permute-start | bytes 4718600 | tf_op jit(solution)/shard_map/ppermute | solution.py:224
  22.3 3.1 %collective-permute-start.2 = (bf16[192,2048]{1,0:T(8,128)(2,1)S(1)}, bf16[192,2048]{1,0:T(8,128)(2,1)S(1)}, u32[]{:S(2)}, u32[]{:S(2)}) collective-permute-start(bf16[192,2048]{1,0:T(8,128)(2,1)S(1)} %collective-permute-done.1.refs_0_.refs_1_), channel_id=1, source_target_pairs={{0,2},{1,3},{2,0},{3,1},{4,6},{5,7},{6,4},{7,5},{8,10},{9,11},{10,... | collective-permute-start | bytes 2359304 | tf_op jit(solution)/shard_map/ppermute | solution.py:224
  23.6 22.6 %copy-start.6 = (f32[384]{0:T(512)S(1)}, f32[384]{0:T(512)}, u32[]{:S(2)}) copy-start(f32[384]{0:T(512)} %param.3) | copy-start | bytes 4612
  23.6 19.2 %collective-permute-start.3 = (bf16[192,2048]{1,0:T(8,128)(2,1)S(1)}, bf16[192,2048]{1,0:T(8,128)(2,1)S(1)}, u32[]{:S(2)}, u32[]{:S(2)}) collective-permute-start(bf16[192,2048]{1,0:T(8,128)(2,1)S(1)} %shard_map.31), channel_id=1, source_target_pairs={{0,1},{1,0},{2,3},{3,2},{4,5},{5,4},{6,7},{7,6},{8,9},{9,8},{10,11... | collective-permute-start | bytes 2359304 | tf_op jit(solution)/shard_map/ppermute | solution.py:224
  25.4 5.8 %copy-start.4 = (bf16[192,2048]{1,0:T(8,128)(2,1)}, bf16[192,2048]{1,0:T(8,128)(2,1)S(1)}, u32[]{:S(2)}) copy-start(bf16[192,2048]{1,0:T(8,128)(2,1)S(1)} %collective-permute-done.2.refs_1_) | copy-start | bytes 2359300
  25.5 40.8 %collective-permute-start.7 = (bf16[384,1280]{1,0:T(8,128)(2,1)S(1)}, bf16[384,1280]{1,0:T(8,128)(2,1)}, u32[]{:S(2)}, u32[]{:S(2)}) collective-permute-start(bf16[384,1280]{1,0:T(8,128)(2,1)S(1)} %shard_map.29.refs_0_.refs_2_), channel_id=1, source_target_pairs={{4,8},{5,9},{0,16},{1,17},{2,24},{3,25},{8,2},{9,3},{12,18},{13,19... | collective-permute-start | bytes 2949128 | tf_op jit(solution)/shard_map/ppermute | solution.py:224
  46.2 3.8 %collective-permute-start.5 = (bf16[192,2048]{1,0:T(8,128)(2,1)}, bf16[192,2048]{1,0:T(8,128)(2,1)}, u32[]{:S(2)}, u32[]{:S(2)}) collective-permute-start(bf16[192,2048]{1,0:T(8,128)(2,1)} %shard_map.32.refs_0_), channel_id=1, source_target_pairs={{0,2},{1,3},{2,0},{3,1},{4,6},{5,7},{6,4},{7,5},{8,10},{9,11},{10,... | collective-permute-start | bytes 2359304 | tf_op jit(solution)/shard_map/ppermute | solution.py:224
  46.2 2.5 %collective-permute-start = (f32[384]{0:T(512)S(1)}, f32[384]{0:T(512)S(1)}, u32[]{:S(2)}, u32[]{:S(2)}) collective-permute-start(f32[384]{0:T(512)S(1)} %copy-done.6), channel_id=1, source_target_pairs={{0,1},{1,0},{2,3},{3,2},{4,5},{5,4},{6,7},{7,6},{8,9},{9,8},{10,11... | collective-permute-start | bytes 4616 | tf_op jit(solution)/shard_map/ppermute | solution.py:224
  46.6 4.9 %copy-start.1 = (bf16[384,4096]{1,0:T(8,128)(2,1)S(1)}, bf16[384,4096]{1,0:T(8,128)(2,1)}, u32[]{:S(2)}) copy-start(bf16[384,4096]{1,0:T(8,128)(2,1)} %slab.3) | copy-start | bytes 9437188
  48.8 1.1 %copy-start.5 = (bf16[192,2048]{1,0:T(8,128)(2,1)S(1)}, bf16[192,2048]{1,0:T(8,128)(2,1)}, u32[]{:S(2)}) copy-start(bf16[192,2048]{1,0:T(8,128)(2,1)} %copy-done.4) | copy-start | bytes 2359300
  53.4 12.9 %copy-start.3 = (bf16[384,2048]{1,0:T(8,128)(2,1)S(1)}, bf16[384,2048]{1,0:T(8,128)(2,1)}, u32[]{:S(2)}) copy-start(bf16[384,2048]{1,0:T(8,128)(2,1)} %copy-done.2) | copy-start | bytes 4718596
  53.5 25.8 %collective-permute-start.6 = (bf16[384,768]{1,0:T(8,128)(2,1)S(1)}, bf16[384,768]{1,0:T(8,128)(2,1)S(1)}, u32[]{:S(2)}, u32[]{:S(2)}) collective-permute-start(bf16[384,768]{1,0:T(8,128)(2,1)S(1)} %shard_map.35), channel_id=1, source_target_pairs={{4,8},{5,9},{0,16},{1,17},{2,24},{3,25},{8,2},{9,3},{12,18},{13,19... | collective-permute-start | bytes 1769480 | tf_op jit(solution)/shard_map/ppermute | solution.py:224

commit v5 on v4

--- a/solution.py
+++ b/solution.py
@@ -7,20 +7,23 @@
 
 AXES = ("row", "col", "pair")
 LANES = 128
+PLACE, CORE, OWN_OR_SENT, STARTS = range(4)
+PARTS = 3
 VMEM = pl.BlockSpec(memory_space=pltpu.VMEM)
 SMEM = pl.BlockSpec(memory_space=pltpu.SMEM)
 ANY = pl.BlockSpec(memory_space=pl.ANY)
+HBM = pl.BlockSpec(memory_space=pltpu.HBM)
 
 
 def params(mib):
     return pltpu.CompilerParams(vmem_limit_bytes=mib * 2**20)
 
 
-def product(source, rows, own, other, result, first, columns):
+def product(places, rows, own, other, result, first, columns):
     depth, height = rows.shape
     pairs, width = own[0].shape[0], other[0].shape[1]
     tile = 1024 if height % 1024 == 0 else height
-    args = [source, rows, *own, *other]
+    args = [places, rows, *own, *other]
     in_specs = [SMEM] + [VMEM] * (len(args) - 1)
     aliases = {}
     if result is not None:
@@ -28,7 +31,7 @@
         in_specs.append(ANY)
         args.append(result)
 
-    def kernel(source, rows, *refs):
+    def kernel(places, rows, *refs):
         out, held = refs[-2:]
 
         @pl.when(pl.program_id(0) == 0)
@@ -38,7 +41,7 @@
                 for i in range(len(choices)):
                     start = first if choices is own else 0
 
-                    @pl.when(source[0] == i)
+                    @pl.when(places[OWN_OR_SENT] == i)
                     def _(part=part, i=skip + i, start=start):
                         held[part, :] = refs[i][:, start : start + width]
 
@@ -55,60 +58,83 @@
         out_shape=jax.ShapeDtypeStruct((height, columns), jnp.float32),
         scratch_shapes=[pltpu.VMEM((depth, width), jnp.bfloat16)],
         input_output_aliases=aliases,
-        compiler_params=params(24),
+        compiler_params=params(5 + (8 * tile + 2 * depth) * width // 2**20),
         cost_estimate=pl.CostEstimate(
             flops=2 * height * width * depth, bytes_accessed=4 * height * width, transcendentals=0
         ),
     )(*args)
 
 
-def weigh(index, slab, weights, other_parts, other_weights, width):
+def weigh(places, slab, weights, others, rest, other_weights, width):
     pairs, height = slab.shape
-    others = other_weights.shape[0]
-    count = len(other_parts)
-    step = 64 if pairs % 64 == 0 else pairs
-
-    def kernel(index, slab, weights, other_weights, *refs):
-        parts, out = refs[:count], refs[-1]
-
-        def scaled(by, rows):
-            return (by * rows.astype(jnp.float32)).astype(out.dtype)
+    half = pairs // 2
+    shifts = len(rest[0][0])
+    step = 64 if half % 64 == 0 else half
+    arrays = [*others, *(m for mine, theirs in rest for m in (*mine, *theirs))]
+
+    def kernel(places, slab, weights, other_weights, *refs):
+        *refs, out, own, arrived = refs
+        fetch = pltpu.make_async_copy(slab, own, arrived)
+        fetch.start()
+
+        def put(rows, by, ref, at, column):
+            start = pl.multiple_of(lax.rem(places[PLACE] * width + column, height), LANES)
+            to = pl.ds(pl.multiple_of(pairs + rows, step), step)
+            value = by[pl.ds(pl.multiple_of(rows, step), step), :] * ref[at, :].astype(jnp.float32)
+            out[to, pl.ds(start, ref.shape[1])] = value.astype(out.dtype)
+
+        @pl.loop(0, shifts * pairs // step)
+        def _(i):
+            at = pl.ds(pl.multiple_of(i * step, step), step)
+            column = 0
+            for ref in refs[: len(others)]:
+                put(i * step, other_weights, ref, at, column)
+                column += ref.shape[1]
+
+        @pl.loop(0, half // step)
+        def _(i):
+            at = pl.ds(pl.multiple_of(i * step, step), step)
+            parts = iter(refs[len(others) :])
+            column = width
+            for mine, _ in rest:
+                for first in (places[CORE], 1 - places[CORE]):
+                    for shift in range(shifts):
+                        put(shift * pairs + first * half + i * step, other_weights, next(parts), at, column)
+                column += mine[0].shape[1]
+
+        fetch.wait()
 
         @pl.loop(0, pairs // step)
         def _(i):
             at = pl.ds(pl.multiple_of(i * step, step), step)
-            out[at, :] = scaled(weights[at, :], slab[at, :])
-
-        @pl.loop(0, others // step)
-        def _(i):
-            at = pl.ds(pl.multiple_of(i * step, step), step)
-            to = pl.ds(pl.multiple_of(pairs + i * step, step), step)
-            by = other_weights[at, :]
-            offset = 0
-            for part in parts:
-                size = part.shape[1]
-                start = lax.rem(index[0] * width + offset, height)
-                out[to, pl.ds(pl.multiple_of(start, LANES), size)] = scaled(by, part[at, :])
-                offset += size
+            out[at, :] = (weights[at, :] * own[at, :].astype(jnp.float32)).astype(out.dtype)
 
     return pl.pallas_call(
         kernel,
-        in_specs=[SMEM] + [VMEM] * (3 + count),
+        in_specs=[SMEM, HBM] + [VMEM] * (2 + len(arrays)),
         out_specs=VMEM,
-        out_shape=jax.ShapeDtypeStruct((pairs + others, height), slab.dtype),
-        compiler_params=params(16),
-    )(index, slab, weights[:, None], other_weights[:, None], *other_parts)
-
-
-def cut_out(starts, slab, shapes):
+        out_shape=jax.ShapeDtypeStruct(((1 + shifts) * pairs, height), slab.dtype),
+        scratch_shapes=[pltpu.VMEM(slab.shape, slab.dtype), pltpu.SemaphoreType.DMA],
+        compiler_params=params(3 + 2 * pairs * height // 2**20),
+    )(places, slab, weights[:, None], other_weights[:, None], *arrays)
+
+
+def split(width, count, last):
+    lanes = (width - last) // LANES
+    count = min(count, lanes)
+    sizes = [LANES * (lanes // count + (i < lanes % count)) for i in range(count)] + [last] * (last > 0)
+    return [(sum(sizes[:i]), size) for i, size in enumerate(sizes)]
+
+
+def cut_out(places, slab, shapes):
     count = len(shapes)
 
-    def kernel(starts, slab, *refs):
+    def kernel(places, slab, *refs):
         outs, done = refs[:count], refs[-1]
         copies = []
         for i, (rows, size) in enumerate(shapes):
-            at = pl.ds(pl.multiple_of(starts[2 * i], 16), rows)
-            across = pl.ds(pl.multiple_of(starts[2 * i + 1], LANES), size)
+            at = pl.ds(pl.multiple_of(places[STARTS + 2 * i], 16), rows)
+            across = pl.ds(pl.multiple_of(places[STARTS + 2 * i + 1], LANES), size)
             copies.append(pltpu.make_async_copy(slab.at[at, across], outs[i], done.at[i]))
         for copy in copies:
             copy.start()
@@ -117,48 +143,51 @@
 
     return pl.pallas_call(
         kernel,
-        in_specs=[SMEM, ANY],
+        in_specs=[SMEM, HBM],
         out_specs=[VMEM] * count,
         out_shape=[jax.ShapeDtypeStruct(shape, slab.dtype) for shape in shapes],
         scratch_shapes=[pltpu.SemaphoreType.DMA((count,))],
-        compiler_params=params(16),
-    )(starts, slab)
-
-
-def assemble(core, mine, theirs, start, size):
+        compiler_params=params(2),
+    )(places, slab)
+
+
+def assemble(places, mine, theirs, start, size, *earlier):
     count = len(mine)
     half = mine[0].shape[0]
 
-    def kernel(core, *refs):
+    def kernel(places, *refs):
         out = refs[-1]
         for i in range(count):
-            for rows, ref in ((core[0], refs[i]), (1 - core[0], refs[count + i])):
+            for rows, ref in ((places[CORE], refs[i]), (1 - places[CORE], refs[count + i])):
                 at = pl.multiple_of((2 * i + rows) * half, half)
                 out[pl.ds(at, half), :] = ref[:, start : start + size]
 
     return pl.pallas_call(
         kernel,
-        in_specs=[SMEM] + [VMEM] * (2 * count),
+        in_specs=[SMEM] + [VMEM] * (2 * count) + [ANY] * len(earlier),
         out_specs=VMEM,
         out_shape=jax.ShapeDtypeStruct((2 * count * half, size), mine[0].dtype),
-        compiler_params=params(16),
-    )(core, *mine, *theirs)
-
-
-def hold(values, *earlier):
+        compiler_params=params(2),
+    )(places, *mine, *theirs, *earlier)
+
+
+def hold(values, spans, *earlier):
     count = len(values)
 
     def kernel(*refs):
-        for value, out in zip(refs[:count], refs[-count:]):
-            out[...] = value[...]
-
-    return pl.pallas_call(
+        outs = iter(refs[count + len(earlier) :])
+        for start, size in spans:
+            for value in refs[:count]:
+                next(outs)[...] = value[:, start : start + size]
+
+    outs = pl.pallas_call(
         kernel,
         in_specs=[VMEM] * count + [ANY] * len(earlier),
-        out_specs=[VMEM] * count,
-        out_shape=[jax.ShapeDtypeStruct(v.shape, v.dtype) for v in values],
-        compiler_params=params(16),
+        out_specs=[VMEM] * (count * len(spans)),
+        out_shape=[jax.ShapeDtypeStruct((v.shape[0], n), v.dtype) for _, n in spans for v in values],
+        compiler_params=params(2),
     )(*values, *earlier)
+    return [outs[i : i + count] for i in range(0, len(outs), count)]
 
 
 def pick_senders(planes, columns):
@@ -235,16 +264,11 @@
     def on_device(slab, weights):
         pairs, block = slab.shape
         width = block // Q
-        wide = max(LANES, width * 5 // 8 // LANES * LANES)
+        spans = split(width, PARTS - 1, max(LANES, width * 1 // 4 // LANES * LANES))
+        halves = split(width, 2, 0)
         shifts = range(1, Q)
         r, c, p = (lax.axis_index(axis) for axis in AXES)
         core = c % 2
-
-        def scalar(value):
-            return value.astype(jnp.int32).reshape(1)
-
-        source = scalar(jnp.where(r == c, 0, 1))
-        core_index = scalar(core)
 
         def share(shift, relative, offset, size):
             start = (p - shift + relative) % Q * width + offset
@@ -260,30 +284,34 @@
 
         blocks = [((0, p * width), (pairs, width))]
         blocks += [share(s, j, 0, width) for j in range(Q) for s in shifts]
-        starts = jnp.stack([jnp.asarray(x, jnp.int32) for start, _ in blocks for x in start])
-        own, *shares = cut_out(starts, slab, [shape for _, shape in blocks])
+        starts = [x for start, _ in blocks for x in start]
+        places = jnp.stack([jnp.asarray(x, jnp.int32) for x in (p, core, jnp.where(r == c, 0, 1), *starts)])
+        own, *shares = cut_out(places, slab, [shape for _, shape in blocks])
         shares = [shares[i : i + Q - 1] for i in range(0, len(shares), Q - 1)]
 
+        other_weights = jnp.concatenate(
+            [permute_all(weights, lambda r, c, p: (r, c, (p - s) % Q)) for s in shifts]
+        )
         direct_own = send(own)
         mine = exchange(shares[0])
         theirs = swap(mine)
-        others = [
-            assemble(core_index, mine, theirs, start, size)
-            for start, size in ((0, wide), (wide, width - wide))
-        ]
-        direct_other0 = send(others[0])
+        others = [assemble(places, mine, theirs, *span) for span in spans]
+        direct_others = [send(others[0])]
         rest = []
         for part in shares[1:]:
-            received = hold(exchange(hold(part, *mine)), direct_own)
-            rest.append(assemble(core_index, received, swap(received), 0, width))
-        other_weights = jnp.concatenate(
-            [permute_all(weights, lambda r, c, p: (r, c, (p - s) % Q)) for s in shifts]
-        )
-        rows = weigh(scalar(p), slab, weights, [*others, *rest], other_weights, width)
-        direct_other1 = send(hold(others[1:], rows)[0])
-        columns = [own, direct_own]
-        result = product(source, rows, columns, [others[0], direct_other0], None, 0, width)
-        return product(source, rows, columns, [others[1], direct_other1], result, wide, width)
+            part = hold(part, [(0, width)], other_weights)[0]
+            for piece in hold(part, halves, *mine):
+                received = exchange(piece)
+                received = hold(received, [(0, received[0].shape[1])], direct_own)[0]
+                rest.append((received, swap(received)))
+        rows = weigh(places, slab, weights, others, rest, other_weights, width)
+        for i, other in enumerate(others[1:], 1):
+            earlier = rows if i == len(others) - 1 else direct_own
+            direct_others.append(send(hold([other], [(0, other.shape[1])], earlier)[0][0]))
+        result = None
+        for other, sent, (start, _) in zip(others, direct_others, spans):
+            result = product(places, rows, [own, direct_own], [other, sent], result, start, width)
+        return result
 
     return jax.shard_map(
         on_device,

time: 87.9 us -> 85.9 us (0.977)
  waiting for transfers between devices: 32.9 us -> 24.4 us
  starting transfers between devices: 24.4 us -> 29.6 us
  Pallas kernels: 26.3 us -> 29 us
  local copies, waits for them, and re-layouts: 3.34 us -> 2.2 us
    ppermute x8 -> x11, waiting for transfers between devices: 32.9 us -> 24.4 us  [permute(): return lax.ppermute(block, AXES, pairs) if pairs else jnp.zeros_like(block)]
    ppermute x8 -> x11, starting transfers between devices: 24.4 us -> 29.6 us  [permute(): return lax.ppermute(block, AXES, pairs) if pairs else jnp.zeros_like(block)]
    pallas_call x2 -> x3, Pallas kernels: 20.9 us -> 23.4 us  [product(): pl.pallas_call(kernel, grid=(height // tile,), in_specs=in_specs, out_spe...]
    unnamed x14 -> x6, local copies, waits for them, and re-layouts: 3.05 us -> 1.9 us
    pallas_call x5, Pallas kernels: 4.43 us -> 5.35 us  [the longest x1 2.68 us: weigh(): pl.pallas_call(kernel, in_specs=[SMEM, HBM] + [VMEM] * (2 + len(arrays)),...]
  transfers between devices with their start and end apart: 8 -> 11, of which waited for: 6 -> 5; matrix products, arithmetic and copies ran while one was open for 0% -> 0% of each run, Pallas kernels for 20% -> 25%
where the time goes in v5:
time: 85.9 us; the launch traced here: 85.4 us
  starting transfers between devices  29.6 us (34%)
  Pallas kernels  29 us (34%)
  waiting for transfers between devices  24.4 us (28%)
  local copies, waits for them, and re-layouts  2.2 us (3%)
    ppermute x11, starting transfers between devices, permute(): return lax.ppermute(block, AXES, pairs) if pairs else jnp.zeros_like(block)  29.6 us
    ppermute x11, waiting for transfers between devices, permute(): return lax.ppermute(block, AXES, pairs) if pairs else jnp.zeros_like(block)  24.4 us
    pallas_call x3, Pallas kernels, product(): pl.pallas_call(kernel, grid=(height // tile,), in_specs=in_specs, out_spe...  23.4 us
    pallas_call x1, Pallas kernels, weigh(): pl.pallas_call(kernel, in_specs=[SMEM, HBM] + [VMEM] * (2 + len(arrays)),...  2.68 us
    unnamed x6, local copies, waits for them, and re-layouts  1.9 us
    pallas_call x3, Pallas kernels, assemble(): pl.pallas_call(kernel, in_specs=[SMEM] + [VMEM] * (2 * count) + [ANY] * l...  1.75 us
  transfers between devices with their start and end apart: 11, of which 5 were waited for; matrix products, arithmetic and copies ran while one was open for 0% of the time, Pallas kernels for 25%

profile of v5, /device:TPU:1, one launch (start us, length us, event | category | flops | bytes accessed | tf_op | source)
XLA Modules:
  0.0 85.4 jit_solution(17863516508471766728)
XLA Ops:
  0.0 0.1 stack.32.places
  0.1 0.0 copy-start
  0.1 1.9 %copy-done = bf16[384,4096]{1,0:T(8,128)(2,1)S(1)} copy-done((bf16[384,4096]{1,0:T(8,128)(2,1)S(1)}, bf16[384,4096]{1,0:T(8,128)(2,1)}, u32[]{:S(2)}) %copy-start) | copy-done | bytes 3145752
  2.0 0.9 %shard_map.28 = (bf16[384,2048]{1,0:T(8,128)(2,1)S(1)}, bf16[192,2048]{1,0:T(8,128)(2,1)S(1)}, bf16[192,2048]{1,0:T(8,128)(2,1)S(1)}) custom-call(s32[9]{0:T(128)S(1)} %stack.32.places, bf16[384,4096]{1,0:T(8,128)(2,1)S(1)} %copy-done), custom_call_target="tpu_custom_call" | custom-call | tf_op jit(solution)/shard_map/pallas_call | solution.py:144
  2.9 2.1 %collective-permute-start.1 = (bf16[192,2048]{1,0:T(8,128)(2,1)S(1)}, bf16[192,2048]{1,0:T(8,128)(2,1)S(1)}, u32[]{:S(2)}, u32[]{:S(2)}) collective-permute-start(bf16[192,2048]{1,0:T(8,128)(2,1)S(1)} %get-tuple-element.10), channel_id=1, source_target_pairs={{0,1},{1,0},{2,3},{3,2},{4,5},{5,4},{6,7},{7,6},{8,9},{9,8},{10,11... | collective-permute-start | bytes 2359304 | tf_op jit(solution)/shard_map/ppermute | solution.py:253
  5.0 6.1 %collective-permute-start.4 = (bf16[384,2048]{1,0:T(8,128)(2,1)S(1)}, bf16[384,2048]{1,0:T(8,128)(2,1)S(1)}, u32[]{:S(2)}, u32[]{:S(2)}) collective-permute-start(bf16[384,2048]{1,0:T(8,128)(2,1)S(1)} %get-tuple-element.13.refs_0_), channel_id=1, source_target_pairs={{4,8},{5,9},{0,16},{1,17},{2,24},{3,25},{8,2},{9,3},{12,18},{13,19... | collective-permute-start | bytes 4718600 | tf_op jit(solution)/shard_map/ppermute | solution.py:253
  11.1 11.2 %collective-permute-done.1.refs_0_.refs_1_ = bf16[192,2048]{1,0:T(8,128)(2,1)S(1)} collective-permute-done((bf16[192,2048]{1,0:T(8,128)(2,1)S(1)}, bf16[192,2048]{1,0:T(8,128)(2,1)S(1)}, u32[]{:S(2)}, u32[]{:S(2)}) %collective-permute-start.1) | collective-permute-done | bytes 786464 | tf_op jit(solution)/shard_map/ppermute | solution.py:253
  22.3 1.2 %collective-permute-start.2 = (bf16[192,2048]{1,0:T(8,128)(2,1)S(1)}, bf16[192,2048]{1,0:T(8,128)(2,1)S(1)}, u32[]{:S(2)}, u32[]{:S(2)}) collective-permute-start(bf16[192,2048]{1,0:T(8,128)(2,1)S(1)} %collective-permute-done.1.refs_0_.refs_1_), channel_id=1, source_target_pairs={{0,2},{1,3},{2,0},{3,1},{4,6},{5,7},{6,4},{7,5},{8,10},{9,11},{10,... | collective-permute-start | bytes 2359304 | tf_op jit(solution)/shard_map/ppermute | solution.py:253
  23.5 1.5 %collective-permute-start = (f32[384]{0:T(512)}, f32[384]{0:T(512)S(1)}, u32[]{:S(2)}, u32[]{:S(2)}) collective-permute-start(f32[384]{0:T(512)} %param.3), channel_id=1, source_target_pairs={{0,1},{1,0},{2,3},{3,2},{4,5},{5,4},{6,7},{7,6},{8,9},{9,8},{10,11... | collective-permute-start | bytes 4616 | tf_op jit(solution)/shard_map/ppermute | solution.py:253
  25.0 1.2 %collective-permute-done.refs_1_ = f32[384]{0:T(512)S(1)} collective-permute-done((f32[384]{0:T(512)}, f32[384]{0:T(512)S(1)}, u32[]{:S(2)}, u32[]{:S(2)}) %collective-permute-start) | collective-permute-done | bytes 1568 | tf_op jit(solution)/shard_map/ppermute | solution.py:253
  26.2 0.1 shard_map.32.refs_0_
  26.2 0.1 shard_map.33
  26.3 0.0 copy-start.2
  26.3 1.5 %collective-permute-start.6 = (bf16[192,1024]{1,0:T(8,128)(2,1)S(1)}, bf16[192,1024]{1,0:T(8,128)(2,1)S(1)}, u32[]{:S(2)}, u32[]{:S(2)}) collective-permute-start(bf16[192,1024]{1,0:T(8,128)(2,1)S(1)} %get-tuple-element.14), channel_id=1, source_target_pairs={{0,1},{1,0},{2,3},{3,2},{4,5},{5,4},{6,7},{7,6},{8,9},{9,8},{10,11... | collective-permute-start | bytes 1179656 | tf_op jit(solution)/shard_map/ppermute | solution.py:253
  27.8 0.1 collective-permute-start.3
  27.9 0.0 collective-permute-done.2.refs_1_
  27.9 0.6 shard_map.29.refs_0_.refs_2_
  28.5 0.0 copy-start.1
  28.5 7.2 %collective-permute-start.10 = (bf16[384,768]{1,0:T(8,128)(2,1)S(1)}, bf16[384,768]{1,0:T(8,128)(2,1)S(1)}, u32[]{:S(2)}, u32[]{:S(2)}) collective-permute-start(bf16[384,768]{1,0:T(8,128)(2,1)S(1)} %shard_map.29.refs_0_.refs_2_), channel_id=1, source_target_pairs={{4,8},{5,9},{0,16},{1,17},{2,24},{3,25},{8,2},{9,3},{12,18},{13,19... | collective-permute-start | bytes 1769480 | tf_op jit(solution)/shard_map/ppermute | solution.py:253
  35.8 0.1 collective-permute-done.6.refs_0_
  35.8 9.4 %collective-permute-done.4.refs_1_ = bf16[384,2048]{1,0:T(8,128)(2,1)S(1)} collective-permute-done((bf16[384,2048]{1,0:T(8,128)(2,1)S(1)}, bf16[384,2048]{1,0:T(8,128)(2,1)S(1)}, u32[]{:S(2)}, u32[]{:S(2)}) %collective-permute-start.4) | collective-permute-done | bytes 1572896 | tf_op jit(solution)/shard_map/ppermute | solution.py:253
  45.2 0.1 collective-permute-start.7
  45.3 0.0 collective-permute-done.3.refs_0_
  45.4 1.1 %collective-permute-start.5 = (bf16[192,1024]{1,0:T(8,128)(2,1)S(1)}, bf16[192,1024]{1,0:T(8,128)(2,1)S(1)}, u32[]{:S(2)}, u32[]{:S(2)}) collective-permute-start(bf16[192,1024]{1,0:T(8,128)(2,1)S(1)} %shard_map.34.refs_3_), channel_id=1, source_target_pairs={{0,2},{1,3},{2,0},{3,1},{4,6},{5,7},{6,4},{7,5},{8,10},{9,11},{10,... | collective-permute-start | bytes 1179656 | tf_op jit(solution)/shard_map/ppermute | solution.py:253
  46.4 0.6 shard_map.30.refs_1_.refs_0_.refs_2_
  47.1 5.7 %collective-permute-start.9 = (bf16[384,768]{1,0:T(8,128)(2,1)S(1)}, bf16[384,768]{1,0:T(8,128)(2,1)S(1)}, u32[]{:S(2)}, u32[]{:S(2)}) collective-permute-start(bf16[384,768]{1,0:T(8,128)(2,1)S(1)} %shard_map.38), channel_id=1, source_target_pairs={{4,8},{5,9},{0,16},{1,17},{2,24},{3,25},{8,2},{9,3},{12,18},{13,19... | collective-permute-start | bytes 1769480 | tf_op jit(solution)/shard_map/ppermute | solution.py:253
  52.8 0.0 copy-done.2
  52.8 0.1 broadcast_in_dim.8.weights
  52.9 0.1 broadcast_in_dim.9.other_weights
  53.0 0.6 shard_map.31.refs_2_.refs_0_
  53.6 0.0 collective-permute-done.7.refs_6_
  53.6 0.0 collective-permute-done.5.refs_4_
  53.6 0.0 copy-done.1
  53.6 2.7 %shard_map.36.refs_1_.rows = bf16[768,4096]{1,0:T(8,128)(2,1)S(1)} custom-call(s32[9]{0:T(128)S(1)} %stack.32.places, bf16[384,4096]{1,0:T(8,128)(2,1)S(1)} %copy-done.1, f32[384,1]{1,0:T(8,128)S(1)} %broadcast_in_dim.8.weights, f32[384,1]{1,0:T(8,128)S(1)} %broadcast_in_dim.9.other_weights, bf16[384,768]{1,0:T(8,128)(2,1)S(1)} %shard_map.29.refs_0_.refs_2_, ...), custom_call_target="tpu_custom_call" | custom-call | tf_op jit(solution)/shard_map/pallas_call | solution.py:112
  56.3 3.1 %collective-permute-start.8 = (bf16[384,512]{1,0:T(8,128)(2,1)S(1)}, bf16[384,512]{1,0:T(8,128)(2,1)S(1)}, u32[]{:S(2)}, u32[]{:S(2)}) collective-permute-start(bf16[384,512]{1,0:T(8,128)(2,1)S(1)} %shard_map.37), channel_id=1, source_target_pairs={{4,8},{5,9},{0,16},{1,17},{2,24},{3,25},{8,2},{9,3},{12,18},{13,19... | collective-permute-start | bytes 1179656 | tf_op jit(solution)/shard_map/ppermute | solution.py:253
  59.4 0.0 collective-permute-done.10.refs_3_
  59.4 8.5 %shard_map.39.refs_4_ = f32[4096,2048]{1,0:T(8,128)} custom-call(s32[9]{0:T(128)S(1)} %stack.32.places, bf16[768,4096]{1,0:T(8,128)(2,1)S(1)} %shard_map.36.refs_1_.rows, bf16[384,2048]{1,0:T(8,128)(2,1)S(1)} %get-tuple-element.13.refs_0_, bf16[384,2048]{1,0:T(8,128)(2,1)S(1)} %collective-permute-done.4.refs_1_, ...), custom_call_target="tpu_custom_call" | custom-call | flops 4831838208 | bytes 12582912 | tf_op jit(solution)/shard_map/pallas_call | solution.py:53
  67.9 2.6 %collective-permute-done.9.refs_3_ = bf16[384,768]{1,0:T(8,128)(2,1)S(1)} collective-permute-done((bf16[384,768]{1,0:T(8,128)(2,1)S(1)}, bf16[384,768]{1,0:T(8,128)(2,1)S(1)}, u32[]{:S(2)}, u32[]{:S(2)}) %collective-permute-start.9) | collective-permute-done | bytes 589856 | tf_op jit(solution)/shard_map/ppermute | solution.py:253
  70.5 8.5 %shard_map.40.refs_4_ = f32[4096,2048]{1,0:T(8,128)} custom-call(s32[9]{0:T(128)S(1)} %stack.32.places, bf16[768,4096]{1,0:T(8,128)(2,1)S(1)} %shard_map.36.refs_1_.rows, bf16[384,2048]{1,0:T(8,128)(2,1)S(1)} %get-tuple-element.13.refs_0_, bf16[384,2048]{1,0:T(8,128)(2,1)S(1)} %collective-permute-done.4.refs_1_, ...), custom_call_target="tpu_custom_call", output_to_operand_aliasing={{}: (6, {})} | custom-call | flops 4831838208 | bytes 12582912 | tf_op jit(solution)/shard_map/pallas_call | solution.py:53
  79.0 0.0 collective-permute-done.8.refs_3_
  79.0 6.4 %shard_map.41 = f32[4096,2048]{1,0:T(8,128)} custom-call(s32[9]{0:T(128)S(1)} %stack.32.places, bf16[768,4096]{1,0:T(8,128)(2,1)S(1)} %shard_map.36.refs_1_.rows, bf16[384,2048]{1,0:T(8,128)(2,1)S(1)} %get-tuple-element.13.refs_0_, bf16[384,2048]{1,0:T(8,128)(2,1)S(1)} %collective-permute-done.4.refs_1_, ...), custom_call_target="tpu_custom_call", output_to_operand_aliasing={{}: (6, {})} | custom-call | flops 3221225472 | bytes 8388608 | tf_op jit(solution)/shard_map/pallas_call | solution.py:53
  (4 shorter events, 0.1 us)
Async XLA Ops:
  0.1 1.9 %copy-start = (bf16[384,4096]{1,0:T(8,128)(2,1)S(1)}, bf16[384,4096]{1,0:T(8,128)(2,1)}, u32[]{:S(2)}) copy-start(bf16[384,4096]{1,0:T(8,128)(2,1)} %slab.3) | copy-start | bytes 9437188
  2.9 19.4 %collective-permute-start.1 = (bf16[192,2048]{1,0:T(8,128)(2,1)S(1)}, bf16[192,2048]{1,0:T(8,128)(2,1)S(1)}, u32[]{:S(2)}, u32[]{:S(2)}) collective-permute-start(bf16[192,2048]{1,0:T(8,128)(2,1)S(1)} %get-tuple-element.10), channel_id=1, source_target_pairs={{0,1},{1,0},{2,3},{3,2},{4,5},{5,4},{6,7},{7,6},{8,9},{9,8},{10,11... | collective-permute-start | bytes 2359304 | tf_op jit(solution)/shard_map/ppermute | solution.py:253
  5.0 40.2 %collective-permute-start.4 = (bf16[384,2048]{1,0:T(8,128)(2,1)S(1)}, bf16[384,2048]{1,0:T(8,128)(2,1)S(1)}, u32[]{:S(2)}, u32[]{:S(2)}) collective-permute-start(bf16[384,2048]{1,0:T(8,128)(2,1)S(1)} %get-tuple-element.13.refs_0_), channel_id=1, source_target_pairs={{4,8},{5,9},{0,16},{1,17},{2,24},{3,25},{8,2},{9,3},{12,18},{13,19... | collective-permute-start | bytes 4718600 | tf_op jit(solution)/shard_map/ppermute | solution.py:253
  22.3 5.6 %collective-permute-start.2 = (bf16[192,2048]{1,0:T(8,128)(2,1)S(1)}, bf16[192,2048]{1,0:T(8,128)(2,1)S(1)}, u32[]{:S(2)}, u32[]{:S(2)}) collective-permute-start(bf16[192,2048]{1,0:T(8,128)(2,1)S(1)} %collective-permute-done.1.refs_0_.refs_1_), channel_id=1, source_target_pairs={{0,2},{1,3},{2,0},{3,1},{4,6},{5,7},{6,4},{7,5},{8,10},{9,11},{10,... | collective-permute-start | bytes 2359304 | tf_op jit(solution)/shard_map/ppermute | solution.py:253
  23.5 2.6 %collective-permute-start = (f32[384]{0:T(512)}, f32[384]{0:T(512)S(1)}, u32[]{:S(2)}, u32[]{:S(2)}) collective-permute-start(f32[384]{0:T(512)} %param.3), channel_id=1, source_target_pairs={{0,1},{1,0},{2,3},{3,2},{4,5},{5,4},{6,7},{7,6},{8,9},{9,8},{10,11... | collective-permute-start | bytes 4616 | tf_op jit(solution)/shard_map/ppermute | solution.py:253
  26.3 26.5 %copy-start.2 = (f32[384]{0:T(512)S(1)}, f32[384]{0:T(512)}, u32[]{:S(2)}) copy-start(f32[384]{0:T(512)} %param.3) | copy-start | bytes 4612
  26.3 9.5 %collective-permute-start.6 = (bf16[192,1024]{1,0:T(8,128)(2,1)S(1)}, bf16[192,1024]{1,0:T(8,128)(2,1)S(1)}, u32[]{:S(2)}, u32[]{:S(2)}) collective-permute-start(bf16[192,1024]{1,0:T(8,128)(2,1)S(1)} %get-tuple-element.14), channel_id=1, source_target_pairs={{0,1},{1,0},{2,3},{3,2},{4,5},{5,4},{6,7},{7,6},{8,9},{9,8},{10,11... | collective-permute-start | bytes 1179656 | tf_op jit(solution)/shard_map/ppermute | solution.py:253
  27.8 17.5 %collective-permute-start.3 = (bf16[192,1024]{1,0:T(8,128)(2,1)S(1)}, bf16[192,1024]{1,0:T(8,128)(2,1)S(1)}, u32[]{:S(2)}, u32[]{:S(2)}) collective-permute-start(bf16[192,1024]{1,0:T(8,128)(2,1)S(1)} %get-tuple-element.12), channel_id=1, source_target_pairs={{0,1},{1,0},{2,3},{3,2},{4,5},{5,4},{6,7},{7,6},{8,9},{9,8},{10,11... | collective-permute-start | bytes 1179656 | tf_op jit(solution)/shard_map/ppermute | solution.py:253
  28.5 25.1 %copy-start.1 = (bf16[384,4096]{1,0:T(8,128)(2,1)S(1)}, bf16[384,4096]{1,0:T(8,128)(2,1)}, u32[]{:S(2)}) copy-start(bf16[384,4096]{1,0:T(8,128)(2,1)} %slab.3) | copy-start | bytes 9437188
  28.5 30.9 %collective-permute-start.10 = (bf16[384,768]{1,0:T(8,128)(2,1)S(1)}, bf16[384,768]{1,0:T(8,128)(2,1)S(1)}, u32[]{:S(2)}, u32[]{:S(2)}) collective-permute-start(bf16[384,768]{1,0:T(8,128)(2,1)S(1)} %shard_map.29.refs_0_.refs_2_), channel_id=1, source_target_pairs={{4,8},{5,9},{0,16},{1,17},{2,24},{3,25},{8,2},{9,3},{12,18},{13,19... | collective-permute-start | bytes 1769480 | tf_op jit(solution)/shard_map/ppermute | solution.py:253
  45.2 8.3 %collective-permute-start.7 = (bf16[192,1024]{1,0:T(8,128)(2,1)S(1)}, bf16[192,1024]{1,0:T(8,128)(2,1)S(1)}, u32[]{:S(2)}, u32[]{:S(2)}) collective-permute-start(bf16[192,1024]{1,0:T(8,128)(2,1)S(1)} %shard_map.35.refs_5_), channel_id=1, source_target_pairs={{0,2},{1,3},{2,0},{3,1},{4,6},{5,7},{6,4},{7,5},{8,10},{9,11},{10,... | collective-permute-start | bytes 1179656 | tf_op jit(solution)/shard_map/ppermute | solution.py:253
  45.4 8.2 %collective-permute-start.5 = (bf16[192,1024]{1,0:T(8,128)(2,1)S(1)}, bf16[192,1024]{1,0:T(8,128)(2,1)S(1)}, u32[]{:S(2)}, u32[]{:S(2)}) collective-permute-start(bf16[192,1024]{1,0:T(8,128)(2,1)S(1)} %shard_map.34.refs_3_), channel_id=1, source_target_pairs={{0,2},{1,3},{2,0},{3,1},{4,6},{5,7},{6,4},{7,5},{8,10},{9,11},{10,... | collective-permute-start | bytes 1179656 | tf_op jit(solution)/shard_map/ppermute | solution.py:253
  47.1 23.4 %collective-permute-start.9 = (bf16[384,768]{1,0:T(8,128)(2,1)S(1)}, bf16[384,768]{1,0:T(8,128)(2,1)S(1)}, u32[]{:S(2)}, u32[]{:S(2)}) collective-permute-start(bf16[384,768]{1,0:T(8,128)(2,1)S(1)} %shard_map.38), channel_id=1, source_target_pairs={{4,8},{5,9},{0,16},{1,17},{2,24},{3,25},{8,2},{9,3},{12,18},{13,19... | collective-permute-start | bytes 1769480 | tf_op jit(solution)/shard_map/ppermute | solution.py:253
  56.3 22.6 %collective-permute-start.8 = (bf16[384,512]{1,0:T(8,128)(2,1)S(1)}, bf16[384,512]{1,0:T(8,128)(2,1)S(1)}, u32[]{:S(2)}, u32[]{:S(2)}) collective-permute-start(bf16[384,512]{1,0:T(8,128)(2,1)S(1)} %shard_map.37), channel_id=1, source_target_pairs={{4,8},{5,9},{0,16},{1,17},{2,24},{3,25},{8,2},{9,3},{12,18},{13,19... | collective-permute-start | bytes 1179656 | tf_op jit(solution)/shard_map/ppermute | solution.py:253

commit v6 on v5

--- a/solution.py
+++ b/solution.py
@@ -151,24 +151,30 @@
     )(places, slab)
 
 
-def assemble(places, mine, theirs, start, size, *earlier):
-    count = len(mine)
-    half = mine[0].shape[0]
+def assemble(places, pieces, start, size):
+    count = len(pieces[0][1])
+    half = pieces[0][1][0].shape[0]
+    arrays = [array for _, mine, theirs in pieces for array in (*mine, *theirs)]
 
     def kernel(places, *refs):
-        out = refs[-1]
-        for i in range(count):
-            for rows, ref in ((places[CORE], refs[i]), (1 - places[CORE], refs[count + i])):
-                at = pl.multiple_of((2 * i + rows) * half, half)
-                out[pl.ds(at, half), :] = ref[:, start : start + size]
+        *refs, out = refs
+        refs = iter(refs)
+        for offset, mine, _ in pieces:
+            low, high = max(start, offset), min(start + size, offset + mine[0].shape[1])
+            for rows in (places[CORE], 1 - places[CORE]):
+                for i in range(count):
+                    ref = next(refs)
+                    if low < high:
+                        at = pl.ds(pl.multiple_of((2 * i + rows) * half, half), half)
+                        out[at, low - start : high - start] = ref[:, low - offset : high - offset]
 
     return pl.pallas_call(
         kernel,
-        in_specs=[SMEM] + [VMEM] * (2 * count) + [ANY] * len(earlier),
+        in_specs=[SMEM] + [VMEM] * len(arrays),
         out_specs=VMEM,
-        out_shape=jax.ShapeDtypeStruct((2 * count * half, size), mine[0].dtype),
+        out_shape=jax.ShapeDtypeStruct((2 * count * half, size), arrays[0].dtype),
         compiler_params=params(2),
-    )(places, *mine, *theirs, *earlier)
+    )(places, *arrays)
 
 
 def hold(values, spans, *earlier):
@@ -283,7 +289,8 @@
             return [permute_all(m, lambda r, c, p: (r, c ^ 1, p)) for m in mine]
 
         blocks = [((0, p * width), (pairs, width))]
-        blocks += [share(s, j, 0, width) for j in range(Q) for s in shifts]
+        blocks += [share(s, 0, *span) for span in halves for s in shifts]
+        blocks += [share(s, j, 0, width) for j in range(1, Q) for s in shifts]
         starts = [x for start, _ in blocks for x in start]
         places = jnp.stack([jnp.asarray(x, jnp.int32) for x in (p, core, jnp.where(r == c, 0, 1), *starts)])
         own, *shares = cut_out(places, slab, [shape for _, shape in blocks])
@@ -293,12 +300,15 @@
             [permute_all(weights, lambda r, c, p: (r, c, (p - s) % Q)) for s in shifts]
         )
         direct_own = send(own)
-        mine = exchange(shares[0])
-        theirs = swap(mine)
-        others = [assemble(places, mine, theirs, *span) for span in spans]
+        pieces = []
+        for (start, _), part in zip(halves, shares):
+            received = exchange(part)
+            pieces.append((start, received, swap(received)))
+        mine = [array for _, received, _ in pieces for array in received]
+        others = [assemble(places, pieces, *span) for span in spans]
         direct_others = [send(others[0])]
         rest = []
-        for part in shares[1:]:
+        for part in shares[len(halves) :]:
             part = hold(part, [(0, width)], other_weights)[0]
             for piece in hold(part, halves, *mine):
                 received = exchange(piece)

time: 85.9 us -> 85.6 us (level)
  starting transfers between devices: 29.6 us -> 22.8 us
  waiting for transfers between devices: 24.4 us -> 31.2 us
    ppermute x11 -> x13, waiting for transfers between devices: 24.4 us -> 31.2 us  [permute(): return lax.ppermute(block, AXES, pairs) if pairs else jnp.zeros_like(block)]
    ppermute x11 -> x13, starting transfers between devices: 29.6 us -> 22.8 us  [permute(): return lax.ppermute(block, AXES, pairs) if pairs else jnp.zeros_like(block)]
  transfers between devices with their start and end apart: 11 -> 13, of which waited for: 5 -> 7; matrix products, arithmetic and copies ran while one was open for 0% -> 0% of each run, Pallas kernels for 25% -> 25%
where the time goes in v6:
time: 85.6 us; the launch traced here: 85.4 us
  waiting for transfers between devices  31.2 us (36%)
  Pallas kernels  29 us (34%)
  starting transfers between devices  22.8 us (27%)
  local copies, waits for them, and re-layouts  2.2 us (3%)
    ppermute x13, waiting for transfers between devices, permute(): return lax.ppermute(block, AXES, pairs) if pairs else jnp.zeros_like(block)  31.2 us
    pallas_call x3, Pallas kernels, product(): pl.pallas_call(kernel, grid=(height // tile,), in_specs=in_specs, out_spe...  23.4 us
    ppermute x13, starting transfers between devices, permute(): return lax.ppermute(block, AXES, pairs) if pairs else jnp.zeros_like(block)  22.8 us
    pallas_call x1, Pallas kernels, weigh(): pl.pallas_call(kernel, in_specs=[SMEM, HBM] + [VMEM] * (2 + len(arrays)),...  2.68 us
    unnamed x6, local copies, waits for them, and re-layouts  1.9 us
    pallas_call x3, Pallas kernels, assemble(): pl.pallas_call(kernel, in_specs=[SMEM] + [VMEM] * len(arrays), out_specs=...  1.75 us
  transfers between devices with their start and end apart: 13, of which 7 were waited for; matrix products, arithmetic and copies ran while one was open for 0% of the time, Pallas kernels for 25%

profile of v6, /device:TPU:1, one launch (start us, length us, event | category | flops | bytes accessed | tf_op | source)
XLA Modules:
  0.0 85.4 jit_solution(7807317342159079842)
XLA Ops:
  0.0 0.1 stack.37.places
  0.1 0.0 copy-start
  0.1 1.9 %copy-done = bf16[384,4096]{1,0:T(8,128)(2,1)S(1)} copy-done((bf16[384,4096]{1,0:T(8,128)(2,1)S(1)}, bf16[384,4096]{1,0:T(8,128)(2,1)}, u32[]{:S(2)}) %copy-start) | copy-done | bytes 3145752
  2.0 0.9 %shard_map.28 = (bf16[384,2048]{1,0:T(8,128)(2,1)S(1)}, bf16[192,1024]{1,0:T(8,128)(2,1)S(1)}, bf16[192,1024]{1,0:T(8,128)(2,1)S(1)}, bf16[192,2048]{1,0:T(8,128)(2,1)S(1)}) custom-call(s32[11]{0:T(128)S(1)} %stack.37.places, bf16[384,4096]{1,0:T(8,128)(2,1)S(1)} %copy-done), custom_call_target="tpu_custom_call" | custom-call | tf_op jit(solution)/shard_map/pallas_call | solution.py:144
  2.9 6.6 %collective-permute-start.6 = (bf16[384,2048]{1,0:T(8,128)(2,1)S(1)}, bf16[384,2048]{1,0:T(8,128)(2,1)S(1)}, u32[]{:S(2)}, u32[]{:S(2)}) collective-permute-start(bf16[384,2048]{1,0:T(8,128)(2,1)S(1)} %get-tuple-element.15.refs_0_), channel_id=1, source_target_pairs={{4,8},{5,9},{0,16},{1,17},{2,24},{3,25},{8,2},{9,3},{12,18},{13,19... | collective-permute-start | bytes 4718600 | tf_op jit(solution)/shard_map/ppermute | solution.py:259
  9.5 1.3 %collective-permute-start.1 = (bf16[192,1024]{1,0:T(8,128)(2,1)S(1)}, bf16[192,1024]{1,0:T(8,128)(2,1)S(1)}, u32[]{:S(2)}, u32[]{:S(2)}) collective-permute-start(bf16[192,1024]{1,0:T(8,128)(2,1)S(1)} %get-tuple-element.11), channel_id=1, source_target_pairs={{0,1},{1,0},{2,3},{3,2},{4,5},{5,4},{6,7},{7,6},{8,9},{9,8},{10,11... | collective-permute-start | bytes 1179656 | tf_op jit(solution)/shard_map/ppermute | solution.py:259
  10.8 0.2 collective-permute-start.3
  11.1 9.7 %collective-permute-done.1.refs_0_.refs_1_ = bf16[192,1024]{1,0:T(8,128)(2,1)S(1)} collective-permute-done((bf16[192,1024]{1,0:T(8,128)(2,1)S(1)}, bf16[192,1024]{1,0:T(8,128)(2,1)S(1)}, u32[]{:S(2)}, u32[]{:S(2)}) %collective-permute-start.1) | collective-permute-done | bytes 393248 | tf_op jit(solution)/shard_map/ppermute | solution.py:259
  20.7 0.3 collective-permute-start.2
  21.0 8.0 %collective-permute-done.3.refs_2_ = bf16[192,1024]{1,0:T(8,128)(2,1)S(1)} collective-permute-done((bf16[192,1024]{1,0:T(8,128)(2,1)S(1)}, bf16[192,1024]{1,0:T(8,128)(2,1)S(1)}, u32[]{:S(2)}, u32[]{:S(2)}) %collective-permute-start.3) | collective-permute-done | bytes 393248 | tf_op jit(solution)/shard_map/ppermute | solution.py:259
  29.0 0.4 collective-permute-start.4
  29.4 1.2 %collective-permute-start = (f32[384]{0:T(512)}, f32[384]{0:T(512)S(1)}, u32[]{:S(2)}, u32[]{:S(2)}) collective-permute-start(f32[384]{0:T(512)} %param.3), channel_id=1, source_target_pairs={{0,1},{1,0},{2,3},{3,2},{4,5},{5,4},{6,7},{7,6},{8,9},{9,8},{10,11... | collective-permute-start | bytes 4616 | tf_op jit(solution)/shard_map/ppermute | solution.py:259
  30.7 1.4 %collective-permute-done.refs_1_ = f32[384]{0:T(512)S(1)} collective-permute-done((f32[384]{0:T(512)}, f32[384]{0:T(512)S(1)}, u32[]{:S(2)}, u32[]{:S(2)}) %collective-permute-start) | collective-permute-done | bytes 1568 | tf_op jit(solution)/shard_map/ppermute | solution.py:259
  32.1 0.1 shard_map.32.refs_0_
  32.1 0.1 shard_map.33
  32.2 0.0 copy-start.2
  32.2 1.3 %collective-permute-start.8 = (bf16[192,1024]{1,0:T(8,128)(2,1)S(1)}, bf16[192,1024]{1,0:T(8,128)(2,1)S(1)}, u32[]{:S(2)}, u32[]{:S(2)}) collective-permute-start(bf16[192,1024]{1,0:T(8,128)(2,1)S(1)} %get-tuple-element.16), channel_id=1, source_target_pairs={{0,1},{1,0},{2,3},{3,2},{4,5},{5,4},{6,7},{7,6},{8,9},{9,8},{10,11... | collective-permute-start | bytes 1179656 | tf_op jit(solution)/shard_map/ppermute | solution.py:259
  33.5 0.2 collective-permute-start.5
  33.7 0.0 collective-permute-done.2.refs_1_
  33.7 0.0 collective-permute-done.4.refs_3_
  33.7 0.6 shard_map.29.refs_0_.refs_2_
  34.3 0.0 copy-start.1
  34.4 2.7 %collective-permute-start.12 = (bf16[384,768]{1,0:T(8,128)(2,1)S(1)}, bf16[384,768]{1,0:T(8,128)(2,1)S(1)}, u32[]{:S(2)}, u32[]{:S(2)}) collective-permute-start(bf16[384,768]{1,0:T(8,128)(2,1)S(1)} %shard_map.29.refs_0_.refs_2_), channel_id=1, source_target_pairs={{4,8},{5,9},{0,16},{1,17},{2,24},{3,25},{8,2},{9,3},{12,18},{13,19... | collective-permute-start | bytes 1769480 | tf_op jit(solution)/shard_map/ppermute | solution.py:259
  37.1 4.5 %collective-permute-done.8.refs_0_ = bf16[192,1024]{1,0:T(8,128)(2,1)S(1)} collective-permute-done((bf16[192,1024]{1,0:T(8,128)(2,1)S(1)}, bf16[192,1024]{1,0:T(8,128)(2,1)S(1)}, u32[]{:S(2)}, u32[]{:S(2)}) %collective-permute-start.8) | collective-permute-done | bytes 393248 | tf_op jit(solution)/shard_map/ppermute | solution.py:259
  41.6 2.1 %collective-permute-done.6.refs_1_ = bf16[384,2048]{1,0:T(8,128)(2,1)S(1)} collective-permute-done((bf16[384,2048]{1,0:T(8,128)(2,1)S(1)}, bf16[384,2048]{1,0:T(8,128)(2,1)S(1)}, u32[]{:S(2)}, u32[]{:S(2)}) %collective-permute-start.6) | collective-permute-done | bytes 1572896 | tf_op jit(solution)/shard_map/ppermute | solution.py:259
  43.7 2.1 %collective-permute-start.9 = (bf16[192,1024]{1,0:T(8,128)(2,1)S(1)}, bf16[192,1024]{1,0:T(8,128)(2,1)S(1)}, u32[]{:S(2)}, u32[]{:S(2)}) collective-permute-start(bf16[192,1024]{1,0:T(8,128)(2,1)S(1)} %shard_map.35.refs_5_), channel_id=1, source_target_pairs={{0,2},{1,3},{2,0},{3,1},{4,6},{5,7},{6,4},{7,5},{8,10},{9,11},{10,... | collective-permute-start | bytes 1179656 | tf_op jit(solution)/shard_map/ppermute | solution.py:259
  45.7 4.3 %collective-permute-done.5.refs_0_ = bf16[192,1024]{1,0:T(8,128)(2,1)S(1)} collective-permute-done((bf16[192,1024]{1,0:T(8,128)(2,1)S(1)}, bf16[192,1024]{1,0:T(8,128)(2,1)S(1)}, u32[]{:S(2)}, u32[]{:S(2)}) %collective-permute-start.5) | collective-permute-done | bytes 393248 | tf_op jit(solution)/shard_map/ppermute | solution.py:259
  50.0 2.3 %collective-permute-start.7 = (bf16[192,1024]{1,0:T(8,128)(2,1)S(1)}, bf16[192,1024]{1,0:T(8,128)(2,1)S(1)}, u32[]{:S(2)}, u32[]{:S(2)}) collective-permute-start(bf16[192,1024]{1,0:T(8,128)(2,1)S(1)} %shard_map.34.refs_3_), channel_id=1, source_target_pairs={{0,2},{1,3},{2,0},{3,1},{4,6},{5,7},{6,4},{7,5},{8,10},{9,11},{10,... | collective-permute-start | bytes 1179656 | tf_op jit(solution)/shard_map/ppermute | solution.py:259
  52.3 0.6 shard_map.30.refs_1_.refs_0_.refs_2_
  53.0 1.9 %collective-permute-start.11 = (bf16[384,768]{1,0:T(8,128)(2,1)S(1)}, bf16[384,768]{1,0:T(8,128)(2,1)S(1)}, u32[]{:S(2)}, u32[]{:S(2)}) collective-permute-start(bf16[384,768]{1,0:T(8,128)(2,1)S(1)} %shard_map.38), channel_id=1, source_target_pairs={{4,8},{5,9},{0,16},{1,17},{2,24},{3,25},{8,2},{9,3},{12,18},{13,19... | collective-permute-start | bytes 1769480 | tf_op jit(solution)/shard_map/ppermute | solution.py:259
  54.9 0.0 copy-done.2
  54.9 0.1 broadcast_in_dim.8.weights
  55.0 0.1 broadcast_in_dim.9.other_weights
  55.1 0.6 shard_map.31.refs_2_.refs_0_
  55.7 0.0 collective-permute-done.9.refs_6_
  55.7 0.0 collective-permute-done.7.refs_4_
  55.8 0.0 copy-done.1
  55.8 2.7 %shard_map.36.refs_1_.rows = bf16[768,4096]{1,0:T(8,128)(2,1)S(1)} custom-call(s32[11]{0:T(128)S(1)} %stack.37.places, bf16[384,4096]{1,0:T(8,128)(2,1)S(1)} %copy-done.1, f32[384,1]{1,0:T(8,128)S(1)} %broadcast_in_dim.8.weights, f32[384,1]{1,0:T(8,128)S(1)} %broadcast_in_dim.9.other_weights, bf16[384,768]{1,0:T(8,128)(2,1)S(1)} %shard_map.29.refs_0_.refs_2_, ...), custom_call_target="tpu_custom_call" | custom-call | tf_op jit(solution)/shard_map/pallas_call | solution.py:112
  58.5 2.2 %collective-permute-start.10 = (bf16[384,512]{1,0:T(8,128)(2,1)S(1)}, bf16[384,512]{1,0:T(8,128)(2,1)S(1)}, u32[]{:S(2)}, u32[]{:S(2)}) collective-permute-start(bf16[384,512]{1,0:T(8,128)(2,1)S(1)} %shard_map.37), channel_id=1, source_target_pairs={{4,8},{5,9},{0,16},{1,17},{2,24},{3,25},{8,2},{9,3},{12,18},{13,19... | collective-permute-start | bytes 1179656 | tf_op jit(solution)/shard_map/ppermute | solution.py:259
  60.7 0.0 collective-permute-done.12.refs_3_
  60.7 8.5 %shard_map.39.refs_4_ = f32[4096,2048]{1,0:T(8,128)} custom-call(s32[11]{0:T(128)S(1)} %stack.37.places, bf16[768,4096]{1,0:T(8,128)(2,1)S(1)} %shard_map.36.refs_1_.rows, bf16[384,2048]{1,0:T(8,128)(2,1)S(1)} %get-tuple-element.15.refs_0_, bf16[384,2048]{1,0:T(8,128)(2,1)S(1)} %collective-permute-done.6.refs_1_, ...), custom_call_target="tpu_custom_call" | custom-call | flops 4831838208 | bytes 12582912 | tf_op jit(solution)/shard_map/pallas_call | solution.py:53
  69.2 1.2 %collective-permute-done.11.refs_3_ = bf16[384,768]{1,0:T(8,128)(2,1)S(1)} collective-permute-done((bf16[384,768]{1,0:T(8,128)(2,1)S(1)}, bf16[384,768]{1,0:T(8,128)(2,1)S(1)}, u32[]{:S(2)}, u32[]{:S(2)}) %collective-permute-start.11) | collective-permute-done | bytes 589856 | tf_op jit(solution)/shard_map/ppermute | solution.py:259
  70.5 8.5 %shard_map.40.refs_4_ = f32[4096,2048]{1,0:T(8,128)} custom-call(s32[11]{0:T(128)S(1)} %stack.37.places, bf16[768,4096]{1,0:T(8,128)(2,1)S(1)} %shard_map.36.refs_1_.rows, bf16[384,2048]{1,0:T(8,128)(2,1)S(1)} %get-tuple-element.15.refs_0_, bf16[384,2048]{1,0:T(8,128)(2,1)S(1)} %collective-permute-done.6.refs_1_, ...), custom_call_target="tpu_custom_call", output_to_operand_aliasing={{}: (6, {})} | custom-call | flops 4831838208 | bytes 12582912 | tf_op jit(solution)/shard_map/pallas_call | solution.py:53
  79.0 0.0 collective-permute-done.10.refs_3_
  79.0 6.4 %shard_map.41 = f32[4096,2048]{1,0:T(8,128)} custom-call(s32[11]{0:T(128)S(1)} %stack.37.places, bf16[768,4096]{1,0:T(8,128)(2,1)S(1)} %shard_map.36.refs_1_.rows, bf16[384,2048]{1,0:T(8,128)(2,1)S(1)} %get-tuple-element.15.refs_0_, bf16[384,2048]{1,0:T(8,128)(2,1)S(1)} %collective-permute-done.6.refs_1_, ...), custom_call_target="tpu_custom_call", output_to_operand_aliasing={{}: (6, {})} | custom-call | flops 3221225472 | bytes 8388608 | tf_op jit(solution)/shard_map/pallas_call | solution.py:53
  (4 shorter events, 0.1 us)
Async XLA Ops:
  0.1 1.9 %copy-start = (bf16[384,4096]{1,0:T(8,128)(2,1)S(1)}, bf16[384,4096]{1,0:T(8,128)(2,1)}, u32[]{:S(2)}) copy-start(bf16[384,4096]{1,0:T(8,128)(2,1)} %slab.3) | copy-start | bytes 9437188
  2.9 40.7 %collective-permute-start.6 = (bf16[384,2048]{1,0:T(8,128)(2,1)S(1)}, bf16[384,2048]{1,0:T(8,128)(2,1)S(1)}, u32[]{:S(2)}, u32[]{:S(2)}) collective-permute-start(bf16[384,2048]{1,0:T(8,128)(2,1)S(1)} %get-tuple-element.15.refs_0_), channel_id=1, source_target_pairs={{4,8},{5,9},{0,16},{1,17},{2,24},{3,25},{8,2},{9,3},{12,18},{13,19... | collective-permute-start | bytes 4718600 | tf_op jit(solution)/shard_map/ppermute | solution.py:259
  9.5 11.2 %collective-permute-start.1 = (bf16[192,1024]{1,0:T(8,128)(2,1)S(1)}, bf16[192,1024]{1,0:T(8,128)(2,1)S(1)}, u32[]{:S(2)}, u32[]{:S(2)}) collective-permute-start(bf16[192,1024]{1,0:T(8,128)(2,1)S(1)} %get-tuple-element.11), channel_id=1, source_target_pairs={{0,1},{1,0},{2,3},{3,2},{4,5},{5,4},{6,7},{7,6},{8,9},{9,8},{10,11... | collective-permute-start | bytes 1179656 | tf_op jit(solution)/shard_map/ppermute | solution.py:259
  10.8 18.2 %collective-permute-start.3 = (bf16[192,1024]{1,0:T(8,128)(2,1)S(1)}, bf16[192,1024]{1,0:T(8,128)(2,1)S(1)}, u32[]{:S(2)}, u32[]{:S(2)}) collective-permute-start(bf16[192,1024]{1,0:T(8,128)(2,1)S(1)} %get-tuple-element.12), channel_id=1, source_target_pairs={{0,1},{1,0},{2,3},{3,2},{4,5},{5,4},{6,7},{7,6},{8,9},{9,8},{10,11... | collective-permute-start | bytes 1179656 | tf_op jit(solution)/shard_map/ppermute | solution.py:259
  20.7 13.0 %collective-permute-start.2 = (bf16[192,1024]{1,0:T(8,128)(2,1)S(1)}, bf16[192,1024]{1,0:T(8,128)(2,1)S(1)}, u32[]{:S(2)}, u32[]{:S(2)}) collective-permute-start(bf16[192,1024]{1,0:T(8,128)(2,1)S(1)} %collective-permute-done.1.refs_0_.refs_1_), channel_id=1, source_target_pairs={{0,2},{1,3},{2,0},{3,1},{4,6},{5,7},{6,4},{7,5},{8,10},{9,11},{10,... | collective-permute-start | bytes 1179656 | tf_op jit(solution)/shard_map/ppermute | solution.py:259
  29.0 4.7 %collective-permute-start.4 = (bf16[192,1024]{1,0:T(8,128)(2,1)S(1)}, bf16[192,1024]{1,0:T(8,128)(2,1)S(1)}, u32[]{:S(2)}, u32[]{:S(2)}) collective-permute-start(bf16[192,1024]{1,0:T(8,128)(2,1)S(1)} %collective-permute-done.3.refs_2_), channel_id=1, source_target_pairs={{0,2},{1,3},{2,0},{3,1},{4,6},{5,7},{6,4},{7,5},{8,10},{9,11},{10,... | collective-permute-start | bytes 1179656 | tf_op jit(solution)/shard_map/ppermute | solution.py:259
  29.4 2.6 %collective-permute-start = (f32[384]{0:T(512)}, f32[384]{0:T(512)S(1)}, u32[]{:S(2)}, u32[]{:S(2)}) collective-permute-start(f32[384]{0:T(512)} %param.3), channel_id=1, source_target_pairs={{0,1},{1,0},{2,3},{3,2},{4,5},{5,4},{6,7},{7,6},{8,9},{9,8},{10,11... | collective-permute-start | bytes 4616 | tf_op jit(solution)/shard_map/ppermute | solution.py:259
  32.2 22.7 %copy-start.2 = (f32[384]{0:T(512)S(1)}, f32[384]{0:T(512)}, u32[]{:S(2)}) copy-start(f32[384]{0:T(512)} %param.3) | copy-start | bytes 4612
  32.2 9.4 %collective-permute-start.8 = (bf16[192,1024]{1,0:T(8,128)(2,1)S(1)}, bf16[192,1024]{1,0:T(8,128)(2,1)S(1)}, u32[]{:S(2)}, u32[]{:S(2)}) collective-permute-start(bf16[192,1024]{1,0:T(8,128)(2,1)S(1)} %get-tuple-element.16), channel_id=1, source_target_pairs={{0,1},{1,0},{2,3},{3,2},{4,5},{5,4},{6,7},{7,6},{8,9},{9,8},{10,11... | collective-permute-start | bytes 1179656 | tf_op jit(solution)/shard_map/ppermute | solution.py:259
  33.5 16.5 %collective-permute-start.5 = (bf16[192,1024]{1,0:T(8,128)(2,1)S(1)}, bf16[192,1024]{1,0:T(8,128)(2,1)S(1)}, u32[]{:S(2)}, u32[]{:S(2)}) collective-permute-start(bf16[192,1024]{1,0:T(8,128)(2,1)S(1)} %get-tuple-element.14), channel_id=1, source_target_pairs={{0,1},{1,0},{2,3},{3,2},{4,5},{5,4},{6,7},{7,6},{8,9},{9,8},{10,11... | collective-permute-start | bytes 1179656 | tf_op jit(solution)/shard_map/ppermute | solution.py:259
  34.3 21.4 %copy-start.1 = (bf16[384,4096]{1,0:T(8,128)(2,1)S(1)}, bf16[384,4096]{1,0:T(8,128)(2,1)}, u32[]{:S(2)}) copy-start(bf16[384,4096]{1,0:T(8,128)(2,1)} %slab.3) | copy-start | bytes 9437188
  34.4 26.4 %collective-permute-start.12 = (bf16[384,768]{1,0:T(8,128)(2,1)S(1)}, bf16[384,768]{1,0:T(8,128)(2,1)S(1)}, u32[]{:S(2)}, u32[]{:S(2)}) collective-permute-start(bf16[384,768]{1,0:T(8,128)(2,1)S(1)} %shard_map.29.refs_0_.refs_2_), channel_id=1, source_target_pairs={{4,8},{5,9},{0,16},{1,17},{2,24},{3,25},{8,2},{9,3},{12,18},{13,19... | collective-permute-start | bytes 1769480 | tf_op jit(solution)/shard_map/ppermute | solution.py:259
  43.7 12.1 %collective-permute-start.9 = (bf16[192,1024]{1,0:T(8,128)(2,1)S(1)}, bf16[192,1024]{1,0:T(8,128)(2,1)S(1)}, u32[]{:S(2)}, u32[]{:S(2)}) collective-permute-start(bf16[192,1024]{1,0:T(8,128)(2,1)S(1)} %shard_map.35.refs_5_), channel_id=1, source_target_pairs={{0,2},{1,3},{2,0},{3,1},{4,6},{5,7},{6,4},{7,5},{8,10},{9,11},{10,... | collective-permute-start | bytes 1179656 | tf_op jit(solution)/shard_map/ppermute | solution.py:259
  50.0 5.7 %collective-permute-start.7 = (bf16[192,1024]{1,0:T(8,128)(2,1)S(1)}, bf16[192,1024]{1,0:T(8,128)(2,1)S(1)}, u32[]{:S(2)}, u32[]{:S(2)}) collective-permute-start(bf16[192,1024]{1,0:T(8,128)(2,1)S(1)} %shard_map.34.refs_3_), channel_id=1, source_target_pairs={{0,2},{1,3},{2,0},{3,1},{4,6},{5,7},{6,4},{7,5},{8,10},{9,11},{10,... | collective-permute-start | bytes 1179656 | tf_op jit(solution)/shard_map/ppermute | solution.py:259
  53.0 17.5 %collective-permute-start.11 = (bf16[384,768]{1,0:T(8,128)(2,1)S(1)}, bf16[384,768]{1,0:T(8,128)(2,1)S(1)}, u32[]{:S(2)}, u32[]{:S(2)}) collective-permute-start(bf16[384,768]{1,0:T(8,128)(2,1)S(1)} %shard_map.38), channel_id=1, source_target_pairs={{4,8},{5,9},{0,16},{1,17},{2,24},{3,25},{8,2},{9,3},{12,18},{13,19... | collective-permute-start | bytes 1769480 | tf_op jit(solution)/shard_map/ppermute | solution.py:259
  58.5 20.5 %collective-permute-start.10 = (bf16[384,512]{1,0:T(8,128)(2,1)S(1)}, bf16[384,512]{1,0:T(8,128)(2,1)S(1)}, u32[]{:S(2)}, u32[]{:S(2)}) collective-permute-start(bf16[384,512]{1,0:T(8,128)(2,1)S(1)} %shard_map.37), channel_id=1, source_target_pairs={{4,8},{5,9},{0,16},{1,17},{2,24},{3,25},{8,2},{9,3},{12,18},{13,19... | collective-permute-start | bytes 1179656 | tf_op jit(solution)/shard_map/ppermute | solution.py:259

commit v7 on v6

--- a/solution.py
+++ b/solution.py
@@ -270,7 +270,7 @@
     def on_device(slab, weights):
         pairs, block = slab.shape
         width = block // Q
-        spans = split(width, PARTS - 1, max(LANES, width * 1 // 4 // LANES * LANES))
+        spans = split(width, PARTS - 1, max(LANES, width * 3 // 16 // LANES * LANES))
         halves = split(width, 2, 0)
         shifts = range(1, Q)
         r, c, p = (lax.axis_index(axis) for axis in AXES)

time: 85.6 us -> 85.9 us (level)
  Pallas kernels: 29 us -> 30.1 us
  waiting for transfers between devices: 31.2 us -> 30.3 us
    pallas_call x3, Pallas kernels: 23.4 us -> 24.5 us  [product(): pl.pallas_call(kernel, grid=(height // tile,), in_specs=in_specs, out_spe...]
    ppermute x13, waiting for transfers between devices: 31.2 us -> 30.3 us  [permute(): return lax.ppermute(block, AXES, pairs) if pairs else jnp.zeros_like(block)]
  transfers between devices with their start and end apart: 13 -> 13, of which waited for: 7 -> 7; matrix products, arithmetic and copies ran while one was open for 0% -> 0% of each run, Pallas kernels for 25% -> 27%
where the time goes in v7:
time: 85.9 us; the launch traced here: 85.5 us
  waiting for transfers between devices  30.3 us (35%)
  Pallas kernels  30.1 us (35%)
  starting transfers between devices  22.8 us (27%)
  local copies, waits for them, and re-layouts  2.2 us (3%)
    ppermute x13, waiting for transfers between devices, permute(): return lax.ppermute(block, AXES, pairs) if pairs else jnp.zeros_like(block)  30.3 us
    pallas_call x3, Pallas kernels, product(): pl.pallas_call(kernel, grid=(height // tile,), in_specs=in_specs, out_spe...  24.5 us
    ppermute x13, starting transfers between devices, permute(): return lax.ppermute(block, AXES, pairs) if pairs else jnp.zeros_like(block)  22.8 us
    pallas_call x1, Pallas kernels, weigh(): pl.pallas_call(kernel, in_specs=[SMEM, HBM] + [VMEM] * (2 + len(arrays)),...  2.69 us
    unnamed x6, local copies, waits for them, and re-layouts  1.9 us
    pallas_call x3, Pallas kernels, assemble(): pl.pallas_call(kernel, in_specs=[SMEM] + [VMEM] * len(arrays), out_specs=...  1.78 us
  transfers between devices with their start and end apart: 13, of which 7 were waited for; matrix products, arithmetic and copies ran while one was open for 0% of the time, Pallas kernels for 27%

profile of v7, /device:TPU:1, one launch (start us, length us, event | category | flops | bytes accessed | tf_op | source)
XLA Modules:
  0.0 85.5 jit_solution(8220283460686257919)
XLA Ops:
  0.0 0.1 stack.37.places
  0.1 0.0 copy-start
  0.1 1.9 %copy-done = bf16[384,4096]{1,0:T(8,128)(2,1)S(1)} copy-done((bf16[384,4096]{1,0:T(8,128)(2,1)S(1)}, bf16[384,4096]{1,0:T(8,128)(2,1)}, u32[]{:S(2)}) %copy-start) | copy-done | bytes 3145752
  2.0 0.9 %shard_map.28 = (bf16[384,2048]{1,0:T(8,128)(2,1)S(1)}, bf16[192,1024]{1,0:T(8,128)(2,1)S(1)}, bf16[192,1024]{1,0:T(8,128)(2,1)S(1)}, bf16[192,2048]{1,0:T(8,128)(2,1)S(1)}) custom-call(s32[11]{0:T(128)S(1)} %stack.37.places, bf16[384,4096]{1,0:T(8,128)(2,1)S(1)} %copy-done), custom_call_target="tpu_custom_call" | custom-call | tf_op jit(solution)/shard_map/pallas_call | solution.py:144
  2.9 6.6 %collective-permute-start.6 = (bf16[384,2048]{1,0:T(8,128)(2,1)S(1)}, bf16[384,2048]{1,0:T(8,128)(2,1)S(1)}, u32[]{:S(2)}, u32[]{:S(2)}) collective-permute-start(bf16[384,2048]{1,0:T(8,128)(2,1)S(1)} %get-tuple-element.15.refs_0_), channel_id=1, source_target_pairs={{4,8},{5,9},{0,16},{1,17},{2,24},{3,25},{8,2},{9,3},{12,18},{13,19... | collective-permute-start | bytes 4718600 | tf_op jit(solution)/shard_map/ppermute | solution.py:259
  9.5 1.3 %collective-permute-start.1 = (bf16[192,1024]{1,0:T(8,128)(2,1)S(1)}, bf16[192,1024]{1,0:T(8,128)(2,1)S(1)}, u32[]{:S(2)}, u32[]{:S(2)}) collective-permute-start(bf16[192,1024]{1,0:T(8,128)(2,1)S(1)} %get-tuple-element.11), channel_id=1, source_target_pairs={{0,1},{1,0},{2,3},{3,2},{4,5},{5,4},{6,7},{7,6},{8,9},{9,8},{10,11... | collective-permute-start | bytes 1179656 | tf_op jit(solution)/shard_map/ppermute | solution.py:259
  10.8 0.2 collective-permute-start.3
  11.1 9.7 %collective-permute-done.1.refs_0_.refs_1_ = bf16[192,1024]{1,0:T(8,128)(2,1)S(1)} collective-permute-done((bf16[192,1024]{1,0:T(8,128)(2,1)S(1)}, bf16[192,1024]{1,0:T(8,128)(2,1)S(1)}, u32[]{:S(2)}, u32[]{:S(2)}) %collective-permute-start.1) | collective-permute-done | bytes 393248 | tf_op jit(solution)/shard_map/ppermute | solution.py:259
  20.7 0.3 collective-permute-start.2
  21.0 8.0 %collective-permute-done.3.refs_2_ = bf16[192,1024]{1,0:T(8,128)(2,1)S(1)} collective-permute-done((bf16[192,1024]{1,0:T(8,128)(2,1)S(1)}, bf16[192,1024]{1,0:T(8,128)(2,1)S(1)}, u32[]{:S(2)}, u32[]{:S(2)}) %collective-permute-start.3) | collective-permute-done | bytes 393248 | tf_op jit(solution)/shard_map/ppermute | solution.py:259
  29.0 0.4 collective-permute-start.4
  29.4 1.2 %collective-permute-start = (f32[384]{0:T(512)}, f32[384]{0:T(512)S(1)}, u32[]{:S(2)}, u32[]{:S(2)}) collective-permute-start(f32[384]{0:T(512)} %param.3), channel_id=1, source_target_pairs={{0,1},{1,0},{2,3},{3,2},{4,5},{5,4},{6,7},{7,6},{8,9},{9,8},{10,11... | collective-permute-start | bytes 4616 | tf_op jit(solution)/shard_map/ppermute | solution.py:259
  30.7 1.4 %collective-permute-done.refs_1_ = f32[384]{0:T(512)S(1)} collective-permute-done((f32[384]{0:T(512)}, f32[384]{0:T(512)S(1)}, u32[]{:S(2)}, u32[]{:S(2)}) %collective-permute-start) | collective-permute-done | bytes 1568 | tf_op jit(solution)/shard_map/ppermute | solution.py:259
  32.1 0.1 shard_map.32.refs_0_
  32.1 0.1 shard_map.33
  32.2 0.0 copy-start.2
  32.2 1.3 %collective-permute-start.8 = (bf16[192,1024]{1,0:T(8,128)(2,1)S(1)}, bf16[192,1024]{1,0:T(8,128)(2,1)S(1)}, u32[]{:S(2)}, u32[]{:S(2)}) collective-permute-start(bf16[192,1024]{1,0:T(8,128)(2,1)S(1)} %get-tuple-element.16), channel_id=1, source_target_pairs={{0,1},{1,0},{2,3},{3,2},{4,5},{5,4},{6,7},{7,6},{8,9},{9,8},{10,11... | collective-permute-start | bytes 1179656 | tf_op jit(solution)/shard_map/ppermute | solution.py:259
  33.5 0.2 collective-permute-start.5
  33.7 0.0 collective-permute-done.2.refs_1_
  33.7 0.0 collective-permute-done.4.refs_3_
  33.7 0.6 shard_map.29.refs_0_.refs_2_
  34.4 0.0 copy-start.1
  34.4 2.7 %collective-permute-start.12 = (bf16[384,896]{1,0:T(8,128)(2,1)S(1)}, bf16[384,896]{1,0:T(8,128)(2,1)S(1)}, u32[]{:S(2)}, u32[]{:S(2)}) collective-permute-start(bf16[384,896]{1,0:T(8,128)(2,1)S(1)} %shard_map.29.refs_0_.refs_2_), channel_id=1, source_target_pairs={{4,8},{5,9},{0,16},{1,17},{2,24},{3,25},{8,2},{9,3},{12,18},{13,19... | collective-permute-start | bytes 2064392 | tf_op jit(solution)/shard_map/ppermute | solution.py:259
  37.1 4.5 %collective-permute-done.8.refs_0_ = bf16[192,1024]{1,0:T(8,128)(2,1)S(1)} collective-permute-done((bf16[192,1024]{1,0:T(8,128)(2,1)S(1)}, bf16[192,1024]{1,0:T(8,128)(2,1)S(1)}, u32[]{:S(2)}, u32[]{:S(2)}) %collective-permute-start.8) | collective-permute-done | bytes 393248 | tf_op jit(solution)/shard_map/ppermute | solution.py:259
  41.6 2.1 %collective-permute-done.6.refs_1_ = bf16[384,2048]{1,0:T(8,128)(2,1)S(1)} collective-permute-done((bf16[384,2048]{1,0:T(8,128)(2,1)S(1)}, bf16[384,2048]{1,0:T(8,128)(2,1)S(1)}, u32[]{:S(2)}, u32[]{:S(2)}) %collective-permute-start.6) | collective-permute-done | bytes 1572896 | tf_op jit(solution)/shard_map/ppermute | solution.py:259
  43.7 2.1 %collective-permute-start.9 = (bf16[192,1024]{1,0:T(8,128)(2,1)S(1)}, bf16[192,1024]{1,0:T(8,128)(2,1)S(1)}, u32[]{:S(2)}, u32[]{:S(2)}) collective-permute-start(bf16[192,1024]{1,0:T(8,128)(2,1)S(1)} %shard_map.35.refs_5_), channel_id=1, source_target_pairs={{0,2},{1,3},{2,0},{3,1},{4,6},{5,7},{6,4},{7,5},{8,10},{9,11},{10,... | collective-permute-start | bytes 1179656 | tf_op jit(solution)/shard_map/ppermute | solution.py:259
  45.7 4.3 %collective-permute-done.5.refs_0_ = bf16[192,1024]{1,0:T(8,128)(2,1)S(1)} collective-permute-done((bf16[192,1024]{1,0:T(8,128)(2,1)S(1)}, bf16[192,1024]{1,0:T(8,128)(2,1)S(1)}, u32[]{:S(2)}, u32[]{:S(2)}) %collective-permute-start.5) | collective-permute-done | bytes 393248 | tf_op jit(solution)/shard_map/ppermute | solution.py:259
  50.0 2.3 %collective-permute-start.7 = (bf16[192,1024]{1,0:T(8,128)(2,1)S(1)}, bf16[192,1024]{1,0:T(8,128)(2,1)S(1)}, u32[]{:S(2)}, u32[]{:S(2)}) collective-permute-start(bf16[192,1024]{1,0:T(8,128)(2,1)S(1)} %shard_map.34.refs_3_), channel_id=1, source_target_pairs={{0,2},{1,3},{2,0},{3,1},{4,6},{5,7},{6,4},{7,5},{8,10},{9,11},{10,... | collective-permute-start | bytes 1179656 | tf_op jit(solution)/shard_map/ppermute | solution.py:259
  52.3 0.6 shard_map.30.refs_1_.refs_0_.refs_2_
  53.0 1.9 %collective-permute-start.11 = (bf16[384,768]{1,0:T(8,128)(2,1)S(1)}, bf16[384,768]{1,0:T(8,128)(2,1)S(1)}, u32[]{:S(2)}, u32[]{:S(2)}) collective-permute-start(bf16[384,768]{1,0:T(8,128)(2,1)S(1)} %shard_map.38), channel_id=1, source_target_pairs={{4,8},{5,9},{0,16},{1,17},{2,24},{3,25},{8,2},{9,3},{12,18},{13,19... | collective-permute-start | bytes 1769480 | tf_op jit(solution)/shard_map/ppermute | solution.py:259
  54.9 0.0 copy-done.2
  54.9 0.1 broadcast_in_dim.8.weights
  55.0 0.1 broadcast_in_dim.9.other_weights
  55.2 0.6 shard_map.31.refs_2_.refs_0_
  55.7 0.0 collective-permute-done.9.refs_6_
  55.8 0.0 collective-permute-done.7.refs_4_
  55.8 0.0 copy-done.1
  55.8 2.7 %shard_map.36.refs_1_.rows = bf16[768,4096]{1,0:T(8,128)(2,1)S(1)} custom-call(s32[11]{0:T(128)S(1)} %stack.37.places, bf16[384,4096]{1,0:T(8,128)(2,1)S(1)} %copy-done.1, f32[384,1]{1,0:T(8,128)S(1)} %broadcast_in_dim.8.weights, f32[384,1]{1,0:T(8,128)S(1)} %broadcast_in_dim.9.other_weights, bf16[384,896]{1,0:T(8,128)(2,1)S(1)} %shard_map.29.refs_0_.refs_2_, ...), custom_call_target="tpu_custom_call" | custom-call | tf_op jit(solution)/shard_map/pallas_call | solution.py:112
  58.5 2.2 %collective-permute-start.10 = (bf16[384,384]{1,0:T(8,128)(2,1)S(1)}, bf16[384,384]{1,0:T(8,128)(2,1)S(1)}, u32[]{:S(2)}, u32[]{:S(2)}) collective-permute-start(bf16[384,384]{1,0:T(8,128)(2,1)S(1)} %shard_map.37), channel_id=1, source_target_pairs={{4,8},{5,9},{0,16},{1,17},{2,24},{3,25},{8,2},{9,3},{12,18},{13,19... | collective-permute-start | bytes 884744 | tf_op jit(solution)/shard_map/ppermute | solution.py:259
  60.7 0.0 collective-permute-done.12.refs_3_
  60.8 10.0 %shard_map.39.refs_4_ = f32[4096,2048]{1,0:T(8,128)} custom-call(s32[11]{0:T(128)S(1)} %stack.37.places, bf16[768,4096]{1,0:T(8,128)(2,1)S(1)} %shard_map.36.refs_1_.rows, bf16[384,2048]{1,0:T(8,128)(2,1)S(1)} %get-tuple-element.15.refs_0_, bf16[384,2048]{1,0:T(8,128)(2,1)S(1)} %collective-permute-done.6.refs_1_, ...), custom_call_target="tpu_custom_call" | custom-call | flops 5637144576 | bytes 14680064 | tf_op jit(solution)/shard_map/pallas_call | solution.py:53
  70.7 0.3 collective-permute-done.11.refs_3_
  71.0 8.5 %shard_map.40.refs_4_ = f32[4096,2048]{1,0:T(8,128)} custom-call(s32[11]{0:T(128)S(1)} %stack.37.places, bf16[768,4096]{1,0:T(8,128)(2,1)S(1)} %shard_map.36.refs_1_.rows, bf16[384,2048]{1,0:T(8,128)(2,1)S(1)} %get-tuple-element.15.refs_0_, bf16[384,2048]{1,0:T(8,128)(2,1)S(1)} %collective-permute-done.6.refs_1_, ...), custom_call_target="tpu_custom_call", output_to_operand_aliasing={{}: (6, {})} | custom-call | flops 4831838208 | bytes 12582912 | tf_op jit(solution)/shard_map/pallas_call | solution.py:53
  79.5 0.0 collective-permute-done.10.refs_3_
  79.5 6.0 %shard_map.41 = f32[4096,2048]{1,0:T(8,128)} custom-call(s32[11]{0:T(128)S(1)} %stack.37.places, bf16[768,4096]{1,0:T(8,128)(2,1)S(1)} %shard_map.36.refs_1_.rows, bf16[384,2048]{1,0:T(8,128)(2,1)S(1)} %get-tuple-element.15.refs_0_, bf16[384,2048]{1,0:T(8,128)(2,1)S(1)} %collective-permute-done.6.refs_1_, ...), custom_call_target="tpu_custom_call", output_to_operand_aliasing={{}: (6, {})} | custom-call | flops 2415919104 | bytes 6291456 | tf_op jit(solution)/shard_map/pallas_call | solution.py:53
  (4 shorter events, 0.1 us)
Async XLA Ops:
  0.1 1.9 %copy-start = (bf16[384,4096]{1,0:T(8,128)(2,1)S(1)}, bf16[384,4096]{1,0:T(8,128)(2,1)}, u32[]{:S(2)}) copy-start(bf16[384,4096]{1,0:T(8,128)(2,1)} %slab.3) | copy-start | bytes 9437188
  2.9 40.7 %collective-permute-start.6 = (bf16[384,2048]{1,0:T(8,128)(2,1)S(1)}, bf16[384,2048]{1,0:T(8,128)(2,1)S(1)}, u32[]{:S(2)}, u32[]{:S(2)}) collective-permute-start(bf16[384,2048]{1,0:T(8,128)(2,1)S(1)} %get-tuple-element.15.refs_0_), channel_id=1, source_target_pairs={{4,8},{5,9},{0,16},{1,17},{2,24},{3,25},{8,2},{9,3},{12,18},{13,19... | collective-permute-start | bytes 4718600 | tf_op jit(solution)/shard_map/ppermute | solution.py:259
  9.5 11.2 %collective-permute-start.1 = (bf16[192,1024]{1,0:T(8,128)(2,1)S(1)}, bf16[192,1024]{1,0:T(8,128)(2,1)S(1)}, u32[]{:S(2)}, u32[]{:S(2)}) collective-permute-start(bf16[192,1024]{1,0:T(8,128)(2,1)S(1)} %get-tuple-element.11), channel_id=1, source_target_pairs={{0,1},{1,0},{2,3},{3,2},{4,5},{5,4},{6,7},{7,6},{8,9},{9,8},{10,11... | collective-permute-start | bytes 1179656 | tf_op jit(solution)/shard_map/ppermute | solution.py:259
  10.8 18.2 %collective-permute-start.3 = (bf16[192,1024]{1,0:T(8,128)(2,1)S(1)}, bf16[192,1024]{1,0:T(8,128)(2,1)S(1)}, u32[]{:S(2)}, u32[]{:S(2)}) collective-permute-start(bf16[192,1024]{1,0:T(8,128)(2,1)S(1)} %get-tuple-element.12), channel_id=1, source_target_pairs={{0,1},{1,0},{2,3},{3,2},{4,5},{5,4},{6,7},{7,6},{8,9},{9,8},{10,11... | collective-permute-start | bytes 1179656 | tf_op jit(solution)/shard_map/ppermute | solution.py:259
  20.7 13.0 %collective-permute-start.2 = (bf16[192,1024]{1,0:T(8,128)(2,1)S(1)}, bf16[192,1024]{1,0:T(8,128)(2,1)S(1)}, u32[]{:S(2)}, u32[]{:S(2)}) collective-permute-start(bf16[192,1024]{1,0:T(8,128)(2,1)S(1)} %collective-permute-done.1.refs_0_.refs_1_), channel_id=1, source_target_pairs={{0,2},{1,3},{2,0},{3,1},{4,6},{5,7},{6,4},{7,5},{8,10},{9,11},{10,... | collective-permute-start | bytes 1179656 | tf_op jit(solution)/shard_map/ppermute | solution.py:259
  29.0 4.7 %collective-permute-start.4 = (bf16[192,1024]{1,0:T(8,128)(2,1)S(1)}, bf16[192,1024]{1,0:T(8,128)(2,1)S(1)}, u32[]{:S(2)}, u32[]{:S(2)}) collective-permute-start(bf16[192,1024]{1,0:T(8,128)(2,1)S(1)} %collective-permute-done.3.refs_2_), channel_id=1, source_target_pairs={{0,2},{1,3},{2,0},{3,1},{4,6},{5,7},{6,4},{7,5},{8,10},{9,11},{10,... | collective-permute-start | bytes 1179656 | tf_op jit(solution)/shard_map/ppermute | solution.py:259
  29.4 2.6 %collective-permute-start = (f32[384]{0:T(512)}, f32[384]{0:T(512)S(1)}, u32[]{:S(2)}, u32[]{:S(2)}) collective-permute-start(f32[384]{0:T(512)} %param.3), channel_id=1, source_target_pairs={{0,1},{1,0},{2,3},{3,2},{4,5},{5,4},{6,7},{7,6},{8,9},{9,8},{10,11... | collective-permute-start | bytes 4616 | tf_op jit(solution)/shard_map/ppermute | solution.py:259
  32.2 22.7 %copy-start.2 = (f32[384]{0:T(512)S(1)}, f32[384]{0:T(512)}, u32[]{:S(2)}) copy-start(f32[384]{0:T(512)} %param.3) | copy-start | bytes 4612
  32.2 9.4 %collective-permute-start.8 = (bf16[192,1024]{1,0:T(8,128)(2,1)S(1)}, bf16[192,1024]{1,0:T(8,128)(2,1)S(1)}, u32[]{:S(2)}, u32[]{:S(2)}) collective-permute-start(bf16[192,1024]{1,0:T(8,128)(2,1)S(1)} %get-tuple-element.16), channel_id=1, source_target_pairs={{0,1},{1,0},{2,3},{3,2},{4,5},{5,4},{6,7},{7,6},{8,9},{9,8},{10,11... | collective-permute-start | bytes 1179656 | tf_op jit(solution)/shard_map/ppermute | solution.py:259
  33.5 16.5 %collective-permute-start.5 = (bf16[192,1024]{1,0:T(8,128)(2,1)S(1)}, bf16[192,1024]{1,0:T(8,128)(2,1)S(1)}, u32[]{:S(2)}, u32[]{:S(2)}) collective-permute-start(bf16[192,1024]{1,0:T(8,128)(2,1)S(1)} %get-tuple-element.14), channel_id=1, source_target_pairs={{0,1},{1,0},{2,3},{3,2},{4,5},{5,4},{6,7},{7,6},{8,9},{9,8},{10,11... | collective-permute-start | bytes 1179656 | tf_op jit(solution)/shard_map/ppermute | solution.py:259
  34.4 21.4 %copy-start.1 = (bf16[384,4096]{1,0:T(8,128)(2,1)S(1)}, bf16[384,4096]{1,0:T(8,128)(2,1)}, u32[]{:S(2)}) copy-start(bf16[384,4096]{1,0:T(8,128)(2,1)} %slab.3) | copy-start | bytes 9437188
  34.4 26.4 %collective-permute-start.12 = (bf16[384,896]{1,0:T(8,128)(2,1)S(1)}, bf16[384,896]{1,0:T(8,128)(2,1)S(1)}, u32[]{:S(2)}, u32[]{:S(2)}) collective-permute-start(bf16[384,896]{1,0:T(8,128)(2,1)S(1)} %shard_map.29.refs_0_.refs_2_), channel_id=1, source_target_pairs={{4,8},{5,9},{0,16},{1,17},{2,24},{3,25},{8,2},{9,3},{12,18},{13,19... | collective-permute-start | bytes 2064392 | tf_op jit(solution)/shard_map/ppermute | solution.py:259
  43.7 12.1 %collective-permute-start.9 = (bf16[192,1024]{1,0:T(8,128)(2,1)S(1)}, bf16[192,1024]{1,0:T(8,128)(2,1)S(1)}, u32[]{:S(2)}, u32[]{:S(2)}) collective-permute-start(bf16[192,1024]{1,0:T(8,128)(2,1)S(1)} %shard_map.35.refs_5_), channel_id=1, source_target_pairs={{0,2},{1,3},{2,0},{3,1},{4,6},{5,7},{6,4},{7,5},{8,10},{9,11},{10,... | collective-permute-start | bytes 1179656 | tf_op jit(solution)/shard_map/ppermute | solution.py:259
  50.0 5.7 %collective-permute-start.7 = (bf16[192,1024]{1,0:T(8,128)(2,1)S(1)}, bf16[192,1024]{1,0:T(8,128)(2,1)S(1)}, u32[]{:S(2)}, u32[]{:S(2)}) collective-permute-start(bf16[192,1024]{1,0:T(8,128)(2,1)S(1)} %shard_map.34.refs_3_), channel_id=1, source_target_pairs={{0,2},{1,3},{2,0},{3,1},{4,6},{5,7},{6,4},{7,5},{8,10},{9,11},{10,... | collective-permute-start | bytes 1179656 | tf_op jit(solution)/shard_map/ppermute | solution.py:259
  53.0 18.0 %collective-permute-start.11 = (bf16[384,768]{1,0:T(8,128)(2,1)S(1)}, bf16[384,768]{1,0:T(8,128)(2,1)S(1)}, u32[]{:S(2)}, u32[]{:S(2)}) collective-permute-start(bf16[384,768]{1,0:T(8,128)(2,1)S(1)} %shard_map.38), channel_id=1, source_target_pairs={{4,8},{5,9},{0,16},{1,17},{2,24},{3,25},{8,2},{9,3},{12,18},{13,19... | collective-permute-start | bytes 1769480 | tf_op jit(solution)/shard_map/ppermute | solution.py:259
  58.5 21.0 %collective-permute-start.10 = (bf16[384,384]{1,0:T(8,128)(2,1)S(1)}, bf16[384,384]{1,0:T(8,128)(2,1)S(1)}, u32[]{:S(2)}, u32[]{:S(2)}) collective-permute-start(bf16[384,384]{1,0:T(8,128)(2,1)S(1)} %shard_map.37), channel_id=1, source_target_pairs={{4,8},{5,9},{0,16},{1,17},{2,24},{3,25},{8,2},{9,3},{12,18},{13,19... | collective-permute-start | bytes 884744 | tf_op jit(solution)/shard_map/ppermute | solution.py:259
